TPU v7x, 32 devices: a whole 2x2x4 slice. The times are simulated.
32 devices in a mesh: role: 2 (over y), band: 4 (over z), turn: 4 (over x, core).
Axes of the slice: x: 2, y: 2, z: 4, core: 2. Of those that a mesh axis runs over, the one named last changes fastest.
Arguments:
- voltages: bfloat16 [8, 2, 256, 3840], P(('role', 'band'), None, 'turn'), may hold values from -6 to 6
- station_flags: int32 [256], P('turn'), may hold values 0 or 1
- filter_taps: bfloat16 [8, 256, 256], replicated, may hold values from -0.125 to 0.125
- kernel_rows: bfloat16 [8, 1, 32, 256], P(('role', 'band')), may hold values from -0.375 to 0.375
- kernel_cols: bfloat16 [8, 1, 32, 256], P(('role', 'band')), may hold values from -0.375 to 0.375
- cell_index: int32 [2, 1024, 1], P(None, ('role', 'band', 'turn')), may hold values from 0 to 4095
Outputs:
- image: float32 [32, 128], P(('role', 'band', 'turn'))
All inputs are finite; a program needn't handle non-finite values. No bound on the sum of `station_flags` on one device may be relied on, other than what follows from the above.
Results may differ from a plain program's by a relative error of at most 0.0071.
Values may be sent and summed in bfloat16 or wider, within the bound.
No kernel may reach another device: no remote copies, remote signals or barrier semaphores. Data moves between devices by JAX's collectives and lax.ppermute only.
A program may use at most 64 MiB of HBM per device.

v0:
```python
import functools
import math

import jax
import jax.numpy as jnp
from jax import lax
from jax.experimental import pallas as pl
from jax.experimental.pallas import tpu as pltpu
from jax.sharding import Mesh
from jax.sharding import PartitionSpec as P

NGRID = 4096
MW = 128
ROWS_DEV = 1
DIGIT = 64
PAD_ROWS = 16
CORES = 2
TURN = ("chip", "core")
EVERYONE = ("role", "band", *TURN)
VMEM_BYTES = 24 * 1024 * 1024


def split_terms(value):
    high = value.astype(jnp.bfloat16)
    return high, (value - high.astype(jnp.float32)).astype(jnp.bfloat16)


def phase(cell, pixel):
    quarter = NGRID // 4
    turned = (cell * pixel) & (NGRID - 1)
    quadrant = (turned + quarter // 2) // quarter
    angle = (turned - quadrant * quarter).astype(jnp.float32) * (2.0 * math.pi / NGRID)
    square = angle * angle
    sine = angle * (1 + square * (-1 / 6 + square * (1 / 120 + square * (-1 / 5040 + square * (1 / 362880)))))
    cosine = 1 + square * (-1 / 2 + square * (1 / 24 + square * (-1 / 720 + square * (1 / 40320))))
    odd = (quadrant & 1) == 1
    real = jnp.where(odd, sine, cosine)
    imag = jnp.where(odd, cosine, sine)
    return (
        jnp.where(((quadrant + 1) & 2) == 2, -real, real),
        jnp.where((quadrant & 2) == 2, -imag, imag),
    )


def tables_kernel(row_ref, col_ref):
    for out_ref, sign in ((row_ref, 1), (col_ref, -1)):
        pixels, cells = out_ref.shape[0] // 2, out_ref.shape[1] // 6
        place = lax.broadcasted_iota(jnp.int32, (2 * pixels, 2 * cells), 0)
        lane = lax.broadcasted_iota(jnp.int32, (2 * pixels, 2 * cells), 1)
        lower, right = place >= pixels, lane >= cells
        pixel = jnp.where(lower, place - pixels, place) - pixels // 2
        cos, sin = phase(jnp.where(right, lane - cells, lane), pixel)
        value = jnp.where(lower == right, cos, sin)
        value = jnp.where(right & (lower == (sign < 0)), -value, value)
        high, low = split_terms(value)
        out_ref[...] = jnp.concatenate([high, low, high], axis=1)


def pack_kernel(flags_ref, cells_ref, _, out_ref):
    out_ref[...] = jnp.zeros_like(out_ref)
    out_ref[0:2, : cells_ref.shape[1]] = cells_ref[...]
    out_ref[2:3, : flags_ref.shape[1]] = flags_ref[...]


def gridding_weights(rows_ref, cols_ref, packed_ref, turn, stations):
    both = jnp.concatenate([rows_ref[0, 0], cols_ref[0, 0]], axis=0).astype(jnp.float32)
    weights = jnp.zeros((both.shape[0], stations), jnp.float32)
    for group in range(lax.axis_size(TURN)):
        weights = jnp.where(turn == group, both[:, group * stations : (group + 1) * stations], weights)
    return (weights * packed_ref[2:3, :stations].astype(jnp.float32)).astype(jnp.bfloat16)


def cell_digits(packed_refs, count, lanes):
    turn = lax.axis_index(TURN)
    digits = jnp.zeros((4, lanes), jnp.float32)
    for index, packed in enumerate(packed_refs):
        place = turn ^ index
        wide = jnp.concatenate([packed[0:2, :count]] * (lanes // count), axis=1)
        lane = lax.broadcasted_iota(jnp.int32, wide.shape, 1)
        wide = jnp.where((lane >= place * count) & (lane < (place + 1) * count), wide, 0)
        digits = digits + jnp.concatenate([wide // DIGIT, wide % DIGIT], axis=0).astype(jnp.float32)
    digits = jnp.concatenate([digits, jnp.zeros((PAD_ROWS - 4, lanes), jnp.float32)], axis=0)
    return digits.astype(jnp.bfloat16)


def gridded_frames(volt_ref, taps_ref, weights, firsts):
    taps, two_fine, _ = taps_ref.shape
    stations = volt_ref.shape[2]
    core = lax.axis_index("core")
    lhs = jnp.concatenate(
        [
            volt_ref[0, core, :, pl.ds(pl.multiple_of(first * two_fine, two_fine), taps * two_fine)]
            for first in firsts
        ],
        axis=0,
    )
    filt = taps_ref[...].reshape(taps * two_fine, two_fine)
    spectra = jnp.dot(lhs, filt, preferred_element_type=jnp.float32).astype(jnp.bfloat16)
    return [
        jnp.dot(weights, spectra[index * stations : (index + 1) * stations], preferred_element_type=jnp.float32)
        for index in range(len(firsts))
    ]


def own_kernel(volt_ref, taps_ref, rows_ref, cols_ref, packed_ref, out_ref):
    weights = gridding_weights(rows_ref, cols_ref, packed_ref, lax.axis_index(TURN), volt_ref.shape[2])
    rows = weights.shape[0]
    for frame, gridded in enumerate(gridded_frames(volt_ref, taps_ref, weights, range(out_ref.shape[0] // rows))):
        out_ref[frame * rows : (frame + 1) * rows] = gridded


def sum_kernel(step, each, count, volt_ref, taps_ref, rows_ref, cols_ref, own_ref, packed_ref, part_ref, *refs):
    out_ref = refs[-1]
    weights = gridding_weights(rows_ref, cols_ref, packed_ref, lax.axis_index(TURN) ^ 1, volt_ref.shape[2])
    rows = weights.shape[0]
    firsts = [(lax.axis_index("chip") ^ step) * each + frame for frame in range(each)]
    for index, gridded in enumerate(gridded_frames(volt_ref, taps_ref, weights, firsts)):
        held = part_ref[pl.ds(pl.multiple_of(firsts[index] * rows, rows), rows)]
        out_ref[index * rows : (index + 1) * rows] = (held + gridded).astype(jnp.bfloat16)
    out_ref[each * rows :] = cell_digits((own_ref, packed_ref), count, out_ref.shape[1])


def image_kernel(pairs_each, *refs):
    *got, row_dft_ref, col_dft_ref, out_ref = refs
    fine = got[0].shape[1] // 2
    sub = row_dft_ref.shape[1] // 6
    row_total = out_ref.shape[0]
    total = got[0][...].astype(jnp.float32)
    for source in got[1:]:
        total = total + source[...].astype(jnp.float32)
    digits = total[pairs_each * 2 * sub :]
    cell_u = (digits[0:1, :fine] * DIGIT + digits[2:3, :fine]).astype(jnp.int32)
    cell_v = (digits[1:2, :fine] * DIGIT + digits[3:4, :fine]).astype(jnp.int32)

    def transform(dft_ref, first, cos, sin):
        held = jnp.concatenate(
            [
                jnp.concatenate(
                    [
                        total[index * 2 * sub + first : index * 2 * sub + first + sub, :fine],
                        total[index * 2 * sub + first : index * 2 * sub + first + sub, fine:],
                    ],
                    axis=0,
                )
                for index in range(pairs_each)
            ],
            axis=1,
        )
        high, low = split_terms(held)
        plain = jnp.dot(
            dft_ref[...], jnp.concatenate([high, high, low], axis=0), preferred_element_type=jnp.float32
        )
        half = plain.shape[0] // 2
        real, imag = plain[:half], plain[half:]
        cos = jnp.concatenate([cos] * pairs_each, axis=1)
        sin = jnp.concatenate([sin] * pairs_each, axis=1)
        return real * cos - imag * sin, real * sin + imag * cos

    row = lax.broadcasted_iota(jnp.int32, (row_total, fine), 0)
    row_real, row_imag = transform(row_dft_ref, 0, *phase(cell_u, row - row_total // 2))
    col = lax.broadcasted_iota(jnp.int32, (MW, fine), 0)
    col_real, col_imag = transform(col_dft_ref, sub, *phase(cell_v, col - MW // 2))
    left = jnp.concatenate([row_real, -row_imag], axis=1).astype(jnp.bfloat16)
    right = jnp.concatenate([col_real, col_imag], axis=1).astype(jnp.bfloat16)
    out_ref[...] = lax.dot_general(left, right, (((1,), (1,)), ((), ())), preferred_element_type=jnp.float32)


def final_kernel(scale_factor, in_ref, out_ref):
    out_ref[...] = jnp.sum(in_ref[...], axis=0) * scale_factor


def call(kernel, shape, args, flops=0):
    moved = sum(math.prod(leaf.shape) * leaf.dtype.itemsize for leaf in [*jax.tree.leaves(shape), *args])
    return pl.pallas_call(
        kernel,
        out_shape=shape,
        in_specs=[pl.BlockSpec(memory_space=pltpu.VMEM)] * len(args),
        out_specs=jax.tree.map(lambda _: pl.BlockSpec(memory_space=pltpu.VMEM), shape),
        compiler_params=pltpu.CompilerParams(vmem_limit_bytes=VMEM_BYTES),
        cost_estimate=pl.CostEstimate(flops=flops, bytes_accessed=moved, transcendentals=0),
    )(*args)


def local(voltages, station_flags, filter_taps, kernel_rows, kernel_cols, cell_index):
    station_rows, width = voltages.shape[2:]
    taps, two_fine, _ = filter_taps.shape
    sub_u, sub_v = kernel_rows.shape[2], kernel_cols.shape[2]
    chips = lax.axis_size("chip")
    row_total = ROWS_DEV * lax.axis_size(EVERYONE)
    channels = two_fine // 2 * lax.axis_size("role") * lax.axis_size("band")
    frames = width // two_fine - taps + 1
    scale_factor = 4.0 / math.sqrt(channels * sub_u * sub_v) / frames
    each = frames // chips
    count = cell_index.shape[1]
    sub_rows = sub_u + sub_v

    swap = [(core, 1 - core) for core in range(CORES)]
    other = lax.ppermute(voltages, "core", swap)
    tables = call(
        tables_kernel,
        (
            jax.ShapeDtypeStruct((2 * row_total, 6 * sub_u), jnp.bfloat16),
            jax.ShapeDtypeStruct((2 * MW, 6 * sub_v), jnp.bfloat16),
        ),
        (),
        flops=2 * voltages.size * two_fine * taps,
    )
    packed = call(
        pack_kernel,
        jax.ShapeDtypeStruct((8, -(-max(station_rows, count) // 128) * 128), jnp.int32),
        (station_flags.reshape(1, -1), cell_index.reshape(2, -1), tables[0]),
    )
    other_packed = lax.ppermute(packed, "core", swap)
    fixed = (filter_taps, kernel_rows, kernel_cols, packed)
    flops = 2 * station_rows * taps * two_fine * two_fine
    part = call(
        own_kernel,
        jax.ShapeDtypeStruct((frames * sub_rows, two_fine), jnp.float32),
        (voltages, *fixed),
        flops=frames * flops,
    )

    after = ()
    got = []
    for step in [*range(1, chips), 0]:
        made = call(
            functools.partial(sum_kernel, step, each, count),
            jax.ShapeDtypeStruct((each * sub_rows + PAD_ROWS, two_fine), jnp.bfloat16),
            (other, *fixed, other_packed, part, *after),
            flops=each * flops,
        )
        after = (made,)
        if step:
            made = lax.ppermute(made, "chip", [(source, source ^ step) for source in range(chips)])
        got.append(made)
    image = call(
        functools.partial(image_kernel, each),
        jax.ShapeDtypeStruct((row_total, MW), jnp.float32),
        (*got, *tables),
    )
    rows = lax.all_to_all(image, EVERYONE, split_axis=0, concat_axis=0, tiled=True)
    return call(
        functools.partial(final_kernel, scale_factor),
        jax.ShapeDtypeStruct((ROWS_DEV, MW), jnp.float32),
        (rows.reshape(-1, ROWS_DEV, MW),),
    )


def solution(mesh):
    roles, bands, turns = (mesh.shape[name] for name in ("role", "band", "turn"))
    split = Mesh(mesh.devices.reshape(roles, bands, turns // CORES, CORES), EVERYONE)
    in_specs = (
        P(("role", "band"), None, TURN, None),
        P(TURN),
        P(),
        P(("role", "band"), None, None, None),
        P(("role", "band"), None, None, None),
        P(None, EVERYONE, None),
    )
    out_specs = P(EVERYONE, None)
    return jax.shard_map(local, mesh=split, in_specs=in_specs, out_specs=out_specs, check_vma=False)
```

profile of v0, /device:TPU:0, one launch (start us, length us, event | category | flops | bytes accessed | tf_op | source)
XLA Modules:
  0.0 24.8 jit_solution(3870963311837090799)
XLA Ops:
  0.0 0.0 copy-start.1
  0.0 0.0 copy-start
  0.0 0.5 %collective-permute-start = (bf16[1,2,64,3840]{3,2,1,0:T(8,128)(2,1)}, bf16[1,2,64,3840]{3,2,1,0:T(8,128)(2,1)S(1)}, u32[]{:S(2)}, u32[]{:S(2)}) collective-permute-start(bf16[1,2,64,3840]{3,2,1,0:T(8,128)(2,1)} %volt_ref.1), channel_id=1, source_target_pairs={{0,1},{1,0},{2,3},{3,2},{4,5},{5,4},{6,7},{7,6},{8,9},{9,8},{10,11... | collective-permute-start | bytes 2949128 | tf_op jit(solution)/shard_map/ppermute | solution.py:198
  0.5 0.4 %shard_map.64 = (bf16[64,192]{1,0:T(8,128)(2,1)S(1)}, bf16[256,192]{1,0:T(8,128)(2,1)S(1)}) custom-call(), custom_call_target="tpu_custom_call" | custom-call | flops 2013265920 | bytes 122880 | tf_op jit(solution)/shard_map/pallas_call | solution.py:174
  0.9 0.0 copy-start.4
  0.9 0.0 copy-start.5
  0.9 0.7 %copy-done.4 = s32[2,32,1]{1,2,0:T(1,128)S(1)} copy-done((s32[2,32,1]{1,2,0:T(1,128)S(1)}, s32[2,32,1]{1,2,0:T(1,128)}, u32[]{:S(2)}) %copy-start.4) | copy-done | bytes 280
  1.5 0.0 copy-done.5
  1.5 0.0 copy-start.2
  1.5 0.0 copy-start.3
  1.5 0.3 %collective-permute-start.1 = (s32[8,128]{1,0:T(8,128)S(1)}, s32[8,128]{1,0:T(8,128)S(1)}, u32[]{:S(2)}, u32[]{:S(2)}) collective-permute-start(s32[8,128]{1,0:T(8,128)S(1)} %shard_map.65.packed_ref.own_ref), channel_id=1, source_target_pairs={{0,1},{1,0},{2,3},{3,2},{4,5},{5,4},{6,7},{7,6},{8,9},{9,8},{10,11... | collective-permute-start | bytes 12296 | tf_op jit(solution)/shard_map/ppermute | solution.py:213
  1.8 0.0 copy-done.1
  1.8 0.0 copy-done
  1.8 0.4 %copy-done.2 = bf16[1,1,32,256]{3,2,1,0:T(8,128)(2,1)S(1)} copy-done((bf16[1,1,32,256]{3,2,1,0:T(8,128)(2,1)S(1)}, bf16[1,1,32,256]{3,2,1,0:T(8,128)(2,1)}, u32[]{:S(2)}) %copy-start.2) | copy-done | bytes 16408
  2.3 0.0 copy-done.3
  2.3 0.9 %shard_map.66.part_ref = f32[512,256]{1,0:T(8,128)S(1)} custom-call(bf16[1,2,64,3840]{3,2,1,0:T(8,128)(2,1)S(1)} %copy-done.1, bf16[8,256,256]{2,1,0:T(8,128)(2,1)S(1)} %copy-done, bf16[1,1,32,256]{3,2,1,0:T(8,128)(2,1)S(1)} %copy-done.2, bf16[1,1,32,256]{3,2,1,0:T(8,128)(2,1)S(1)} %copy-done.3, s32[8,128]{1,0:T(8,128)S(1)} %shard_map.65.packed_ref.own_ref), custom_call_target="tpu_custom_call" | custom-call | flops 536870912 | bytes 2592768 | tf_op jit(solution)/shard_map/pallas_call | solution.py:174
  3.2 0.0 collective-permute-done.1.packed_ref
  3.2 0.0 collective-permute-done.volt_ref
  3.2 0.6 %shard_map.67.refs_0_ = bf16[272,256]{1,0:T(8,128)(2,1)S(1)} custom-call(bf16[1,2,64,3840]{3,2,1,0:T(8,128)(2,1)S(1)} %collective-permute-done.volt_ref, bf16[8,256,256]{2,1,0:T(8,128)(2,1)S(1)} %copy-done, bf16[1,1,32,256]{3,2,1,0:T(8,128)(2,1)S(1)} %copy-done.2, bf16[1,1,32,256]{3,2,1,0:T(8,128)(2,1)S(1)} %copy-done.3, ...), custom_call_target="tpu_custom_call" | custom-call | flops 268435456 | bytes 2736128 | tf_op jit(solution)/shard_map/pallas_call | solution.py:174
  3.8 2.8 %collective-permute-start.2 = (bf16[272,256]{1,0:T(8,128)(2,1)S(1)}, bf16[272,256]{1,0:T(8,128)(2,1)S(1)}, u32[]{:S(2)}, u32[]{:S(2)}) collective-permute-start(bf16[272,256]{1,0:T(8,128)(2,1)S(1)} %shard_map.67.refs_0_), channel_id=1, source_target_pairs={{0,2},{2,0},{1,3},{3,1},{4,6},{6,4},{5,7},{7,5},{8,10},{10,8},{9,1... | collective-permute-start | bytes 417800 | tf_op jit(solution)/shard_map/ppermute | solution.py:234
  6.7 0.6 %shard_map.68.refs_1_ = bf16[272,256]{1,0:T(8,128)(2,1)S(1)} custom-call(bf16[1,2,64,3840]{3,2,1,0:T(8,128)(2,1)S(1)} %collective-permute-done.volt_ref, bf16[8,256,256]{2,1,0:T(8,128)(2,1)S(1)} %copy-done, bf16[1,1,32,256]{3,2,1,0:T(8,128)(2,1)S(1)} %copy-done.2, bf16[1,1,32,256]{3,2,1,0:T(8,128)(2,1)S(1)} %copy-done.3, ...), custom_call_target="tpu_custom_call" | custom-call | flops 268435456 | bytes 2875392 | tf_op jit(solution)/shard_map/pallas_call | solution.py:174
  7.3 3.5 %collective-permute-done.2.refs_0_ = bf16[272,256]{1,0:T(8,128)(2,1)S(1)} collective-permute-done((bf16[272,256]{1,0:T(8,128)(2,1)S(1)}, bf16[272,256]{1,0:T(8,128)(2,1)S(1)}, u32[]{:S(2)}, u32[]{:S(2)}) %collective-permute-start.2) | collective-permute-done | bytes 139296 | tf_op jit(solution)/shard_map/ppermute | solution.py:234
  10.7 0.5 %shard_map.69 = f32[32,128]{1,0:T(8,128)S(1)} custom-call(bf16[272,256]{1,0:T(8,128)(2,1)S(1)} %collective-permute-done.2.refs_0_, bf16[272,256]{1,0:T(8,128)(2,1)S(1)} %shard_map.68.refs_1_, bf16[64,192]{1,0:T(8,128)(2,1)S(1)} %get-tuple-element.7._.refs_2_, bf16[256,192]{1,0:T(8,128)(2,1)S(1)} %get-tuple-element.8.refs_3_), custom_call_target="tpu_custom_call" | custom-call | bytes 417792 | tf_op jit(solution)/shard_map/pallas_call | solution.py:174
  11.2 13.1 %all_to_all.9.in_ref = f32[32,1,128]{2,1,0:T(1,128)S(1)} all-to-all(f32[32,1,128]{2,1,0:T(1,128)S(1)} %bitcast.3), channel_id=1, replica_groups=mesh['role'=2,'band'=4,'chip'=2,'core'=2] {'role','band','chip','core'}, dimensions={0} | all-to-all | bytes 32768 | tf_op jit(solution)/shard_map/all_to_all | solution.py:241
  24.3 0.5 %shard_map.70 = f32[1,128]{1,0:T(1,128)} custom-call(f32[32,1,128]{2,1,0:T(1,128)S(1)} %all_to_all.9.in_ref), custom_call_target="tpu_custom_call" | custom-call | bytes 16896 | tf_op jit(solution)/shard_map/pallas_call | solution.py:174
  (1 shorter events, 0.0 us)
Async XLA Ops:
  0.0 1.8 %copy-start.1 = (bf16[1,2,64,3840]{3,2,1,0:T(8,128)(2,1)S(1)}, bf16[1,2,64,3840]{3,2,1,0:T(8,128)(2,1)}, u32[]{:S(2)}) copy-start(bf16[1,2,64,3840]{3,2,1,0:T(8,128)(2,1)} %volt_ref.1) | copy-start | bytes 2949124
  0.0 1.8 %copy-start = (bf16[8,256,256]{2,1,0:T(8,128)(2,1)S(1)}, bf16[8,256,256]{2,1,0:T(8,128)(2,1)}, u32[]{:S(2)}) copy-start(bf16[8,256,256]{2,1,0:T(8,128)(2,1)} %taps_ref.5) | copy-start | bytes 3145732
  0.0 3.2 %collective-permute-start = (bf16[1,2,64,3840]{3,2,1,0:T(8,128)(2,1)}, bf16[1,2,64,3840]{3,2,1,0:T(8,128)(2,1)S(1)}, u32[]{:S(2)}, u32[]{:S(2)}) collective-permute-start(bf16[1,2,64,3840]{3,2,1,0:T(8,128)(2,1)} %volt_ref.1), channel_id=1, source_target_pairs={{0,1},{1,0},{2,3},{3,2},{4,5},{5,4},{6,7},{7,6},{8,9},{9,8},{10,11... | collective-permute-start | bytes 2949128 | tf_op jit(solution)/shard_map/ppermute | solution.py:198
  0.9 0.7 %copy-start.4 = (s32[2,32,1]{1,2,0:T(1,128)S(1)}, s32[2,32,1]{1,2,0:T(1,128)}, u32[]{:S(2)}) copy-start(s32[2,32,1]{1,2,0:T(1,128)} %param.11) | copy-start | bytes 772
  0.9 0.7 %copy-start.5 = (s32[64]{0:T(128)S(1)}, s32[64]{0:T(128)}, u32[]{:S(2)}) copy-start(s32[64]{0:T(128)} %param.7) | copy-start | bytes 772
  1.5 0.7 %copy-start.2 = (bf16[1,1,32,256]{3,2,1,0:T(8,128)(2,1)S(1)}, bf16[1,1,32,256]{3,2,1,0:T(8,128)(2,1)}, u32[]{:S(2)}) copy-start(bf16[1,1,32,256]{3,2,1,0:T(8,128)(2,1)} %rows_ref.5) | copy-start | bytes 49156
  1.5 0.7 %copy-start.3 = (bf16[1,1,32,256]{3,2,1,0:T(8,128)(2,1)S(1)}, bf16[1,1,32,256]{3,2,1,0:T(8,128)(2,1)}, u32[]{:S(2)}) copy-start(bf16[1,1,32,256]{3,2,1,0:T(8,128)(2,1)} %cols_ref.5) | copy-start | bytes 49156
  1.5 1.6 %collective-permute-start.1 = (s32[8,128]{1,0:T(8,128)S(1)}, s32[8,128]{1,0:T(8,128)S(1)}, u32[]{:S(2)}, u32[]{:S(2)}) collective-permute-start(s32[8,128]{1,0:T(8,128)S(1)} %shard_map.65.packed_ref.own_ref), channel_id=1, source_target_pairs={{0,1},{1,0},{2,3},{3,2},{4,5},{5,4},{6,7},{7,6},{8,9},{9,8},{10,11... | collective-permute-start | bytes 12296 | tf_op jit(solution)/shard_map/ppermute | solution.py:213
  3.8 6.9 %collective-permute-start.2 = (bf16[272,256]{1,0:T(8,128)(2,1)S(1)}, bf16[272,256]{1,0:T(8,128)(2,1)S(1)}, u32[]{:S(2)}, u32[]{:S(2)}) collective-permute-start(bf16[272,256]{1,0:T(8,128)(2,1)S(1)} %shard_map.67.refs_0_), channel_id=1, source_target_pairs={{0,2},{2,0},{1,3},{3,1},{4,6},{6,4},{5,7},{7,5},{8,10},{10,8},{9,1... | collective-permute-start | bytes 417800 | tf_op jit(solution)/shard_map/ppermute | solution.py:234
where the time goes:
time: 25.2 us; the launch traced here: 24.8 us
  blocking collectives  13.1 us (52%)
  Pallas kernels  3.58 us (14%)
  starting transfers between devices  3.54 us (14%)
  waiting for transfers between devices  3.47 us (14%)
  local copies, waits for them, and re-layouts  1.13 us (4%)
    all_to_all x1, blocking collectives, local(): lax.all_to_all(image, EVERYONE, split_axis=0, concat_axis=0, tiled=True)  13.1 us
    pallas_call x7, Pallas kernels, call(): pl.pallas_call(kernel, out_shape=shape, in_specs=[pl.BlockSpec(memory_spa...  3.58 us
    ppermute x1, waiting for transfers between devices, local(): lax.ppermute(made, 'chip', [(source, source ^ step) for source in range(c...  3.46 us
    ppermute x1, starting transfers between devices, local(): lax.ppermute(made, 'chip', [(source, source ^ step) for source in range(c...  2.81 us
    unnamed x12, local copies, waits for them, and re-layouts  1.13 us
  transfers between devices with their start and end apart: 3, of which 1 were waited for; matrix products, arithmetic and copies ran while one was open for 0% of the time, Pallas kernels for 8%

commit v1 on v0

--- a/solution.py
+++ b/solution.py
@@ -42,7 +42,10 @@
     )
 
 
-def tables_kernel(row_ref, col_ref):
+def first_kernel(flags_ref, cells_ref, row_ref, col_ref, packed_ref):
+    packed_ref[...] = jnp.zeros_like(packed_ref)
+    packed_ref[0:2, : cells_ref.shape[1]] = cells_ref[...]
+    packed_ref[2:3, : flags_ref.shape[1]] = flags_ref[...]
     for out_ref, sign in ((row_ref, 1), (col_ref, -1)):
         pixels, cells = out_ref.shape[0] // 2, out_ref.shape[1] // 6
         place = lax.broadcasted_iota(jnp.int32, (2 * pixels, 2 * cells), 0)
@@ -56,12 +59,6 @@
         out_ref[...] = jnp.concatenate([high, low, high], axis=1)
 
 
-def pack_kernel(flags_ref, cells_ref, _, out_ref):
-    out_ref[...] = jnp.zeros_like(out_ref)
-    out_ref[0:2, : cells_ref.shape[1]] = cells_ref[...]
-    out_ref[2:3, : flags_ref.shape[1]] = flags_ref[...]
-
-
 def gridding_weights(rows_ref, cols_ref, packed_ref, turn, stations):
     both = jnp.concatenate([rows_ref[0, 0], cols_ref[0, 0]], axis=0).astype(jnp.float32)
     weights = jnp.zeros((both.shape[0], stations), jnp.float32)
@@ -83,41 +80,40 @@
     return digits.astype(jnp.bfloat16)
 
 
-def gridded_frames(volt_ref, taps_ref, weights, firsts):
+def channelized(grid_ref, taps_ref, first, digits, out_ref):
     taps, two_fine, _ = taps_ref.shape
-    stations = volt_ref.shape[2]
-    core = lax.axis_index("core")
+    each = (out_ref.shape[0] - PAD_ROWS) // grid_ref.shape[0]
     lhs = jnp.concatenate(
         [
-            volt_ref[0, core, :, pl.ds(pl.multiple_of(first * two_fine, two_fine), taps * two_fine)]
-            for first in firsts
+            grid_ref[:, pl.ds(pl.multiple_of((first + frame) * two_fine, two_fine), taps * two_fine)]
+            for frame in range(each)
         ],
         axis=0,
     )
-    filt = taps_ref[...].reshape(taps * two_fine, two_fine)
-    spectra = jnp.dot(lhs, filt, preferred_element_type=jnp.float32).astype(jnp.bfloat16)
-    return [
-        jnp.dot(weights, spectra[index * stations : (index + 1) * stations], preferred_element_type=jnp.float32)
-        for index in range(len(firsts))
+    made = jnp.dot(lhs, taps_ref[...].reshape(taps * two_fine, two_fine), preferred_element_type=jnp.float32)
+    out_ref[: out_ref.shape[0] - PAD_ROWS] = made.astype(jnp.bfloat16)
+    out_ref[out_ref.shape[0] - PAD_ROWS :] = digits
+
+
+def grid_kernel(own_ref, other_ref, taps_ref, rows_ref, cols_ref, packed_ref, other_packed_ref, *refs, count):
+    grid_ref, digits_ref, *outs = refs
+    turn, core, stations = lax.axis_index(TURN), lax.axis_index("core"), own_ref.shape[2]
+    weights = [
+        gridding_weights(rows_ref, cols_ref, packed, turn ^ index, stations)
+        for index, packed in enumerate((packed_ref, other_packed_ref))
     ]
-
-
-def own_kernel(volt_ref, taps_ref, rows_ref, cols_ref, packed_ref, out_ref):
-    weights = gridding_weights(rows_ref, cols_ref, packed_ref, lax.axis_index(TURN), volt_ref.shape[2])
-    rows = weights.shape[0]
-    for frame, gridded in enumerate(gridded_frames(volt_ref, taps_ref, weights, range(out_ref.shape[0] // rows))):
-        out_ref[frame * rows : (frame + 1) * rows] = gridded
-
-
-def sum_kernel(step, each, count, volt_ref, taps_ref, rows_ref, cols_ref, own_ref, packed_ref, part_ref, *refs):
-    out_ref = refs[-1]
-    weights = gridding_weights(rows_ref, cols_ref, packed_ref, lax.axis_index(TURN) ^ 1, volt_ref.shape[2])
-    rows = weights.shape[0]
-    firsts = [(lax.axis_index("chip") ^ step) * each + frame for frame in range(each)]
-    for index, gridded in enumerate(gridded_frames(volt_ref, taps_ref, weights, firsts)):
-        held = part_ref[pl.ds(pl.multiple_of(firsts[index] * rows, rows), rows)]
-        out_ref[index * rows : (index + 1) * rows] = (held + gridded).astype(jnp.bfloat16)
-    out_ref[each * rows :] = cell_digits((own_ref, packed_ref), count, out_ref.shape[1])
+    held = jnp.concatenate([own_ref[0, core], other_ref[0, core]], axis=0)
+    gridded = jnp.dot(jnp.concatenate(weights, axis=1), held, preferred_element_type=jnp.float32)
+    grid_ref[...] = gridded.astype(jnp.bfloat16)
+    digits_ref[...] = cell_digits((packed_ref, other_packed_ref), count, digits_ref.shape[1])
+    each = (outs[0].shape[0] - PAD_ROWS) // grid_ref.shape[0]
+    for step, out_ref in enumerate(outs, 1):
+        channelized(grid_ref, taps_ref, (lax.axis_index("chip") ^ step) * each, digits_ref[...], out_ref)
+
+
+def near_kernel(grid_ref, taps_ref, digits_ref, out_ref):
+    each = (out_ref.shape[0] - PAD_ROWS) // grid_ref.shape[0]
+    channelized(grid_ref, taps_ref, lax.axis_index("chip") * each, digits_ref[...], out_ref)
 
 
 def image_kernel(pairs_each, *refs):
@@ -196,43 +192,33 @@
 
     swap = [(core, 1 - core) for core in range(CORES)]
     other = lax.ppermute(voltages, "core", swap)
-    tables = call(
-        tables_kernel,
+    *tables, packed = call(
+        first_kernel,
         (
             jax.ShapeDtypeStruct((2 * row_total, 6 * sub_u), jnp.bfloat16),
             jax.ShapeDtypeStruct((2 * MW, 6 * sub_v), jnp.bfloat16),
+            jax.ShapeDtypeStruct((8, -(-max(station_rows, count) // 128) * 128), jnp.int32),
         ),
-        (),
+        (station_flags.reshape(1, -1), cell_index.reshape(2, -1)),
         flops=2 * voltages.size * two_fine * taps,
     )
-    packed = call(
-        pack_kernel,
-        jax.ShapeDtypeStruct((8, -(-max(station_rows, count) // 128) * 128), jnp.int32),
-        (station_flags.reshape(1, -1), cell_index.reshape(2, -1), tables[0]),
-    )
     other_packed = lax.ppermute(packed, "core", swap)
-    fixed = (filter_taps, kernel_rows, kernel_cols, packed)
-    flops = 2 * station_rows * taps * two_fine * two_fine
-    part = call(
-        own_kernel,
-        jax.ShapeDtypeStruct((frames * sub_rows, two_fine), jnp.float32),
-        (voltages, *fixed),
-        flops=frames * flops,
-    )
-
-    after = ()
-    got = []
-    for step in [*range(1, chips), 0]:
-        made = call(
-            functools.partial(sum_kernel, step, each, count),
-            jax.ShapeDtypeStruct((each * sub_rows + PAD_ROWS, two_fine), jnp.bfloat16),
-            (other, *fixed, other_packed, part, *after),
-            flops=each * flops,
-        )
-        after = (made,)
-        if step:
-            made = lax.ppermute(made, "chip", [(source, source ^ step) for source in range(chips)])
-        got.append(made)
+
+    piece = jax.ShapeDtypeStruct((each * sub_rows + PAD_ROWS, two_fine), jnp.bfloat16)
+    flops = 2 * each * sub_rows * taps * two_fine * two_fine
+    grid, digits, *far = call(
+        functools.partial(grid_kernel, count=count),
+        (
+            jax.ShapeDtypeStruct((sub_rows, width), jnp.bfloat16),
+            jax.ShapeDtypeStruct((PAD_ROWS, two_fine), jnp.bfloat16),
+            *[piece] * (chips - 1),
+        ),
+        (voltages, other, filter_taps, kernel_rows, kernel_cols, packed, other_packed),
+        flops=4 * sub_rows * station_rows * width + (chips - 1) * flops,
+    )
+    got = [call(near_kernel, piece, (grid, filter_taps, digits), flops=flops)]
+    for step, part in enumerate(far, 1):
+        got.append(lax.ppermute(part, "chip", [(source, source ^ step) for source in range(chips)]))
     image = call(
         functools.partial(image_kernel, each),
         jax.ShapeDtypeStruct((row_total, MW), jnp.float32),

time: 25.2 us -> 25.1 us (level)
  waiting for transfers between devices: 3.47 us -> 4.76 us
  Pallas kernels: 3.58 us -> 2.85 us
  local copies, waits for them, and re-layouts: 1.13 us -> 0.7 us
    ppermute x1, waiting for transfers between devices: 0.01 us -> 1.11 us  [local(): other_packed = lax.ppermute(packed, 'core', swap)]
    pallas_call x7 -> x5, Pallas kernels: 3.58 us -> 2.85 us  [call(): pl.pallas_call(kernel, out_shape=shape, in_specs=[pl.BlockSpec(memory_spa...]
    unnamed x12, local copies, waits for them, and re-layouts: 1.13 us -> 0.7 us
  transfers between devices with their start and end apart: 3 -> 3, of which waited for: 1 -> 3; matrix products, arithmetic and copies ran while one was open for 0% -> 0% of each run, Pallas kernels for 8% -> 3%
where the time goes in v1:
time: 25.1 us; the launch traced here: 24.9 us
  blocking collectives  13.1 us (52%)
  waiting for transfers between devices  4.76 us (19%)
  starting transfers between devices  3.44 us (14%)
  Pallas kernels  2.85 us (11%)
  local copies, waits for them, and re-layouts  0.7 us (3%)
    all_to_all x1, blocking collectives, local(): lax.all_to_all(image, EVERYONE, split_axis=0, concat_axis=0, tiled=True)  13.1 us
    ppermute x1, waiting for transfers between devices, local(): lax.ppermute(part, 'chip', [(source, source ^ step) for source in range(c...  3.52 us
    ppermute x1, starting transfers between devices, local(): lax.ppermute(part, 'chip', [(source, source ^ step) for source in range(c...  2.92 us
    pallas_call x5, Pallas kernels, call(): pl.pallas_call(kernel, out_shape=shape, in_specs=[pl.BlockSpec(memory_spa...  2.85 us
    ppermute x1, waiting for transfers between devices, local(): other_packed = lax.ppermute(packed, 'core', swap)  1.11 us
    unnamed x12, local copies, waits for them, and re-layouts  0.7 us
  transfers between devices with their start and end apart: 3, of which 3 were waited for; matrix products, arithmetic and copies ran while one was open for 0% of the time, Pallas kernels for 3%

profile of v1, /device:TPU:0, one launch (start us, length us, event | category | flops | bytes accessed | tf_op | source)
XLA Modules:
  0.0 24.9 jit_solution(156639316316003443)
XLA Ops:
  0.0 0.5 %collective-permute-start = (bf16[1,2,64,3840]{3,2,1,0:T(8,128)(2,1)}, bf16[1,2,64,3840]{3,2,1,0:T(8,128)(2,1)S(1)}, u32[]{:S(2)}, u32[]{:S(2)}) collective-permute-start(bf16[1,2,64,3840]{3,2,1,0:T(8,128)(2,1)} %own_ref.1), channel_id=1, source_target_pairs={{0,1},{1,0},{2,3},{3,2},{4,5},{5,4},{6,7},{7,6},{8,9},{9,8},{10,11... | collective-permute-start | bytes 2949128 | tf_op jit(solution)/shard_map/ppermute | solution.py:194
  0.5 0.0 copy-start.4
  0.5 0.0 copy-start.5
  0.5 0.7 %copy-done.4 = s32[2,32,1]{1,2,0:T(1,128)S(1)} copy-done((s32[2,32,1]{1,2,0:T(1,128)S(1)}, s32[2,32,1]{1,2,0:T(1,128)}, u32[]{:S(2)}) %copy-start.4) | copy-done | bytes 280
  1.1 0.0 copy-done.5
  1.1 0.0 copy-start
  1.1 0.0 copy-start.1
  1.1 0.0 copy-start.2
  1.1 0.0 copy-start.3
  1.2 0.4 %shard_map.64 = (bf16[64,192]{1,0:T(8,128)(2,1)S(1)}, bf16[256,192]{1,0:T(8,128)(2,1)S(1)}, s32[8,128]{1,0:T(8,128)S(1)}) custom-call(s32[1,64]{1,0:T(1,128)S(1)} %bitcast.5, s32[2,32]{1,0:T(2,128)S(1)} %bitcast.4), custom_call_target="tpu_custom_call" | custom-call | flops 2013265920 | bytes 127488 | tf_op jit(solution)/shard_map/pallas_call | solution.py:170
  1.6 0.1 collective-permute-start.1
  1.6 1.1 %collective-permute-done.1.other_packed_ref = s32[8,128]{1,0:T(8,128)S(1)} collective-permute-done((s32[8,128]{1,0:T(8,128)S(1)}, s32[8,128]{1,0:T(8,128)S(1)}, u32[]{:S(2)}, u32[]{:S(2)}) %collective-permute-start.1) | collective-permute-done | bytes 4128 | tf_op jit(solution)/shard_map/ppermute | solution.py:205
  2.7 0.1 collective-permute-done.other_ref
  2.9 0.0 copy-done
  2.9 0.0 copy-done.1
  2.9 0.0 copy-done.2
  2.9 0.0 copy-done.3
  2.9 1.0 %shard_map.65 = (bf16[64,3840]{1,0:T(8,128)(2,1)S(1)}, bf16[16,256]{1,0:T(8,128)(2,1)S(1)}, bf16[272,256]{1,0:T(8,128)(2,1)S(1)}) custom-call(bf16[1,2,64,3840]{3,2,1,0:T(8,128)(2,1)S(1)} %copy-done.1, bf16[1,2,64,3840]{3,2,1,0:T(8,128)(2,1)S(1)} %collective-permute-done.other_ref, bf16[8,256,256]{2,1,0:T(8,128)(2,1)S(1)} %copy-done, ...), custom_call_target="tpu_custom_call" | custom-call | flops 331350016 | bytes 3694592 | tf_op jit(solution)/shard_map/pallas_call | solution.py:170
  3.9 2.9 %collective-permute-start.2 = (bf16[272,256]{1,0:T(8,128)(2,1)S(1)}, bf16[272,256]{1,0:T(8,128)(2,1)S(1)}, u32[]{:S(2)}, u32[]{:S(2)}) collective-permute-start(bf16[272,256]{1,0:T(8,128)(2,1)S(1)} %get-tuple-element.14), channel_id=1, source_target_pairs={{0,2},{2,0},{1,3},{3,1},{4,6},{6,4},{5,7},{7,5},{8,10},{10,8},{9,1... | collective-permute-start | bytes 417800 | tf_op jit(solution)/shard_map/ppermute | solution.py:221
  6.8 0.4 %shard_map.66.refs_0_ = bf16[272,256]{1,0:T(8,128)(2,1)S(1)} custom-call(bf16[64,3840]{1,0:T(8,128)(2,1)S(1)} %get-tuple-element.12.grid_ref, bf16[8,256,256]{2,1,0:T(8,128)(2,1)S(1)} %copy-done, bf16[16,256]{1,0:T(8,128)(2,1)S(1)} %get-tuple-element.13.digits_ref), custom_call_target="tpu_custom_call" | custom-call | flops 268435456 | bytes 1687552 | tf_op jit(solution)/shard_map/pallas_call | solution.py:170
  7.2 3.5 %collective-permute-done.2.refs_1_ = bf16[272,256]{1,0:T(8,128)(2,1)S(1)} collective-permute-done((bf16[272,256]{1,0:T(8,128)(2,1)S(1)}, bf16[272,256]{1,0:T(8,128)(2,1)S(1)}, u32[]{:S(2)}, u32[]{:S(2)}) %collective-permute-start.2) | collective-permute-done | bytes 139296 | tf_op jit(solution)/shard_map/ppermute | solution.py:221
  10.8 0.5 %shard_map.67 = f32[32,128]{1,0:T(8,128)S(1)} custom-call(bf16[272,256]{1,0:T(8,128)(2,1)S(1)} %shard_map.66.refs_0_, bf16[272,256]{1,0:T(8,128)(2,1)S(1)} %collective-permute-done.2.refs_1_, bf16[64,192]{1,0:T(8,128)(2,1)S(1)} %get-tuple-element.15.refs_2_, bf16[256,192]{1,0:T(8,128)(2,1)S(1)} %get-tuple-element.16.refs_3_), custom_call_target="tpu_custom_call" | custom-call | bytes 417792 | tf_op jit(solution)/shard_map/pallas_call | solution.py:170
  11.2 13.1 %all_to_all.9.in_ref = f32[32,1,128]{2,1,0:T(1,128)S(1)} all-to-all(f32[32,1,128]{2,1,0:T(1,128)S(1)} %bitcast.3), channel_id=1, replica_groups=mesh['role'=2,'band'=4,'chip'=2,'core'=2] {'role','band','chip','core'}, dimensions={0} | all-to-all | bytes 32768 | tf_op jit(solution)/shard_map/all_to_all | solution.py:227
  24.3 0.5 %shard_map.68 = f32[1,128]{1,0:T(1,128)} custom-call(f32[32,1,128]{2,1,0:T(1,128)S(1)} %all_to_all.9.in_ref), custom_call_target="tpu_custom_call" | custom-call | bytes 16896 | tf_op jit(solution)/shard_map/pallas_call | solution.py:170
Async XLA Ops:
  0.0 2.9 %collective-permute-start = (bf16[1,2,64,3840]{3,2,1,0:T(8,128)(2,1)}, bf16[1,2,64,3840]{3,2,1,0:T(8,128)(2,1)S(1)}, u32[]{:S(2)}, u32[]{:S(2)}) collective-permute-start(bf16[1,2,64,3840]{3,2,1,0:T(8,128)(2,1)} %own_ref.1), channel_id=1, source_target_pairs={{0,1},{1,0},{2,3},{3,2},{4,5},{5,4},{6,7},{7,6},{8,9},{9,8},{10,11... | collective-permute-start | bytes 2949128 | tf_op jit(solution)/shard_map/ppermute | solution.py:194
  0.5 0.7 %copy-start.4 = (s32[2,32,1]{1,2,0:T(1,128)S(1)}, s32[2,32,1]{1,2,0:T(1,128)}, u32[]{:S(2)}) copy-start(s32[2,32,1]{1,2,0:T(1,128)} %param.11) | copy-start | bytes 772
  0.5 0.7 %copy-start.5 = (s32[64]{0:T(128)S(1)}, s32[64]{0:T(128)}, u32[]{:S(2)}) copy-start(s32[64]{0:T(128)} %param.7) | copy-start | bytes 772
  1.1 1.7 %copy-start = (bf16[8,256,256]{2,1,0:T(8,128)(2,1)S(1)}, bf16[8,256,256]{2,1,0:T(8,128)(2,1)}, u32[]{:S(2)}) copy-start(bf16[8,256,256]{2,1,0:T(8,128)(2,1)} %taps_ref.3) | copy-start | bytes 3145732
  1.1 1.7 %copy-start.1 = (bf16[1,2,64,3840]{3,2,1,0:T(8,128)(2,1)S(1)}, bf16[1,2,64,3840]{3,2,1,0:T(8,128)(2,1)}, u32[]{:S(2)}) copy-start(bf16[1,2,64,3840]{3,2,1,0:T(8,128)(2,1)} %own_ref.1) | copy-start | bytes 2949124
  1.1 1.7 %copy-start.2 = (bf16[1,1,32,256]{3,2,1,0:T(8,128)(2,1)S(1)}, bf16[1,1,32,256]{3,2,1,0:T(8,128)(2,1)}, u32[]{:S(2)}) copy-start(bf16[1,1,32,256]{3,2,1,0:T(8,128)(2,1)} %rows_ref.1) | copy-start | bytes 49156
  1.1 1.7 %copy-start.3 = (bf16[1,1,32,256]{3,2,1,0:T(8,128)(2,1)S(1)}, bf16[1,1,32,256]{3,2,1,0:T(8,128)(2,1)}, u32[]{:S(2)}) copy-start(bf16[1,1,32,256]{3,2,1,0:T(8,128)(2,1)} %cols_ref.1) | copy-start | bytes 49156
  1.6 1.2 %collective-permute-start.1 = (s32[8,128]{1,0:T(8,128)S(1)}, s32[8,128]{1,0:T(8,128)S(1)}, u32[]{:S(2)}, u32[]{:S(2)}) collective-permute-start(s32[8,128]{1,0:T(8,128)S(1)} %get-tuple-element.11.packed_ref), channel_id=1, source_target_pairs={{0,1},{1,0},{2,3},{3,2},{4,5},{5,4},{6,7},{7,6},{8,9},{9,8},{10,11... | collective-permute-start | bytes 12296 | tf_op jit(solution)/shard_map/ppermute | solution.py:205
  3.9 6.9 %collective-permute-start.2 = (bf16[272,256]{1,0:T(8,128)(2,1)S(1)}, bf16[272,256]{1,0:T(8,128)(2,1)S(1)}, u32[]{:S(2)}, u32[]{:S(2)}) collective-permute-start(bf16[272,256]{1,0:T(8,128)(2,1)S(1)} %get-tuple-element.14), channel_id=1, source_target_pairs={{0,2},{2,0},{1,3},{3,1},{4,6},{6,4},{5,7},{7,5},{8,10},{10,8},{9,1... | collective-permute-start | bytes 417800 | tf_op jit(solution)/shard_map/ppermute | solution.py:221

commit v2 on v0

--- a/solution.py
+++ b/solution.py
@@ -165,8 +165,12 @@
     out_ref[...] = lax.dot_general(left, right, (((1,), (1,)), ((), ())), preferred_element_type=jnp.float32)
 
 
-def final_kernel(scale_factor, in_ref, out_ref):
-    out_ref[...] = jnp.sum(in_ref[...], axis=0) * scale_factor
+def scale_kernel(scale_factor, _, out_ref):
+    out_ref[...] = jnp.full(out_ref.shape, scale_factor, out_ref.dtype)
+
+
+def final_kernel(in_ref, scale_ref, out_ref):
+    out_ref[...] = jnp.sum(in_ref[...], axis=0) * scale_ref[...]
 
 
 def call(kernel, shape, args, flops=0):
@@ -239,11 +243,9 @@
         (*got, *tables),
     )
     rows = lax.all_to_all(image, EVERYONE, split_axis=0, concat_axis=0, tiled=True)
-    return call(
-        functools.partial(final_kernel, scale_factor),
-        jax.ShapeDtypeStruct((ROWS_DEV, MW), jnp.float32),
-        (rows.reshape(-1, ROWS_DEV, MW),),
-    )
+    row = jax.ShapeDtypeStruct((ROWS_DEV, MW), jnp.float32)
+    scale = call(functools.partial(scale_kernel, scale_factor), row, (image,), flops=2 * image.size * row_total)
+    return call(final_kernel, row, (rows.reshape(-1, ROWS_DEV, MW), scale))
 
 
 def solution(mesh):

time: 25.2 us -> 26.1 us (1.036)
  blocking collectives: 13.1 us -> 0 us
  waiting for transfers between devices: 3.47 us -> 9.85 us
  starting transfers between devices: 3.54 us -> 9.64 us
  Pallas kernels: 3.58 us -> 4.96 us
    all_to_all x1 -> x0, blocking collectives: 13.1 us -> none  [local(): lax.all_to_all(image, EVERYONE, split_axis=0, concat_axis=0, tiled=True)]
    all_to_all x0 -> x1, waiting for transfers between devices: none -> 6.39 us  [local(): lax.all_to_all(image, EVERYONE, split_axis=0, concat_axis=0, tiled=True)]
    all_to_all x0 -> x1, starting transfers between devices: none -> 6.1 us  [local(): lax.all_to_all(image, EVERYONE, split_axis=0, concat_axis=0, tiled=True)]
    pallas_call x7 -> x8, Pallas kernels: 3.58 us -> 4.96 us  [call(): pl.pallas_call(kernel, out_shape=shape, in_specs=[pl.BlockSpec(memory_spa...]
  transfers between devices with their start and end apart: 3 -> 4, of which waited for: 1 -> 2; matrix products, arithmetic and copies ran while one was open for 0% -> 0% of each run, Pallas kernels for 8% -> 10%
where the time goes in v2:
time: 26.1 us; the launch traced here: 25.6 us
  waiting for transfers between devices  9.85 us (38%)
  starting transfers between devices  9.64 us (37%)
  Pallas kernels  4.96 us (19%)
  local copies, waits for them, and re-layouts  1.13 us (4%)
    all_to_all x1, waiting for transfers between devices, local(): lax.all_to_all(image, EVERYONE, split_axis=0, concat_axis=0, tiled=True)  6.39 us
    all_to_all x1, starting transfers between devices, local(): lax.all_to_all(image, EVERYONE, split_axis=0, concat_axis=0, tiled=True)  6.1 us
    pallas_call x8, Pallas kernels, call(): pl.pallas_call(kernel, out_shape=shape, in_specs=[pl.BlockSpec(memory_spa...  4.96 us
    ppermute x1, waiting for transfers between devices, local(): lax.ppermute(made, 'chip', [(source, source ^ step) for source in range(c...  3.46 us
    ppermute x1, starting transfers between devices, local(): lax.ppermute(made, 'chip', [(source, source ^ step) for source in range(c...  2.81 us
    unnamed x12, local copies, waits for them, and re-layouts  1.13 us
  transfers between devices with their start and end apart: 4, of which 2 were waited for; matrix products, arithmetic and copies ran while one was open for 0% of the time, Pallas kernels for 10%

profile of v2, /device:TPU:0, one launch (start us, length us, event | category | flops | bytes accessed | tf_op | source)
XLA Modules:
  0.0 25.6 jit_solution(10825579081594398782)
XLA Ops:
  0.0 0.0 copy-start.1
  0.0 0.0 copy-start
  0.0 0.5 %collective-permute-start = (bf16[1,2,64,3840]{3,2,1,0:T(8,128)(2,1)}, bf16[1,2,64,3840]{3,2,1,0:T(8,128)(2,1)S(1)}, u32[]{:S(2)}, u32[]{:S(2)}) collective-permute-start(bf16[1,2,64,3840]{3,2,1,0:T(8,128)(2,1)} %volt_ref.1), channel_id=1, source_target_pairs={{0,1},{1,0},{2,3},{3,2},{4,5},{5,4},{6,7},{7,6},{8,9},{9,8},{10,11... | collective-permute-start | bytes 2949128 | tf_op jit(solution)/shard_map/ppermute | solution.py:202
  0.5 0.4 %shard_map.64 = (bf16[64,192]{1,0:T(8,128)(2,1)S(1)}, bf16[256,192]{1,0:T(8,128)(2,1)S(1)}) custom-call(), custom_call_target="tpu_custom_call" | custom-call | flops 2013265920 | bytes 122880 | tf_op jit(solution)/shard_map/pallas_call | solution.py:178
  0.9 0.0 copy-start.4
  0.9 0.0 copy-start.5
  0.9 0.7 %copy-done.4 = s32[2,32,1]{1,2,0:T(1,128)S(1)} copy-done((s32[2,32,1]{1,2,0:T(1,128)S(1)}, s32[2,32,1]{1,2,0:T(1,128)}, u32[]{:S(2)}) %copy-start.4) | copy-done | bytes 280
  1.5 0.0 copy-done.5
  1.5 0.0 copy-start.2
  1.5 0.0 copy-start.3
  1.5 0.3 %collective-permute-start.1 = (s32[8,128]{1,0:T(8,128)S(1)}, s32[8,128]{1,0:T(8,128)S(1)}, u32[]{:S(2)}, u32[]{:S(2)}) collective-permute-start(s32[8,128]{1,0:T(8,128)S(1)} %shard_map.65.packed_ref.own_ref), channel_id=1, source_target_pairs={{0,1},{1,0},{2,3},{3,2},{4,5},{5,4},{6,7},{7,6},{8,9},{9,8},{10,11... | collective-permute-start | bytes 12296 | tf_op jit(solution)/shard_map/ppermute | solution.py:217
  1.8 0.0 copy-done.1
  1.8 0.0 copy-done
  1.8 0.4 %copy-done.2 = bf16[1,1,32,256]{3,2,1,0:T(8,128)(2,1)S(1)} copy-done((bf16[1,1,32,256]{3,2,1,0:T(8,128)(2,1)S(1)}, bf16[1,1,32,256]{3,2,1,0:T(8,128)(2,1)}, u32[]{:S(2)}) %copy-start.2) | copy-done | bytes 16408
  2.3 0.0 copy-done.3
  2.3 0.9 %shard_map.66.part_ref = f32[512,256]{1,0:T(8,128)S(1)} custom-call(bf16[1,2,64,3840]{3,2,1,0:T(8,128)(2,1)S(1)} %copy-done.1, bf16[8,256,256]{2,1,0:T(8,128)(2,1)S(1)} %copy-done, bf16[1,1,32,256]{3,2,1,0:T(8,128)(2,1)S(1)} %copy-done.2, bf16[1,1,32,256]{3,2,1,0:T(8,128)(2,1)S(1)} %copy-done.3, s32[8,128]{1,0:T(8,128)S(1)} %shard_map.65.packed_ref.own_ref), custom_call_target="tpu_custom_call" | custom-call | flops 536870912 | bytes 2592768 | tf_op jit(solution)/shard_map/pallas_call | solution.py:178
  3.2 0.0 collective-permute-done.1.packed_ref
  3.2 0.0 collective-permute-done.volt_ref
  3.2 0.6 %shard_map.67.refs_0_ = bf16[272,256]{1,0:T(8,128)(2,1)S(1)} custom-call(bf16[1,2,64,3840]{3,2,1,0:T(8,128)(2,1)S(1)} %collective-permute-done.volt_ref, bf16[8,256,256]{2,1,0:T(8,128)(2,1)S(1)} %copy-done, bf16[1,1,32,256]{3,2,1,0:T(8,128)(2,1)S(1)} %copy-done.2, bf16[1,1,32,256]{3,2,1,0:T(8,128)(2,1)S(1)} %copy-done.3, ...), custom_call_target="tpu_custom_call" | custom-call | flops 268435456 | bytes 2736128 | tf_op jit(solution)/shard_map/pallas_call | solution.py:178
  3.8 2.8 %collective-permute-start.2 = (bf16[272,256]{1,0:T(8,128)(2,1)S(1)}, bf16[272,256]{1,0:T(8,128)(2,1)S(1)}, u32[]{:S(2)}, u32[]{:S(2)}) collective-permute-start(bf16[272,256]{1,0:T(8,128)(2,1)S(1)} %shard_map.67.refs_0_), channel_id=1, source_target_pairs={{0,2},{2,0},{1,3},{3,1},{4,6},{6,4},{5,7},{7,5},{8,10},{10,8},{9,1... | collective-permute-start | bytes 417800 | tf_op jit(solution)/shard_map/ppermute | solution.py:238
  6.7 0.6 %shard_map.68.refs_1_ = bf16[272,256]{1,0:T(8,128)(2,1)S(1)} custom-call(bf16[1,2,64,3840]{3,2,1,0:T(8,128)(2,1)S(1)} %collective-permute-done.volt_ref, bf16[8,256,256]{2,1,0:T(8,128)(2,1)S(1)} %copy-done, bf16[1,1,32,256]{3,2,1,0:T(8,128)(2,1)S(1)} %copy-done.2, bf16[1,1,32,256]{3,2,1,0:T(8,128)(2,1)S(1)} %copy-done.3, ...), custom_call_target="tpu_custom_call" | custom-call | flops 268435456 | bytes 2875392 | tf_op jit(solution)/shard_map/pallas_call | solution.py:178
  7.3 3.5 %collective-permute-done.2.refs_0_ = bf16[272,256]{1,0:T(8,128)(2,1)S(1)} collective-permute-done((bf16[272,256]{1,0:T(8,128)(2,1)S(1)}, bf16[272,256]{1,0:T(8,128)(2,1)S(1)}, u32[]{:S(2)}, u32[]{:S(2)}) %collective-permute-start.2) | collective-permute-done | bytes 139296 | tf_op jit(solution)/shard_map/ppermute | solution.py:238
  10.7 1.1 %shard_map.69._ = f32[32,128]{1,0:T(8,128)} custom-call(bf16[272,256]{1,0:T(8,128)(2,1)S(1)} %collective-permute-done.2.refs_0_, bf16[272,256]{1,0:T(8,128)(2,1)S(1)} %shard_map.68.refs_1_, bf16[64,192]{1,0:T(8,128)(2,1)S(1)} %get-tuple-element.7._.refs_2_, bf16[256,192]{1,0:T(8,128)(2,1)S(1)} %get-tuple-element.8.refs_3_), custom_call_target="tpu_custom_call" | custom-call | bytes 417792 | tf_op jit(solution)/shard_map/pallas_call | solution.py:178
  11.8 6.1 %all-to-all-start = ((f32[32,1,128]{2,1,0:T(1,128)}), f32[32,1,128]{2,1,0:T(1,128)S(1)}, u32[]{:S(2)}, u32[]{:S(2)}) async-start(f32[32,1,128]{2,1,0:T(1,128)} %bitcast.2), calls=%async_computation | async-start | bytes 32768 | tf_op jit(solution)/shard_map/all_to_all | solution.py:245
  17.9 0.8 %shard_map.70.scale_ref = f32[1,128]{1,0:T(1,128)S(1)} custom-call(f32[32,128]{1,0:T(8,128)} %shard_map.69._), custom_call_target="tpu_custom_call" | custom-call | flops 262144 | bytes 16896 | tf_op jit(solution)/shard_map/pallas_call | solution.py:178
  18.7 6.4 %all-to-all-done.in_ref = f32[32,1,128]{2,1,0:T(1,128)S(1)} async-done(((f32[32,1,128]{2,1,0:T(1,128)}), f32[32,1,128]{2,1,0:T(1,128)S(1)}, u32[]{:S(2)}, u32[]{:S(2)}) %all-to-all-start) | async-done | bytes 16416 | tf_op jit(solution)/shard_map/all_to_all | solution.py:245
  25.1 0.5 %shard_map.71 = f32[1,128]{1,0:T(1,128)} custom-call(f32[32,1,128]{2,1,0:T(1,128)S(1)} %all-to-all-done.in_ref, f32[1,128]{1,0:T(1,128)S(1)} %shard_map.70.scale_ref), custom_call_target="tpu_custom_call" | custom-call | bytes 17408 | tf_op jit(solution)/shard_map/pallas_call | solution.py:178
  (1 shorter events, 0.0 us)
Async XLA Ops:
  0.0 1.8 %copy-start.1 = (bf16[1,2,64,3840]{3,2,1,0:T(8,128)(2,1)S(1)}, bf16[1,2,64,3840]{3,2,1,0:T(8,128)(2,1)}, u32[]{:S(2)}) copy-start(bf16[1,2,64,3840]{3,2,1,0:T(8,128)(2,1)} %volt_ref.1) | copy-start | bytes 2949124
  0.0 1.8 %copy-start = (bf16[8,256,256]{2,1,0:T(8,128)(2,1)S(1)}, bf16[8,256,256]{2,1,0:T(8,128)(2,1)}, u32[]{:S(2)}) copy-start(bf16[8,256,256]{2,1,0:T(8,128)(2,1)} %taps_ref.5) | copy-start | bytes 3145732
  0.0 3.2 %collective-permute-start = (bf16[1,2,64,3840]{3,2,1,0:T(8,128)(2,1)}, bf16[1,2,64,3840]{3,2,1,0:T(8,128)(2,1)S(1)}, u32[]{:S(2)}, u32[]{:S(2)}) collective-permute-start(bf16[1,2,64,3840]{3,2,1,0:T(8,128)(2,1)} %volt_ref.1), channel_id=1, source_target_pairs={{0,1},{1,0},{2,3},{3,2},{4,5},{5,4},{6,7},{7,6},{8,9},{9,8},{10,11... | collective-permute-start | bytes 2949128 | tf_op jit(solution)/shard_map/ppermute | solution.py:202
  0.9 0.7 %copy-start.4 = (s32[2,32,1]{1,2,0:T(1,128)S(1)}, s32[2,32,1]{1,2,0:T(1,128)}, u32[]{:S(2)}) copy-start(s32[2,32,1]{1,2,0:T(1,128)} %param.11) | copy-start | bytes 772
  0.9 0.7 %copy-start.5 = (s32[64]{0:T(128)S(1)}, s32[64]{0:T(128)}, u32[]{:S(2)}) copy-start(s32[64]{0:T(128)} %param.7) | copy-start | bytes 772
  1.5 0.7 %copy-start.2 = (bf16[1,1,32,256]{3,2,1,0:T(8,128)(2,1)S(1)}, bf16[1,1,32,256]{3,2,1,0:T(8,128)(2,1)}, u32[]{:S(2)}) copy-start(bf16[1,1,32,256]{3,2,1,0:T(8,128)(2,1)} %rows_ref.5) | copy-start | bytes 49156
  1.5 0.7 %copy-start.3 = (bf16[1,1,32,256]{3,2,1,0:T(8,128)(2,1)S(1)}, bf16[1,1,32,256]{3,2,1,0:T(8,128)(2,1)}, u32[]{:S(2)}) copy-start(bf16[1,1,32,256]{3,2,1,0:T(8,128)(2,1)} %cols_ref.5) | copy-start | bytes 49156
  1.5 1.6 %collective-permute-start.1 = (s32[8,128]{1,0:T(8,128)S(1)}, s32[8,128]{1,0:T(8,128)S(1)}, u32[]{:S(2)}, u32[]{:S(2)}) collective-permute-start(s32[8,128]{1,0:T(8,128)S(1)} %shard_map.65.packed_ref.own_ref), channel_id=1, source_target_pairs={{0,1},{1,0},{2,3},{3,2},{4,5},{5,4},{6,7},{7,6},{8,9},{9,8},{10,11... | collective-permute-start | bytes 12296 | tf_op jit(solution)/shard_map/ppermute | solution.py:217
  3.8 6.9 %collective-permute-start.2 = (bf16[272,256]{1,0:T(8,128)(2,1)S(1)}, bf16[272,256]{1,0:T(8,128)(2,1)S(1)}, u32[]{:S(2)}, u32[]{:S(2)}) collective-permute-start(bf16[272,256]{1,0:T(8,128)(2,1)S(1)} %shard_map.67.refs_0_), channel_id=1, source_target_pairs={{0,2},{2,0},{1,3},{3,1},{4,6},{6,4},{5,7},{7,5},{8,10},{10,8},{9,1... | collective-permute-start | bytes 417800 | tf_op jit(solution)/shard_map/ppermute | solution.py:238
  11.8 13.2 %all-to-all-start = ((f32[32,1,128]{2,1,0:T(1,128)}), f32[32,1,128]{2,1,0:T(1,128)S(1)}, u32[]{:S(2)}, u32[]{:S(2)}) async-start(f32[32,1,128]{2,1,0:T(1,128)} %bitcast.2), calls=%async_computation | async-start | bytes 32768 | tf_op jit(solution)/shard_map/all_to_all | solution.py:245

commit v3 on v0

--- a/solution.py
+++ b/solution.py
@@ -56,31 +56,28 @@
         out_ref[...] = jnp.concatenate([high, low, high], axis=1)
 
 
-def pack_kernel(flags_ref, cells_ref, _, out_ref):
-    out_ref[...] = jnp.zeros_like(out_ref)
-    out_ref[0:2, : cells_ref.shape[1]] = cells_ref[...]
-    out_ref[2:3, : flags_ref.shape[1]] = flags_ref[...]
-
-
-def gridding_weights(rows_ref, cols_ref, packed_ref, turn, stations):
+def pack_kernel(flags_ref, cells_ref, rows_ref, cols_ref, _, packed_ref, *weights_refs):
+    turn, turns = lax.axis_index(TURN), lax.axis_size(TURN)
+    count, lanes = cells_ref.shape[1], packed_ref.shape[1]
+    wide = jnp.concatenate([cells_ref[...]] * (lanes // count), axis=1)
+    lane = lax.broadcasted_iota(jnp.int32, wide.shape, 1)
+    wide = jnp.where((lane >= turn * count) & (lane < (turn + 1) * count), wide, 0)
+    packed_ref[...] = jnp.zeros_like(packed_ref)
+    packed_ref[0:2] = (wide // DIGIT).astype(jnp.float32)
+    packed_ref[2:4] = (wide % DIGIT).astype(jnp.float32)
+    packed_ref[4:5, : flags_ref.shape[1]] = flags_ref[...].astype(jnp.float32)
     both = jnp.concatenate([rows_ref[0, 0], cols_ref[0, 0]], axis=0).astype(jnp.float32)
-    weights = jnp.zeros((both.shape[0], stations), jnp.float32)
-    for group in range(lax.axis_size(TURN)):
-        weights = jnp.where(turn == group, both[:, group * stations : (group + 1) * stations], weights)
-    return (weights * packed_ref[2:3, :stations].astype(jnp.float32)).astype(jnp.bfloat16)
-
-
-def cell_digits(packed_refs, count, lanes):
-    turn = lax.axis_index(TURN)
-    digits = jnp.zeros((4, lanes), jnp.float32)
-    for index, packed in enumerate(packed_refs):
-        place = turn ^ index
-        wide = jnp.concatenate([packed[0:2, :count]] * (lanes // count), axis=1)
-        lane = lax.broadcasted_iota(jnp.int32, wide.shape, 1)
-        wide = jnp.where((lane >= place * count) & (lane < (place + 1) * count), wide, 0)
-        digits = digits + jnp.concatenate([wide // DIGIT, wide % DIGIT], axis=0).astype(jnp.float32)
-    digits = jnp.concatenate([digits, jnp.zeros((PAD_ROWS - 4, lanes), jnp.float32)], axis=0)
-    return digits.astype(jnp.bfloat16)
+    for index, weights_ref in enumerate(weights_refs):
+        stations = weights_ref.shape[1]
+        weights = jnp.zeros(weights_ref.shape, jnp.float32)
+        for group in range(turns):
+            piece = both[:, group * stations : (group + 1) * stations]
+            weights = jnp.where(turn ^ index == group, piece, weights)
+        weights_ref[...] = weights
+
+
+def flagged(weights_ref, packed_ref):
+    return (weights_ref[...] * packed_ref[4:5, : weights_ref.shape[1]]).astype(jnp.bfloat16)
 
 
 def gridded_frames(volt_ref, taps_ref, weights, firsts):
@@ -102,22 +99,23 @@
     ]
 
 
-def own_kernel(volt_ref, taps_ref, rows_ref, cols_ref, packed_ref, out_ref):
-    weights = gridding_weights(rows_ref, cols_ref, packed_ref, lax.axis_index(TURN), volt_ref.shape[2])
-    rows = weights.shape[0]
-    for frame, gridded in enumerate(gridded_frames(volt_ref, taps_ref, weights, range(out_ref.shape[0] // rows))):
+def own_kernel(volt_ref, taps_ref, weights_ref, packed_ref, out_ref):
+    rows = weights_ref.shape[0]
+    firsts = range(out_ref.shape[0] // rows)
+    for frame, gridded in enumerate(gridded_frames(volt_ref, taps_ref, flagged(weights_ref, packed_ref), firsts)):
         out_ref[frame * rows : (frame + 1) * rows] = gridded
 
 
-def sum_kernel(step, each, count, volt_ref, taps_ref, rows_ref, cols_ref, own_ref, packed_ref, part_ref, *refs):
+def sum_kernel(step, each, volt_ref, taps_ref, weights_ref, own_ref, packed_ref, part_ref, *refs):
     out_ref = refs[-1]
-    weights = gridding_weights(rows_ref, cols_ref, packed_ref, lax.axis_index(TURN) ^ 1, volt_ref.shape[2])
-    rows = weights.shape[0]
+    rows = weights_ref.shape[0]
     firsts = [(lax.axis_index("chip") ^ step) * each + frame for frame in range(each)]
-    for index, gridded in enumerate(gridded_frames(volt_ref, taps_ref, weights, firsts)):
+    for index, gridded in enumerate(gridded_frames(volt_ref, taps_ref, flagged(weights_ref, packed_ref), firsts)):
         held = part_ref[pl.ds(pl.multiple_of(firsts[index] * rows, rows), rows)]
         out_ref[index * rows : (index + 1) * rows] = (held + gridded).astype(jnp.bfloat16)
-    out_ref[each * rows :] = cell_digits((own_ref, packed_ref), count, out_ref.shape[1])
+    digits = own_ref[...] + packed_ref[...]
+    digits = jnp.concatenate([digits, jnp.zeros((PAD_ROWS - digits.shape[0], digits.shape[1]), jnp.float32)], axis=0)
+    out_ref[each * rows :] = digits.astype(jnp.bfloat16)
 
 
 def image_kernel(pairs_each, *refs):
@@ -191,7 +189,6 @@
     frames = width // two_fine - taps + 1
     scale_factor = 4.0 / math.sqrt(channels * sub_u * sub_v) / frames
     each = frames // chips
-    count = cell_index.shape[1]
     sub_rows = sub_u + sub_v
 
     swap = [(core, 1 - core) for core in range(CORES)]
@@ -205,18 +202,18 @@
         (),
         flops=2 * voltages.size * two_fine * taps,
     )
-    packed = call(
+    weights = jax.ShapeDtypeStruct((sub_rows, station_rows), jnp.float32)
+    packed, own_weights, other_weights = call(
         pack_kernel,
-        jax.ShapeDtypeStruct((8, -(-max(station_rows, count) // 128) * 128), jnp.int32),
-        (station_flags.reshape(1, -1), cell_index.reshape(2, -1), tables[0]),
+        (jax.ShapeDtypeStruct((8, two_fine), jnp.float32), weights, weights),
+        (station_flags.reshape(1, -1), cell_index.reshape(2, -1), kernel_rows, kernel_cols, tables[0]),
     )
     other_packed = lax.ppermute(packed, "core", swap)
-    fixed = (filter_taps, kernel_rows, kernel_cols, packed)
     flops = 2 * station_rows * taps * two_fine * two_fine
     part = call(
         own_kernel,
         jax.ShapeDtypeStruct((frames * sub_rows, two_fine), jnp.float32),
-        (voltages, *fixed),
+        (voltages, filter_taps, own_weights, packed),
         flops=frames * flops,
     )
 
@@ -224,9 +221,9 @@
     got = []
     for step in [*range(1, chips), 0]:
         made = call(
-            functools.partial(sum_kernel, step, each, count),
+            functools.partial(sum_kernel, step, each),
             jax.ShapeDtypeStruct((each * sub_rows + PAD_ROWS, two_fine), jnp.bfloat16),
-            (other, *fixed, other_packed, part, *after),
+            (other, filter_taps, other_weights, packed, other_packed, part, *after),
             flops=each * flops,
         )
         after = (made,)

time: 25.2 us -> 24.8 us (0.984)
  local copies, waits for them, and re-layouts: 1.13 us -> 0.69 us
  Pallas kernels: 3.58 us -> 3.84 us
    unnamed x12, local copies, waits for them, and re-layouts: 1.13 us -> 0.69 us
    pallas_call x7, Pallas kernels: 3.58 us -> 3.84 us  [call(): pl.pallas_call(kernel, out_shape=shape, in_specs=[pl.BlockSpec(memory_spa...]
  transfers between devices with their start and end apart: 3 -> 3, of which waited for: 1 -> 1; matrix products, arithmetic and copies ran while one was open for 0% -> 0% of each run, Pallas kernels for 8% -> 9%
where the time goes in v3:
time: 24.8 us; the launch traced here: 24.7 us
  blocking collectives  13.1 us (53%)
  Pallas kernels  3.84 us (15%)
  starting transfers between devices  3.55 us (14%)
  waiting for transfers between devices  3.47 us (14%)
  local copies, waits for them, and re-layouts  0.69 us (3%)
    all_to_all x1, blocking collectives, local(): lax.all_to_all(image, EVERYONE, split_axis=0, concat_axis=0, tiled=True)  13.1 us
    pallas_call x7, Pallas kernels, call(): pl.pallas_call(kernel, out_shape=shape, in_specs=[pl.BlockSpec(memory_spa...  3.84 us
    ppermute x1, waiting for transfers between devices, local(): lax.ppermute(made, 'chip', [(source, source ^ step) for source in range(c...  3.45 us
    ppermute x1, starting transfers between devices, local(): lax.ppermute(made, 'chip', [(source, source ^ step) for source in range(c...  2.82 us
    unnamed x12, local copies, waits for them, and re-layouts  0.69 us
  transfers between devices with their start and end apart: 3, of which 1 were waited for; matrix products, arithmetic and copies ran while one was open for 0% of the time, Pallas kernels for 9%

profile of v3, /device:TPU:0, one launch (start us, length us, event | category | flops | bytes accessed | tf_op | source)
XLA Modules:
  0.0 24.7 jit_solution(2582736033891244127)
XLA Ops:
  0.0 0.0 copy-start.1
  0.0 0.0 copy-start
  0.0 0.5 %collective-permute-start = (bf16[1,2,64,3840]{3,2,1,0:T(8,128)(2,1)}, bf16[1,2,64,3840]{3,2,1,0:T(8,128)(2,1)S(1)}, u32[]{:S(2)}, u32[]{:S(2)}) collective-permute-start(bf16[1,2,64,3840]{3,2,1,0:T(8,128)(2,1)} %volt_ref.1), channel_id=1, source_target_pairs={{0,1},{1,0},{2,3},{3,2},{4,5},{5,4},{6,7},{7,6},{8,9},{9,8},{10,11... | collective-permute-start | bytes 2949128 | tf_op jit(solution)/shard_map/ppermute | solution.py:195
  0.5 0.0 copy-start.2
  0.5 0.0 copy-start.3
  0.5 0.4 %shard_map.64 = (bf16[64,192]{1,0:T(8,128)(2,1)S(1)}, bf16[256,192]{1,0:T(8,128)(2,1)S(1)}) custom-call(), custom_call_target="tpu_custom_call" | custom-call | flops 2013265920 | bytes 122880 | tf_op jit(solution)/shard_map/pallas_call | solution.py:172
  0.9 0.0 copy-start.4
  0.9 0.0 copy-start.5
  0.9 0.5 %copy-done.2 = bf16[1,1,32,256]{3,2,1,0:T(8,128)(2,1)S(1)} copy-done((bf16[1,1,32,256]{3,2,1,0:T(8,128)(2,1)S(1)}, bf16[1,1,32,256]{3,2,1,0:T(8,128)(2,1)}, u32[]{:S(2)}) %copy-start.2) | copy-done | bytes 16408
  1.3 0.0 copy-done.3
  1.3 0.2 copy-done.4
  1.5 0.0 copy-done.5
  1.5 0.3 %shard_map.65 = (f32[8,256]{1,0:T(8,128)S(1)}, f32[64,64]{1,0:T(8,128)S(1)}, f32[64,64]{1,0:T(8,128)S(1)}) custom-call(s32[1,64]{1,0:T(1,128)S(1)} %bitcast.5, s32[2,32]{1,0:T(2,128)S(1)} %bitcast.4, bf16[1,1,32,256]{3,2,1,0:T(8,128)(2,1)S(1)} %copy-done.2, bf16[1,1,32,256]{3,2,1,0:T(8,128)(2,1)S(1)} %copy-done.3, ...), custom_call_target="tpu_custom_call" | custom-call | bytes 98816 | tf_op jit(solution)/shard_map/pallas_call | solution.py:172
  1.8 0.3 %collective-permute-start.1 = (f32[8,256]{1,0:T(8,128)S(1)}, f32[8,256]{1,0:T(8,128)S(1)}, u32[]{:S(2)}, u32[]{:S(2)}) collective-permute-start(f32[8,256]{1,0:T(8,128)S(1)} %get-tuple-element.12.packed_ref.own_ref), channel_id=1, source_target_pairs={{0,1},{1,0},{2,3},{3,2},{4,5},{5,4},{6,7},{7,6},{8,9},{9,8},{10,11... | collective-permute-start | bytes 24584 | tf_op jit(solution)/shard_map/ppermute | solution.py:211
  2.1 0.0 copy-done.1
  2.1 0.0 copy-done
  2.1 0.9 %shard_map.66.part_ref = f32[512,256]{1,0:T(8,128)S(1)} custom-call(bf16[1,2,64,3840]{3,2,1,0:T(8,128)(2,1)S(1)} %copy-done.1, bf16[8,256,256]{2,1,0:T(8,128)(2,1)S(1)} %copy-done, f32[64,64]{1,0:T(8,128)S(1)} %get-tuple-element.13.weights_ref, f32[8,256]{1,0:T(8,128)S(1)} %get-tuple-element.12.packed_ref.own_ref), custom_call_target="tpu_custom_call" | custom-call | flops 536870912 | bytes 2580480 | tf_op jit(solution)/shard_map/pallas_call | solution.py:172
  3.0 0.0 collective-permute-done.1.packed_ref
  3.0 0.0 collective-permute-done.volt_ref
  3.0 0.6 %shard_map.67.refs_0_ = bf16[272,256]{1,0:T(8,128)(2,1)S(1)} custom-call(bf16[1,2,64,3840]{3,2,1,0:T(8,128)(2,1)S(1)} %collective-permute-done.volt_ref, bf16[8,256,256]{2,1,0:T(8,128)(2,1)S(1)} %copy-done, f32[64,64]{1,0:T(8,128)S(1)} %get-tuple-element.11.weights_ref, f32[8,256]{1,0:T(8,128)S(1)} %get-tuple-element.12.packed_ref.own_ref, ...), custom_call_target="tpu_custom_call" | custom-call | flops 268435456 | bytes 2727936 | tf_op jit(solution)/shard_map/pallas_call | solution.py:172
  3.7 2.8 %collective-permute-start.2 = (bf16[272,256]{1,0:T(8,128)(2,1)S(1)}, bf16[272,256]{1,0:T(8,128)(2,1)S(1)}, u32[]{:S(2)}, u32[]{:S(2)}) collective-permute-start(bf16[272,256]{1,0:T(8,128)(2,1)S(1)} %shard_map.67.refs_0_), channel_id=1, source_target_pairs={{0,2},{2,0},{1,3},{3,1},{4,6},{6,4},{5,7},{7,5},{8,10},{10,8},{9,1... | collective-permute-start | bytes 417800 | tf_op jit(solution)/shard_map/ppermute | solution.py:231
  6.5 0.6 %shard_map.68.refs_1_ = bf16[272,256]{1,0:T(8,128)(2,1)S(1)} custom-call(bf16[1,2,64,3840]{3,2,1,0:T(8,128)(2,1)S(1)} %collective-permute-done.volt_ref, bf16[8,256,256]{2,1,0:T(8,128)(2,1)S(1)} %copy-done, f32[64,64]{1,0:T(8,128)S(1)} %get-tuple-element.11.weights_ref, f32[8,256]{1,0:T(8,128)S(1)} %get-tuple-element.12.packed_ref.own_ref, ...), custom_call_target="tpu_custom_call" | custom-call | flops 268435456 | bytes 2867200 | tf_op jit(solution)/shard_map/pallas_call | solution.py:172
  7.1 3.5 %collective-permute-done.2.refs_0_ = bf16[272,256]{1,0:T(8,128)(2,1)S(1)} collective-permute-done((bf16[272,256]{1,0:T(8,128)(2,1)S(1)}, bf16[272,256]{1,0:T(8,128)(2,1)S(1)}, u32[]{:S(2)}, u32[]{:S(2)}) %collective-permute-start.2) | collective-permute-done | bytes 139296 | tf_op jit(solution)/shard_map/ppermute | solution.py:231
  10.6 0.5 %shard_map.69 = f32[32,128]{1,0:T(8,128)S(1)} custom-call(bf16[272,256]{1,0:T(8,128)(2,1)S(1)} %collective-permute-done.2.refs_0_, bf16[272,256]{1,0:T(8,128)(2,1)S(1)} %shard_map.68.refs_1_, bf16[64,192]{1,0:T(8,128)(2,1)S(1)} %get-tuple-element.10._.refs_2_, bf16[256,192]{1,0:T(8,128)(2,1)S(1)} %get-tuple-element.14.refs_3_), custom_call_target="tpu_custom_call" | custom-call | bytes 417792 | tf_op jit(solution)/shard_map/pallas_call | solution.py:172
  11.0 13.1 %all_to_all.9.in_ref = f32[32,1,128]{2,1,0:T(1,128)S(1)} all-to-all(f32[32,1,128]{2,1,0:T(1,128)S(1)} %bitcast.3), channel_id=1, replica_groups=mesh['role'=2,'band'=4,'chip'=2,'core'=2] {'role','band','chip','core'}, dimensions={0} | all-to-all | bytes 32768 | tf_op jit(solution)/shard_map/all_to_all | solution.py:238
  24.1 0.5 %shard_map.70 = f32[1,128]{1,0:T(1,128)} custom-call(f32[32,1,128]{2,1,0:T(1,128)S(1)} %all_to_all.9.in_ref), custom_call_target="tpu_custom_call" | custom-call | bytes 16896 | tf_op jit(solution)/shard_map/pallas_call | solution.py:172
Async XLA Ops:
  0.0 2.1 %copy-start.1 = (bf16[1,2,64,3840]{3,2,1,0:T(8,128)(2,1)S(1)}, bf16[1,2,64,3840]{3,2,1,0:T(8,128)(2,1)}, u32[]{:S(2)}) copy-start(bf16[1,2,64,3840]{3,2,1,0:T(8,128)(2,1)} %volt_ref.1) | copy-start | bytes 2949124
  0.0 2.1 %copy-start = (bf16[8,256,256]{2,1,0:T(8,128)(2,1)S(1)}, bf16[8,256,256]{2,1,0:T(8,128)(2,1)}, u32[]{:S(2)}) copy-start(bf16[8,256,256]{2,1,0:T(8,128)(2,1)} %taps_ref.5) | copy-start | bytes 3145732
  0.0 3.0 %collective-permute-start = (bf16[1,2,64,3840]{3,2,1,0:T(8,128)(2,1)}, bf16[1,2,64,3840]{3,2,1,0:T(8,128)(2,1)S(1)}, u32[]{:S(2)}, u32[]{:S(2)}) collective-permute-start(bf16[1,2,64,3840]{3,2,1,0:T(8,128)(2,1)} %volt_ref.1), channel_id=1, source_target_pairs={{0,1},{1,0},{2,3},{3,2},{4,5},{5,4},{6,7},{7,6},{8,9},{9,8},{10,11... | collective-permute-start | bytes 2949128 | tf_op jit(solution)/shard_map/ppermute | solution.py:195
  0.5 0.9 %copy-start.2 = (bf16[1,1,32,256]{3,2,1,0:T(8,128)(2,1)S(1)}, bf16[1,1,32,256]{3,2,1,0:T(8,128)(2,1)}, u32[]{:S(2)}) copy-start(bf16[1,1,32,256]{3,2,1,0:T(8,128)(2,1)} %rows_ref.1) | copy-start | bytes 49156
  0.5 0.9 %copy-start.3 = (bf16[1,1,32,256]{3,2,1,0:T(8,128)(2,1)S(1)}, bf16[1,1,32,256]{3,2,1,0:T(8,128)(2,1)}, u32[]{:S(2)}) copy-start(bf16[1,1,32,256]{3,2,1,0:T(8,128)(2,1)} %cols_ref.1) | copy-start | bytes 49156
  0.9 0.7 %copy-start.4 = (s32[2,32,1]{1,2,0:T(1,128)S(1)}, s32[2,32,1]{1,2,0:T(1,128)}, u32[]{:S(2)}) copy-start(s32[2,32,1]{1,2,0:T(1,128)} %param.11) | copy-start | bytes 772
  0.9 0.7 %copy-start.5 = (s32[64]{0:T(128)S(1)}, s32[64]{0:T(128)}, u32[]{:S(2)}) copy-start(s32[64]{0:T(128)} %param.7) | copy-start | bytes 772
  1.8 1.2 %collective-permute-start.1 = (f32[8,256]{1,0:T(8,128)S(1)}, f32[8,256]{1,0:T(8,128)S(1)}, u32[]{:S(2)}, u32[]{:S(2)}) collective-permute-start(f32[8,256]{1,0:T(8,128)S(1)} %get-tuple-element.12.packed_ref.own_ref), channel_id=1, source_target_pairs={{0,1},{1,0},{2,3},{3,2},{4,5},{5,4},{6,7},{7,6},{8,9},{9,8},{10,11... | collective-permute-start | bytes 24584 | tf_op jit(solution)/shard_map/ppermute | solution.py:211
  3.7 6.9 %collective-permute-start.2 = (bf16[272,256]{1,0:T(8,128)(2,1)S(1)}, bf16[272,256]{1,0:T(8,128)(2,1)S(1)}, u32[]{:S(2)}, u32[]{:S(2)}) collective-permute-start(bf16[272,256]{1,0:T(8,128)(2,1)S(1)} %shard_map.67.refs_0_), channel_id=1, source_target_pairs={{0,2},{2,0},{1,3},{3,1},{4,6},{6,4},{5,7},{7,5},{8,10},{10,8},{9,1... | collective-permute-start | bytes 417800 | tf_op jit(solution)/shard_map/ppermute | solution.py:231

commit v4 on v3

--- a/solution.py
+++ b/solution.py
@@ -56,8 +56,8 @@
         out_ref[...] = jnp.concatenate([high, low, high], axis=1)
 
 
-def pack_kernel(flags_ref, cells_ref, rows_ref, cols_ref, _, packed_ref, *weights_refs):
-    turn, turns = lax.axis_index(TURN), lax.axis_size(TURN)
+def pack_kernel(flags_ref, cells_ref, _rows_ref, _cols_ref, _table_ref, packed_ref):
+    turn = lax.axis_index(TURN)
     count, lanes = cells_ref.shape[1], packed_ref.shape[1]
     wide = jnp.concatenate([cells_ref[...]] * (lanes // count), axis=1)
     lane = lax.broadcasted_iota(jnp.int32, wide.shape, 1)
@@ -66,18 +66,14 @@
     packed_ref[0:2] = (wide // DIGIT).astype(jnp.float32)
     packed_ref[2:4] = (wide % DIGIT).astype(jnp.float32)
     packed_ref[4:5, : flags_ref.shape[1]] = flags_ref[...].astype(jnp.float32)
+
+
+def gridding_weights(rows_ref, cols_ref, packed_ref, turn, stations):
     both = jnp.concatenate([rows_ref[0, 0], cols_ref[0, 0]], axis=0).astype(jnp.float32)
-    for index, weights_ref in enumerate(weights_refs):
-        stations = weights_ref.shape[1]
-        weights = jnp.zeros(weights_ref.shape, jnp.float32)
-        for group in range(turns):
-            piece = both[:, group * stations : (group + 1) * stations]
-            weights = jnp.where(turn ^ index == group, piece, weights)
-        weights_ref[...] = weights
-
-
-def flagged(weights_ref, packed_ref):
-    return (weights_ref[...] * packed_ref[4:5, : weights_ref.shape[1]]).astype(jnp.bfloat16)
+    weights = jnp.zeros((both.shape[0], stations), jnp.float32)
+    for group in range(lax.axis_size(TURN)):
+        weights = jnp.where(turn == group, both[:, group * stations : (group + 1) * stations], weights)
+    return (weights * packed_ref[4:5, :stations]).astype(jnp.bfloat16)
 
 
 def gridded_frames(volt_ref, taps_ref, weights, firsts):
@@ -93,24 +89,26 @@
     )
     filt = taps_ref[...].reshape(taps * two_fine, two_fine)
     spectra = jnp.dot(lhs, filt, preferred_element_type=jnp.float32).astype(jnp.bfloat16)
-    return [
-        jnp.dot(weights, spectra[index * stations : (index + 1) * stations], preferred_element_type=jnp.float32)
-        for index in range(len(firsts))
-    ]
-
-
-def own_kernel(volt_ref, taps_ref, weights_ref, packed_ref, out_ref):
-    rows = weights_ref.shape[0]
-    firsts = range(out_ref.shape[0] // rows)
-    for frame, gridded in enumerate(gridded_frames(volt_ref, taps_ref, flagged(weights_ref, packed_ref), firsts)):
+    beside = jnp.concatenate(
+        [spectra[index * stations : (index + 1) * stations] for index in range(len(firsts))], axis=1
+    )
+    gridded = jnp.dot(weights, beside, preferred_element_type=jnp.float32)
+    return [gridded[:, index * two_fine : (index + 1) * two_fine] for index in range(len(firsts))]
+
+
+def own_kernel(volt_ref, taps_ref, rows_ref, cols_ref, packed_ref, out_ref):
+    weights = gridding_weights(rows_ref, cols_ref, packed_ref, lax.axis_index(TURN), volt_ref.shape[2])
+    rows = weights.shape[0]
+    for frame, gridded in enumerate(gridded_frames(volt_ref, taps_ref, weights, range(out_ref.shape[0] // rows))):
         out_ref[frame * rows : (frame + 1) * rows] = gridded
 
 
-def sum_kernel(step, each, volt_ref, taps_ref, weights_ref, own_ref, packed_ref, part_ref, *refs):
+def sum_kernel(step, each, volt_ref, taps_ref, rows_ref, cols_ref, own_ref, packed_ref, part_ref, *refs):
     out_ref = refs[-1]
-    rows = weights_ref.shape[0]
+    weights = gridding_weights(rows_ref, cols_ref, packed_ref, lax.axis_index(TURN) ^ 1, volt_ref.shape[2])
+    rows = weights.shape[0]
     firsts = [(lax.axis_index("chip") ^ step) * each + frame for frame in range(each)]
-    for index, gridded in enumerate(gridded_frames(volt_ref, taps_ref, flagged(weights_ref, packed_ref), firsts)):
+    for index, gridded in enumerate(gridded_frames(volt_ref, taps_ref, weights, firsts)):
         held = part_ref[pl.ds(pl.multiple_of(firsts[index] * rows, rows), rows)]
         out_ref[index * rows : (index + 1) * rows] = (held + gridded).astype(jnp.bfloat16)
     digits = own_ref[...] + packed_ref[...]
@@ -202,10 +200,9 @@
         (),
         flops=2 * voltages.size * two_fine * taps,
     )
-    weights = jax.ShapeDtypeStruct((sub_rows, station_rows), jnp.float32)
-    packed, own_weights, other_weights = call(
+    packed = call(
         pack_kernel,
-        (jax.ShapeDtypeStruct((8, two_fine), jnp.float32), weights, weights),
+        jax.ShapeDtypeStruct((8, two_fine), jnp.float32),
         (station_flags.reshape(1, -1), cell_index.reshape(2, -1), kernel_rows, kernel_cols, tables[0]),
     )
     other_packed = lax.ppermute(packed, "core", swap)
@@ -213,7 +210,7 @@
     part = call(
         own_kernel,
         jax.ShapeDtypeStruct((frames * sub_rows, two_fine), jnp.float32),
-        (voltages, filter_taps, own_weights, packed),
+        (voltages, filter_taps, kernel_rows, kernel_cols, packed),
         flops=frames * flops,
     )
 
@@ -223,7 +220,7 @@
         made = call(
             functools.partial(sum_kernel, step, each),
             jax.ShapeDtypeStruct((each * sub_rows + PAD_ROWS, two_fine), jnp.bfloat16),
-            (other, filter_taps, other_weights, packed, other_packed, part, *after),
+            (other, filter_taps, kernel_rows, kernel_cols, packed, other_packed, part, *after),
             flops=each * flops,
         )
         after = (made,)

time: 24.8 us -> 24.7 us (level)
  transfers between devices with their start and end apart: 3 -> 3, of which waited for: 1 -> 1; matrix products, arithmetic and copies ran while one was open for 0% -> 0% of each run, Pallas kernels for 9% -> 8%
where the time goes in v4:
time: 24.7 us; the launch traced here: 24.5 us
  blocking collectives  13.1 us (53%)
  starting transfers between devices  3.67 us (15%)
  Pallas kernels  3.64 us (15%)
  waiting for transfers between devices  3.38 us (14%)
  local copies, waits for them, and re-layouts  0.69 us (3%)
    all_to_all x1, blocking collectives, local(): lax.all_to_all(image, EVERYONE, split_axis=0, concat_axis=0, tiled=True)  13.1 us
    pallas_call x7, Pallas kernels, call(): pl.pallas_call(kernel, out_shape=shape, in_specs=[pl.BlockSpec(memory_spa...  3.64 us
    ppermute x1, waiting for transfers between devices, local(): lax.ppermute(made, 'chip', [(source, source ^ step) for source in range(c...  3.36 us
    ppermute x1, starting transfers between devices, local(): lax.ppermute(made, 'chip', [(source, source ^ step) for source in range(c...  2.91 us
    unnamed x12, local copies, waits for them, and re-layouts  0.69 us
  transfers between devices with their start and end apart: 3, of which 1 were waited for; matrix products, arithmetic and copies ran while one was open for 0% of the time, Pallas kernels for 8%

profile of v4, /device:TPU:0, one launch (start us, length us, event | category | flops | bytes accessed | tf_op | source)
XLA Modules:
  0.0 24.5 jit_solution(8256208756653412830)
XLA Ops:
  0.0 0.0 copy-start.1
  0.0 0.0 copy-start
  0.0 0.5 %collective-permute-start = (bf16[1,2,64,3840]{3,2,1,0:T(8,128)(2,1)}, bf16[1,2,64,3840]{3,2,1,0:T(8,128)(2,1)S(1)}, u32[]{:S(2)}, u32[]{:S(2)}) collective-permute-start(bf16[1,2,64,3840]{3,2,1,0:T(8,128)(2,1)} %volt_ref.1), channel_id=1, source_target_pairs={{0,1},{1,0},{2,3},{3,2},{4,5},{5,4},{6,7},{7,6},{8,9},{9,8},{10,11... | collective-permute-start | bytes 2949128 | tf_op jit(solution)/shard_map/ppermute | solution.py:193
  0.5 0.0 copy-start.2
  0.5 0.0 copy-start.3
  0.5 0.4 %shard_map.64 = (bf16[64,192]{1,0:T(8,128)(2,1)S(1)}, bf16[256,192]{1,0:T(8,128)(2,1)S(1)}) custom-call(), custom_call_target="tpu_custom_call" | custom-call | flops 2013265920 | bytes 122880 | tf_op jit(solution)/shard_map/pallas_call | solution.py:170
  0.9 0.0 copy-start.4
  0.9 0.0 copy-start.5
  0.9 0.5 %copy-done.2 = bf16[1,1,32,256]{3,2,1,0:T(8,128)(2,1)S(1)} copy-done((bf16[1,1,32,256]{3,2,1,0:T(8,128)(2,1)S(1)}, bf16[1,1,32,256]{3,2,1,0:T(8,128)(2,1)}, u32[]{:S(2)}) %copy-start.2) | copy-done | bytes 16408
  1.3 0.0 copy-done.3
  1.3 0.2 copy-done.4
  1.5 0.0 copy-done.5
  1.5 0.1 shard_map.65.packed_ref.own_ref
  1.6 0.3 %collective-permute-start.1 = (f32[8,256]{1,0:T(8,128)S(1)}, f32[8,256]{1,0:T(8,128)S(1)}, u32[]{:S(2)}, u32[]{:S(2)}) collective-permute-start(f32[8,256]{1,0:T(8,128)S(1)} %shard_map.65.packed_ref.own_ref), channel_id=1, source_target_pairs={{0,1},{1,0},{2,3},{3,2},{4,5},{5,4},{6,7},{7,6},{8,9},{9,8},{10,11... | collective-permute-start | bytes 24584 | tf_op jit(solution)/shard_map/ppermute | solution.py:208
  1.9 0.0 copy-done.1
  1.9 0.0 copy-done
  1.9 0.9 %shard_map.66.part_ref = f32[512,256]{1,0:T(8,128)S(1)} custom-call(bf16[1,2,64,3840]{3,2,1,0:T(8,128)(2,1)S(1)} %copy-done.1, bf16[8,256,256]{2,1,0:T(8,128)(2,1)S(1)} %copy-done, bf16[1,1,32,256]{3,2,1,0:T(8,128)(2,1)S(1)} %copy-done.2, bf16[1,1,32,256]{3,2,1,0:T(8,128)(2,1)S(1)} %copy-done.3, f32[8,256]{1,0:T(8,128)S(1)} %shard_map.65.packed_ref.own_ref), custom_call_target="tpu_custom_call" | custom-call | flops 536870912 | bytes 2596864 | tf_op jit(solution)/shard_map/pallas_call | solution.py:170
  2.8 0.0 collective-permute-done.1.packed_ref
  2.9 0.0 collective-permute-done.volt_ref
  2.9 0.6 %shard_map.67.refs_0_ = bf16[272,256]{1,0:T(8,128)(2,1)S(1)} custom-call(bf16[1,2,64,3840]{3,2,1,0:T(8,128)(2,1)S(1)} %collective-permute-done.volt_ref, bf16[8,256,256]{2,1,0:T(8,128)(2,1)S(1)} %copy-done, bf16[1,1,32,256]{3,2,1,0:T(8,128)(2,1)S(1)} %copy-done.2, bf16[1,1,32,256]{3,2,1,0:T(8,128)(2,1)S(1)} %copy-done.3, ...), custom_call_target="tpu_custom_call" | custom-call | flops 268435456 | bytes 2744320 | tf_op jit(solution)/shard_map/pallas_call | solution.py:170
  3.5 2.9 %collective-permute-start.2 = (bf16[272,256]{1,0:T(8,128)(2,1)S(1)}, bf16[272,256]{1,0:T(8,128)(2,1)S(1)}, u32[]{:S(2)}, u32[]{:S(2)}) collective-permute-start(bf16[272,256]{1,0:T(8,128)(2,1)S(1)} %shard_map.67.refs_0_), channel_id=1, source_target_pairs={{0,2},{2,0},{1,3},{3,1},{4,6},{6,4},{5,7},{7,5},{8,10},{10,8},{9,1... | collective-permute-start | bytes 417800 | tf_op jit(solution)/shard_map/ppermute | solution.py:228
  6.4 0.6 %shard_map.68.refs_1_ = bf16[272,256]{1,0:T(8,128)(2,1)S(1)} custom-call(bf16[1,2,64,3840]{3,2,1,0:T(8,128)(2,1)S(1)} %collective-permute-done.volt_ref, bf16[8,256,256]{2,1,0:T(8,128)(2,1)S(1)} %copy-done, bf16[1,1,32,256]{3,2,1,0:T(8,128)(2,1)S(1)} %copy-done.2, bf16[1,1,32,256]{3,2,1,0:T(8,128)(2,1)S(1)} %copy-done.3, ...), custom_call_target="tpu_custom_call" | custom-call | flops 268435456 | bytes 2883584 | tf_op jit(solution)/shard_map/pallas_call | solution.py:170
  7.0 3.4 %collective-permute-done.2.refs_0_ = bf16[272,256]{1,0:T(8,128)(2,1)S(1)} collective-permute-done((bf16[272,256]{1,0:T(8,128)(2,1)S(1)}, bf16[272,256]{1,0:T(8,128)(2,1)S(1)}, u32[]{:S(2)}, u32[]{:S(2)}) %collective-permute-start.2) | collective-permute-done | bytes 139296 | tf_op jit(solution)/shard_map/ppermute | solution.py:228
  10.4 0.5 %shard_map.69 = f32[32,128]{1,0:T(8,128)S(1)} custom-call(bf16[272,256]{1,0:T(8,128)(2,1)S(1)} %collective-permute-done.2.refs_0_, bf16[272,256]{1,0:T(8,128)(2,1)S(1)} %shard_map.68.refs_1_, bf16[64,192]{1,0:T(8,128)(2,1)S(1)} %get-tuple-element.7._table_ref.refs_2_, bf16[256,192]{1,0:T(8,128)(2,1)S(1)} %get-tuple-element.8.refs_3_), custom_call_target="tpu_custom_call" | custom-call | bytes 417792 | tf_op jit(solution)/shard_map/pallas_call | solution.py:170
  10.9 13.1 %all_to_all.9.in_ref = f32[32,1,128]{2,1,0:T(1,128)S(1)} all-to-all(f32[32,1,128]{2,1,0:T(1,128)S(1)} %bitcast.3), channel_id=1, replica_groups=mesh['role'=2,'band'=4,'chip'=2,'core'=2] {'role','band','chip','core'}, dimensions={0} | all-to-all | bytes 32768 | tf_op jit(solution)/shard_map/all_to_all | solution.py:235
  24.0 0.5 %shard_map.70 = f32[1,128]{1,0:T(1,128)} custom-call(f32[32,1,128]{2,1,0:T(1,128)S(1)} %all_to_all.9.in_ref), custom_call_target="tpu_custom_call" | custom-call | bytes 16896 | tf_op jit(solution)/shard_map/pallas_call | solution.py:170
Async XLA Ops:
  0.0 1.9 %copy-start.1 = (bf16[1,2,64,3840]{3,2,1,0:T(8,128)(2,1)S(1)}, bf16[1,2,64,3840]{3,2,1,0:T(8,128)(2,1)}, u32[]{:S(2)}) copy-start(bf16[1,2,64,3840]{3,2,1,0:T(8,128)(2,1)} %volt_ref.1) | copy-start | bytes 2949124
  0.0 1.9 %copy-start = (bf16[8,256,256]{2,1,0:T(8,128)(2,1)S(1)}, bf16[8,256,256]{2,1,0:T(8,128)(2,1)}, u32[]{:S(2)}) copy-start(bf16[8,256,256]{2,1,0:T(8,128)(2,1)} %taps_ref.5) | copy-start | bytes 3145732
  0.0 2.9 %collective-permute-start = (bf16[1,2,64,3840]{3,2,1,0:T(8,128)(2,1)}, bf16[1,2,64,3840]{3,2,1,0:T(8,128)(2,1)S(1)}, u32[]{:S(2)}, u32[]{:S(2)}) collective-permute-start(bf16[1,2,64,3840]{3,2,1,0:T(8,128)(2,1)} %volt_ref.1), channel_id=1, source_target_pairs={{0,1},{1,0},{2,3},{3,2},{4,5},{5,4},{6,7},{7,6},{8,9},{9,8},{10,11... | collective-permute-start | bytes 2949128 | tf_op jit(solution)/shard_map/ppermute | solution.py:193
  0.5 0.9 %copy-start.2 = (bf16[1,1,32,256]{3,2,1,0:T(8,128)(2,1)S(1)}, bf16[1,1,32,256]{3,2,1,0:T(8,128)(2,1)}, u32[]{:S(2)}) copy-start(bf16[1,1,32,256]{3,2,1,0:T(8,128)(2,1)} %rows_ref.5) | copy-start | bytes 49156
  0.5 0.9 %copy-start.3 = (bf16[1,1,32,256]{3,2,1,0:T(8,128)(2,1)S(1)}, bf16[1,1,32,256]{3,2,1,0:T(8,128)(2,1)}, u32[]{:S(2)}) copy-start(bf16[1,1,32,256]{3,2,1,0:T(8,128)(2,1)} %cols_ref.5) | copy-start | bytes 49156
  0.9 0.7 %copy-start.4 = (s32[2,32,1]{1,2,0:T(1,128)S(1)}, s32[2,32,1]{1,2,0:T(1,128)}, u32[]{:S(2)}) copy-start(s32[2,32,1]{1,2,0:T(1,128)} %param.11) | copy-start | bytes 772
  0.9 0.7 %copy-start.5 = (s32[64]{0:T(128)S(1)}, s32[64]{0:T(128)}, u32[]{:S(2)}) copy-start(s32[64]{0:T(128)} %param.7) | copy-start | bytes 772
  1.6 1.2 %collective-permute-start.1 = (f32[8,256]{1,0:T(8,128)S(1)}, f32[8,256]{1,0:T(8,128)S(1)}, u32[]{:S(2)}, u32[]{:S(2)}) collective-permute-start(f32[8,256]{1,0:T(8,128)S(1)} %shard_map.65.packed_ref.own_ref), channel_id=1, source_target_pairs={{0,1},{1,0},{2,3},{3,2},{4,5},{5,4},{6,7},{7,6},{8,9},{9,8},{10,11... | collective-permute-start | bytes 24584 | tf_op jit(solution)/shard_map/ppermute | solution.py:208
  3.5 6.9 %collective-permute-start.2 = (bf16[272,256]{1,0:T(8,128)(2,1)S(1)}, bf16[272,256]{1,0:T(8,128)(2,1)S(1)}, u32[]{:S(2)}, u32[]{:S(2)}) collective-permute-start(bf16[272,256]{1,0:T(8,128)(2,1)S(1)} %shard_map.67.refs_0_), channel_id=1, source_target_pairs={{0,2},{2,0},{1,3},{3,1},{4,6},{6,4},{5,7},{7,5},{8,10},{10,8},{9,1... | collective-permute-start | bytes 417800 | tf_op jit(solution)/shard_map/ppermute | solution.py:228

commit v5 on v4

--- a/solution.py
+++ b/solution.py
@@ -80,15 +80,17 @@
     taps, two_fine, _ = taps_ref.shape
     stations = volt_ref.shape[2]
     core = lax.axis_index("core")
-    lhs = jnp.concatenate(
-        [
-            volt_ref[0, core, :, pl.ds(pl.multiple_of(first * two_fine, two_fine), taps * two_fine)]
-            for first in firsts
-        ],
-        axis=0,
-    )
-    filt = taps_ref[...].reshape(taps * two_fine, two_fine)
-    spectra = jnp.dot(lhs, filt, preferred_element_type=jnp.float32).astype(jnp.bfloat16)
+    spectra = jnp.zeros((len(firsts) * stations, two_fine), jnp.float32)
+    for tap in range(taps):
+        block = jnp.concatenate(
+            [
+                volt_ref[0, core, :, pl.ds(pl.multiple_of((first + tap) * two_fine, two_fine), two_fine)]
+                for first in firsts
+            ],
+            axis=0,
+        )
+        spectra = spectra + jnp.dot(block, taps_ref[tap], preferred_element_type=jnp.float32)
+    spectra = spectra.astype(jnp.bfloat16)
     beside = jnp.concatenate(
         [spectra[index * stations : (index + 1) * stations] for index in range(len(firsts))], axis=1
     )
@@ -158,7 +160,7 @@
     col_real, col_imag = transform(col_dft_ref, sub, *phase(cell_v, col - MW // 2))
     left = jnp.concatenate([row_real, -row_imag], axis=1).astype(jnp.bfloat16)
     right = jnp.concatenate([col_real, col_imag], axis=1).astype(jnp.bfloat16)
-    out_ref[...] = lax.dot_general(left, right, (((1,), (1,)), ((), ())), preferred_element_type=jnp.float32)
+    out_ref[...] = lax.dot_general(right, left, (((1,), (1,)), ((), ())), preferred_element_type=jnp.float32).T
 
 
 def final_kernel(scale_factor, in_ref, out_ref):

time: 24.7 us -> 24.7 us (level)
  no operation moved by 1% of the time
where the time goes in v5:
time: 24.7 us; the launch traced here: 24.5 us
  blocking collectives  13.1 us (53%)
  Pallas kernels  3.71 us (15%)
  starting transfers between devices  3.67 us (15%)
  waiting for transfers between devices  3.38 us (14%)
  local copies, waits for them, and re-layouts  0.69 us (3%)
    all_to_all x1, blocking collectives, local(): lax.all_to_all(image, EVERYONE, split_axis=0, concat_axis=0, tiled=True)  13.1 us
    pallas_call x7, Pallas kernels, call(): pl.pallas_call(kernel, out_shape=shape, in_specs=[pl.BlockSpec(memory_spa...  3.71 us
    ppermute x1, waiting for transfers between devices, local(): lax.ppermute(made, 'chip', [(source, source ^ step) for source in range(c...  3.36 us
    ppermute x1, starting transfers between devices, local(): lax.ppermute(made, 'chip', [(source, source ^ step) for source in range(c...  2.91 us
    unnamed x12, local copies, waits for them, and re-layouts  0.69 us
  transfers between devices with their start and end apart: 3, of which 1 were waited for; matrix products, arithmetic and copies ran while one was open for 0% of the time, Pallas kernels for 8%

profile of v5, /device:TPU:0, one launch (start us, length us, event | category | flops | bytes accessed | tf_op | source)
XLA Modules:
  0.0 24.5 jit_solution(17206953890080054161)
XLA Ops:
  0.0 0.0 copy-start.1
  0.0 0.0 copy-start
  0.0 0.5 %collective-permute-start = (bf16[1,2,64,3840]{3,2,1,0:T(8,128)(2,1)}, bf16[1,2,64,3840]{3,2,1,0:T(8,128)(2,1)S(1)}, u32[]{:S(2)}, u32[]{:S(2)}) collective-permute-start(bf16[1,2,64,3840]{3,2,1,0:T(8,128)(2,1)} %volt_ref.1), channel_id=1, source_target_pairs={{0,1},{1,0},{2,3},{3,2},{4,5},{5,4},{6,7},{7,6},{8,9},{9,8},{10,11... | collective-permute-start | bytes 2949128 | tf_op jit(solution)/shard_map/ppermute | solution.py:195
  0.5 0.0 copy-start.2
  0.5 0.0 copy-start.3
  0.5 0.4 %shard_map.64 = (bf16[64,192]{1,0:T(8,128)(2,1)S(1)}, bf16[256,192]{1,0:T(8,128)(2,1)S(1)}) custom-call(), custom_call_target="tpu_custom_call" | custom-call | flops 2013265920 | bytes 122880 | tf_op jit(solution)/shard_map/pallas_call | solution.py:172
  0.9 0.0 copy-start.4
  0.9 0.0 copy-start.5
  0.9 0.5 %copy-done.2 = bf16[1,1,32,256]{3,2,1,0:T(8,128)(2,1)S(1)} copy-done((bf16[1,1,32,256]{3,2,1,0:T(8,128)(2,1)S(1)}, bf16[1,1,32,256]{3,2,1,0:T(8,128)(2,1)}, u32[]{:S(2)}) %copy-start.2) | copy-done | bytes 16408
  1.3 0.0 copy-done.3
  1.3 0.2 copy-done.4
  1.5 0.0 copy-done.5
  1.5 0.1 shard_map.65.packed_ref.own_ref
  1.6 0.3 %collective-permute-start.1 = (f32[8,256]{1,0:T(8,128)S(1)}, f32[8,256]{1,0:T(8,128)S(1)}, u32[]{:S(2)}, u32[]{:S(2)}) collective-permute-start(f32[8,256]{1,0:T(8,128)S(1)} %shard_map.65.packed_ref.own_ref), channel_id=1, source_target_pairs={{0,1},{1,0},{2,3},{3,2},{4,5},{5,4},{6,7},{7,6},{8,9},{9,8},{10,11... | collective-permute-start | bytes 24584 | tf_op jit(solution)/shard_map/ppermute | solution.py:210
  1.9 0.0 copy-done.1
  1.9 0.0 copy-done
  1.9 0.9 %shard_map.66.part_ref = f32[512,256]{1,0:T(8,128)S(1)} custom-call(bf16[1,2,64,3840]{3,2,1,0:T(8,128)(2,1)S(1)} %copy-done.1, bf16[8,256,256]{2,1,0:T(8,128)(2,1)S(1)} %copy-done, bf16[1,1,32,256]{3,2,1,0:T(8,128)(2,1)S(1)} %copy-done.2, bf16[1,1,32,256]{3,2,1,0:T(8,128)(2,1)S(1)} %copy-done.3, f32[8,256]{1,0:T(8,128)S(1)} %shard_map.65.packed_ref.own_ref), custom_call_target="tpu_custom_call" | custom-call | flops 536870912 | bytes 2596864 | tf_op jit(solution)/shard_map/pallas_call | solution.py:172
  2.9 0.0 collective-permute-done.1.packed_ref
  2.9 0.0 collective-permute-done.volt_ref
  2.9 0.6 %shard_map.67.refs_0_ = bf16[272,256]{1,0:T(8,128)(2,1)S(1)} custom-call(bf16[1,2,64,3840]{3,2,1,0:T(8,128)(2,1)S(1)} %collective-permute-done.volt_ref, bf16[8,256,256]{2,1,0:T(8,128)(2,1)S(1)} %copy-done, bf16[1,1,32,256]{3,2,1,0:T(8,128)(2,1)S(1)} %copy-done.2, bf16[1,1,32,256]{3,2,1,0:T(8,128)(2,1)S(1)} %copy-done.3, ...), custom_call_target="tpu_custom_call" | custom-call | flops 268435456 | bytes 2744320 | tf_op jit(solution)/shard_map/pallas_call | solution.py:172
  3.5 2.9 %collective-permute-start.2 = (bf16[272,256]{1,0:T(8,128)(2,1)S(1)}, bf16[272,256]{1,0:T(8,128)(2,1)S(1)}, u32[]{:S(2)}, u32[]{:S(2)}) collective-permute-start(bf16[272,256]{1,0:T(8,128)(2,1)S(1)} %shard_map.67.refs_0_), channel_id=1, source_target_pairs={{0,2},{2,0},{1,3},{3,1},{4,6},{6,4},{5,7},{7,5},{8,10},{10,8},{9,1... | collective-permute-start | bytes 417800 | tf_op jit(solution)/shard_map/ppermute | solution.py:230
  6.4 0.6 %shard_map.68.refs_1_ = bf16[272,256]{1,0:T(8,128)(2,1)S(1)} custom-call(bf16[1,2,64,3840]{3,2,1,0:T(8,128)(2,1)S(1)} %collective-permute-done.volt_ref, bf16[8,256,256]{2,1,0:T(8,128)(2,1)S(1)} %copy-done, bf16[1,1,32,256]{3,2,1,0:T(8,128)(2,1)S(1)} %copy-done.2, bf16[1,1,32,256]{3,2,1,0:T(8,128)(2,1)S(1)} %copy-done.3, ...), custom_call_target="tpu_custom_call" | custom-call | flops 268435456 | bytes 2883584 | tf_op jit(solution)/shard_map/pallas_call | solution.py:172
  7.0 3.4 %collective-permute-done.2.refs_0_ = bf16[272,256]{1,0:T(8,128)(2,1)S(1)} collective-permute-done((bf16[272,256]{1,0:T(8,128)(2,1)S(1)}, bf16[272,256]{1,0:T(8,128)(2,1)S(1)}, u32[]{:S(2)}, u32[]{:S(2)}) %collective-permute-start.2) | collective-permute-done | bytes 139296 | tf_op jit(solution)/shard_map/ppermute | solution.py:230
  10.4 0.5 %shard_map.69 = f32[32,128]{1,0:T(8,128)S(1)} custom-call(bf16[272,256]{1,0:T(8,128)(2,1)S(1)} %collective-permute-done.2.refs_0_, bf16[272,256]{1,0:T(8,128)(2,1)S(1)} %shard_map.68.refs_1_, bf16[64,192]{1,0:T(8,128)(2,1)S(1)} %get-tuple-element.7._table_ref.refs_2_, bf16[256,192]{1,0:T(8,128)(2,1)S(1)} %get-tuple-element.8.refs_3_), custom_call_target="tpu_custom_call" | custom-call | bytes 417792 | tf_op jit(solution)/shard_map/pallas_call | solution.py:172
  10.9 13.1 %all_to_all.9.in_ref = f32[32,1,128]{2,1,0:T(1,128)S(1)} all-to-all(f32[32,1,128]{2,1,0:T(1,128)S(1)} %bitcast.3), channel_id=1, replica_groups=mesh['role'=2,'band'=4,'chip'=2,'core'=2] {'role','band','chip','core'}, dimensions={0} | all-to-all | bytes 32768 | tf_op jit(solution)/shard_map/all_to_all | solution.py:237
  24.0 0.5 %shard_map.70 = f32[1,128]{1,0:T(1,128)} custom-call(f32[32,1,128]{2,1,0:T(1,128)S(1)} %all_to_all.9.in_ref), custom_call_target="tpu_custom_call" | custom-call | bytes 16896 | tf_op jit(solution)/shard_map/pallas_call | solution.py:172
Async XLA Ops:
  0.0 1.9 %copy-start.1 = (bf16[1,2,64,3840]{3,2,1,0:T(8,128)(2,1)S(1)}, bf16[1,2,64,3840]{3,2,1,0:T(8,128)(2,1)}, u32[]{:S(2)}) copy-start(bf16[1,2,64,3840]{3,2,1,0:T(8,128)(2,1)} %volt_ref.1) | copy-start | bytes 2949124
  0.0 1.9 %copy-start = (bf16[8,256,256]{2,1,0:T(8,128)(2,1)S(1)}, bf16[8,256,256]{2,1,0:T(8,128)(2,1)}, u32[]{:S(2)}) copy-start(bf16[8,256,256]{2,1,0:T(8,128)(2,1)} %taps_ref.5) | copy-start | bytes 3145732
  0.0 2.9 %collective-permute-start = (bf16[1,2,64,3840]{3,2,1,0:T(8,128)(2,1)}, bf16[1,2,64,3840]{3,2,1,0:T(8,128)(2,1)S(1)}, u32[]{:S(2)}, u32[]{:S(2)}) collective-permute-start(bf16[1,2,64,3840]{3,2,1,0:T(8,128)(2,1)} %volt_ref.1), channel_id=1, source_target_pairs={{0,1},{1,0},{2,3},{3,2},{4,5},{5,4},{6,7},{7,6},{8,9},{9,8},{10,11... | collective-permute-start | bytes 2949128 | tf_op jit(solution)/shard_map/ppermute | solution.py:195
  0.5 0.9 %copy-start.2 = (bf16[1,1,32,256]{3,2,1,0:T(8,128)(2,1)S(1)}, bf16[1,1,32,256]{3,2,1,0:T(8,128)(2,1)}, u32[]{:S(2)}) copy-start(bf16[1,1,32,256]{3,2,1,0:T(8,128)(2,1)} %rows_ref.5) | copy-start | bytes 49156
  0.5 0.9 %copy-start.3 = (bf16[1,1,32,256]{3,2,1,0:T(8,128)(2,1)S(1)}, bf16[1,1,32,256]{3,2,1,0:T(8,128)(2,1)}, u32[]{:S(2)}) copy-start(bf16[1,1,32,256]{3,2,1,0:T(8,128)(2,1)} %cols_ref.5) | copy-start | bytes 49156
  0.9 0.7 %copy-start.4 = (s32[2,32,1]{1,2,0:T(1,128)S(1)}, s32[2,32,1]{1,2,0:T(1,128)}, u32[]{:S(2)}) copy-start(s32[2,32,1]{1,2,0:T(1,128)} %param.11) | copy-start | bytes 772
  0.9 0.7 %copy-start.5 = (s32[64]{0:T(128)S(1)}, s32[64]{0:T(128)}, u32[]{:S(2)}) copy-start(s32[64]{0:T(128)} %param.7) | copy-start | bytes 772
  1.6 1.2 %collective-permute-start.1 = (f32[8,256]{1,0:T(8,128)S(1)}, f32[8,256]{1,0:T(8,128)S(1)}, u32[]{:S(2)}, u32[]{:S(2)}) collective-permute-start(f32[8,256]{1,0:T(8,128)S(1)} %shard_map.65.packed_ref.own_ref), channel_id=1, source_target_pairs={{0,1},{1,0},{2,3},{3,2},{4,5},{5,4},{6,7},{7,6},{8,9},{9,8},{10,11... | collective-permute-start | bytes 24584 | tf_op jit(solution)/shard_map/ppermute | solution.py:210
  3.5 6.9 %collective-permute-start.2 = (bf16[272,256]{1,0:T(8,128)(2,1)S(1)}, bf16[272,256]{1,0:T(8,128)(2,1)S(1)}, u32[]{:S(2)}, u32[]{:S(2)}) collective-permute-start(bf16[272,256]{1,0:T(8,128)(2,1)S(1)} %shard_map.67.refs_0_), channel_id=1, source_target_pairs={{0,2},{2,0},{1,3},{3,1},{4,6},{6,4},{5,7},{7,5},{8,10},{10,8},{9,1... | collective-permute-start | bytes 417800 | tf_op jit(solution)/shard_map/ppermute | solution.py:230

commit v6 on v4

--- a/solution.py
+++ b/solution.py
@@ -13,7 +13,6 @@
 MW = 128
 ROWS_DEV = 1
 DIGIT = 64
-PAD_ROWS = 16
 CORES = 2
 TURN = ("chip", "core")
 EVERYONE = ("role", "band", *TURN)
@@ -103,7 +102,7 @@
         out_ref[frame * rows : (frame + 1) * rows] = gridded
 
 
-def sum_kernel(step, each, volt_ref, taps_ref, rows_ref, cols_ref, own_ref, packed_ref, part_ref, *refs):
+def sum_kernel(step, each, volt_ref, taps_ref, rows_ref, cols_ref, packed_ref, part_ref, *refs):
     out_ref = refs[-1]
     weights = gridding_weights(rows_ref, cols_ref, packed_ref, lax.axis_index(TURN) ^ 1, volt_ref.shape[2])
     rows = weights.shape[0]
@@ -111,23 +110,30 @@
     for index, gridded in enumerate(gridded_frames(volt_ref, taps_ref, weights, firsts)):
         held = part_ref[pl.ds(pl.multiple_of(firsts[index] * rows, rows), rows)]
         out_ref[index * rows : (index + 1) * rows] = (held + gridded).astype(jnp.bfloat16)
-    digits = own_ref[...] + packed_ref[...]
-    digits = jnp.concatenate([digits, jnp.zeros((PAD_ROWS - digits.shape[0], digits.shape[1]), jnp.float32)], axis=0)
-    out_ref[each * rows :] = digits.astype(jnp.bfloat16)
+
+
+def add_kernel(left_ref, right_ref, _, out_ref):
+    out_ref[...] = left_ref[...] + right_ref[...]
+
+
+def phases_kernel(*refs):
+    *tiles, _, row_cos, row_sin, col_cos, col_sin = refs
+    digits = tiles[0][...]
+    for tile in tiles[1:]:
+        digits = digits + tile[...]
+    for index, (cos_ref, sin_ref) in enumerate(((row_cos, row_sin), (col_cos, col_sin))):
+        cell = (digits[index : index + 1] * DIGIT + digits[index + 2 : index + 3]).astype(jnp.int32)
+        pixel = lax.broadcasted_iota(jnp.int32, cos_ref.shape, 0) - cos_ref.shape[0] // 2
+        cos_ref[...], sin_ref[...] = phase(cell, pixel)
 
 
 def image_kernel(pairs_each, *refs):
-    *got, row_dft_ref, col_dft_ref, out_ref = refs
+    *got, row_dft_ref, col_dft_ref, row_cos, row_sin, col_cos, col_sin, out_ref = refs
     fine = got[0].shape[1] // 2
     sub = row_dft_ref.shape[1] // 6
-    row_total = out_ref.shape[0]
     total = got[0][...].astype(jnp.float32)
     for source in got[1:]:
         total = total + source[...].astype(jnp.float32)
-    digits = total[pairs_each * 2 * sub :]
-    cell_u = (digits[0:1, :fine] * DIGIT + digits[2:3, :fine]).astype(jnp.int32)
-    cell_v = (digits[1:2, :fine] * DIGIT + digits[3:4, :fine]).astype(jnp.int32)
-
     def transform(dft_ref, first, cos, sin):
         held = jnp.concatenate(
             [
@@ -152,10 +158,8 @@
         sin = jnp.concatenate([sin] * pairs_each, axis=1)
         return real * cos - imag * sin, real * sin + imag * cos
 
-    row = lax.broadcasted_iota(jnp.int32, (row_total, fine), 0)
-    row_real, row_imag = transform(row_dft_ref, 0, *phase(cell_u, row - row_total // 2))
-    col = lax.broadcasted_iota(jnp.int32, (MW, fine), 0)
-    col_real, col_imag = transform(col_dft_ref, sub, *phase(cell_v, col - MW // 2))
+    row_real, row_imag = transform(row_dft_ref, 0, row_cos[...], row_sin[...])
+    col_real, col_imag = transform(col_dft_ref, sub, col_cos[...], col_sin[...])
     left = jnp.concatenate([row_real, -row_imag], axis=1).astype(jnp.bfloat16)
     right = jnp.concatenate([col_real, col_imag], axis=1).astype(jnp.bfloat16)
     out_ref[...] = lax.dot_general(left, right, (((1,), (1,)), ((), ())), preferred_element_type=jnp.float32)
@@ -202,7 +206,7 @@
     )
     packed = call(
         pack_kernel,
-        jax.ShapeDtypeStruct((8, two_fine), jnp.float32),
+        jax.ShapeDtypeStruct((8, two_fine // 2), jnp.float32),
         (station_flags.reshape(1, -1), cell_index.reshape(2, -1), kernel_rows, kernel_cols, tables[0]),
     )
     other_packed = lax.ppermute(packed, "core", swap)
@@ -214,23 +218,34 @@
         flops=frames * flops,
     )
 
+    def beside(value, step):
+        return lax.ppermute(value, "chip", [(source, source ^ step) for source in range(chips)])
+
+    def summed(step, after):
+        return call(
+            functools.partial(sum_kernel, step, each),
+            jax.ShapeDtypeStruct((each * sub_rows, two_fine), jnp.bfloat16),
+            (other, filter_taps, kernel_rows, kernel_cols, other_packed, part, *after),
+            flops=each * flops,
+        )
+
     after = ()
     got = []
-    for step in [*range(1, chips), 0]:
-        made = call(
-            functools.partial(sum_kernel, step, each),
-            jax.ShapeDtypeStruct((each * sub_rows + PAD_ROWS, two_fine), jnp.bfloat16),
-            (other, filter_taps, kernel_rows, kernel_cols, packed, other_packed, part, *after),
-            flops=each * flops,
-        )
+    for step in range(1, chips):
+        made = summed(step, after)
         after = (made,)
-        if step:
-            made = lax.ppermute(made, "chip", [(source, source ^ step) for source in range(chips)])
-        got.append(made)
+        got.append(beside(made, step))
+    tile = call(add_kernel, packed, (packed, other_packed, *after))
+    tiles = [tile] + [beside(tile, step) for step in range(1, chips)]
+    made = summed(0, (tile,))
+    got.append(made)
+    by_row = jax.ShapeDtypeStruct((row_total, two_fine // 2), jnp.float32)
+    by_col = jax.ShapeDtypeStruct((MW, two_fine // 2), jnp.float32)
+    phases = call(phases_kernel, (by_row, by_row, by_col, by_col), (*tiles, made))
     image = call(
         functools.partial(image_kernel, each),
         jax.ShapeDtypeStruct((row_total, MW), jnp.float32),
-        (*got, *tables),
+        (*got, *tables, *phases),
     )
     rows = lax.all_to_all(image, EVERYONE, split_axis=0, concat_axis=0, tiled=True)
     return call(

time: 24.7 us -> 24.8 us (level)
    ppermute x1 -> x2, waiting for transfers between devices: 3.36 us -> 3.18 us  [beside(): lax.ppermute(value, 'chip', [(source, source ^ step) for source in range(...]
    pallas_call x7 -> x9, Pallas kernels: 3.64 us -> 3.81 us  [call(): pl.pallas_call(kernel, out_shape=shape, in_specs=[pl.BlockSpec(memory_spa...]
    ppermute x1 -> x2, starting transfers between devices: 2.91 us -> 3.01 us  [beside(): lax.ppermute(value, 'chip', [(source, source ^ step) for source in range(...]
  transfers between devices with their start and end apart: 3 -> 4, of which waited for: 1 -> 1; matrix products, arithmetic and copies ran while one was open for 0% -> 0% of each run, Pallas kernels for 8% -> 9%
where the time goes in v6:
time: 24.8 us; the launch traced here: 24.6 us
  blocking collectives  13.1 us (53%)
  Pallas kernels  3.81 us (15%)
  starting transfers between devices  3.75 us (15%)
  waiting for transfers between devices  3.19 us (13%)
  local copies, waits for them, and re-layouts  0.69 us (3%)
    all_to_all x1, blocking collectives, local(): lax.all_to_all(image, EVERYONE, split_axis=0, concat_axis=0, tiled=True)  13.1 us
    pallas_call x9, Pallas kernels, call(): pl.pallas_call(kernel, out_shape=shape, in_specs=[pl.BlockSpec(memory_spa...  3.81 us
    ppermute x2, waiting for transfers between devices, beside(): lax.ppermute(value, 'chip', [(source, source ^ step) for source in range(...  3.18 us
    ppermute x2, starting transfers between devices, beside(): lax.ppermute(value, 'chip', [(source, source ^ step) for source in range(...  3.01 us
    unnamed x12, local copies, waits for them, and re-layouts  0.69 us
  transfers between devices with their start and end apart: 4, of which 1 were waited for; matrix products, arithmetic and copies ran while one was open for 0% of the time, Pallas kernels for 9%

profile of v6, /device:TPU:0, one launch (start us, length us, event | category | flops | bytes accessed | tf_op | source)
XLA Modules:
  0.0 24.6 jit_solution(18178394993303265382)
XLA Ops:
  0.0 0.0 copy-start.1
  0.0 0.0 copy-start
  0.0 0.5 %collective-permute-start = (bf16[1,2,64,3840]{3,2,1,0:T(8,128)(2,1)}, bf16[1,2,64,3840]{3,2,1,0:T(8,128)(2,1)S(1)}, u32[]{:S(2)}, u32[]{:S(2)}) collective-permute-start(bf16[1,2,64,3840]{3,2,1,0:T(8,128)(2,1)} %volt_ref.1), channel_id=1, source_target_pairs={{0,1},{1,0},{2,3},{3,2},{4,5},{5,4},{6,7},{7,6},{8,9},{9,8},{10,11... | collective-permute-start | bytes 2949128 | tf_op jit(solution)/shard_map/ppermute | solution.py:197
  0.5 0.0 copy-start.2
  0.5 0.0 copy-start.3
  0.5 0.4 %shard_map.64 = (bf16[64,192]{1,0:T(8,128)(2,1)S(1)}, bf16[256,192]{1,0:T(8,128)(2,1)S(1)}) custom-call(), custom_call_target="tpu_custom_call" | custom-call | flops 2013265920 | bytes 122880 | tf_op jit(solution)/shard_map/pallas_call | solution.py:174
  0.9 0.0 copy-start.4
  0.9 0.0 copy-start.5
  0.9 0.5 %copy-done.2 = bf16[1,1,32,256]{3,2,1,0:T(8,128)(2,1)S(1)} copy-done((bf16[1,1,32,256]{3,2,1,0:T(8,128)(2,1)S(1)}, bf16[1,1,32,256]{3,2,1,0:T(8,128)(2,1)}, u32[]{:S(2)}) %copy-start.2) | copy-done | bytes 16408
  1.3 0.0 copy-done.3
  1.3 0.2 copy-done.4
  1.5 0.0 copy-done.5
  1.5 0.1 shard_map.65.packed_ref.left_ref
  1.6 0.3 %collective-permute-start.1 = (f32[8,128]{1,0:T(8,128)S(1)}, f32[8,128]{1,0:T(8,128)S(1)}, u32[]{:S(2)}, u32[]{:S(2)}) collective-permute-start(f32[8,128]{1,0:T(8,128)S(1)} %shard_map.65.packed_ref.left_ref), channel_id=1, source_target_pairs={{0,1},{1,0},{2,3},{3,2},{4,5},{5,4},{6,7},{7,6},{8,9},{9,8},{10,11... | collective-permute-start | bytes 12296 | tf_op jit(solution)/shard_map/ppermute | solution.py:212
  1.9 0.0 copy-done.1
  1.9 0.0 copy-done
  1.9 0.9 %shard_map.66.part_ref = f32[512,256]{1,0:T(8,128)S(1)} custom-call(bf16[1,2,64,3840]{3,2,1,0:T(8,128)(2,1)S(1)} %copy-done.1, bf16[8,256,256]{2,1,0:T(8,128)(2,1)S(1)} %copy-done, bf16[1,1,32,256]{3,2,1,0:T(8,128)(2,1)S(1)} %copy-done.2, bf16[1,1,32,256]{3,2,1,0:T(8,128)(2,1)S(1)} %copy-done.3, f32[8,128]{1,0:T(8,128)S(1)} %shard_map.65.packed_ref.left_ref), custom_call_target="tpu_custom_call" | custom-call | flops 536870912 | bytes 2592768 | tf_op jit(solution)/shard_map/pallas_call | solution.py:174
  2.8 0.0 collective-permute-done.1.packed_ref.right_ref
  2.9 0.0 collective-permute-done.volt_ref
  2.9 0.6 %shard_map.67._ = bf16[256,256]{1,0:T(8,128)(2,1)S(1)} custom-call(bf16[1,2,64,3840]{3,2,1,0:T(8,128)(2,1)S(1)} %collective-permute-done.volt_ref, bf16[8,256,256]{2,1,0:T(8,128)(2,1)S(1)} %copy-done, bf16[1,1,32,256]{3,2,1,0:T(8,128)(2,1)S(1)} %copy-done.2, bf16[1,1,32,256]{3,2,1,0:T(8,128)(2,1)S(1)} %copy-done.3, ...), custom_call_target="tpu_custom_call" | custom-call | flops 268435456 | bytes 2723840 | tf_op jit(solution)/shard_map/pallas_call | solution.py:174
  3.5 2.9 %collective-permute-start.2 = (bf16[256,256]{1,0:T(8,128)(2,1)S(1)}, bf16[256,256]{1,0:T(8,128)(2,1)S(1)}, u32[]{:S(2)}, u32[]{:S(2)}) collective-permute-start(bf16[256,256]{1,0:T(8,128)(2,1)S(1)} %shard_map.67._), channel_id=1, source_target_pairs={{0,2},{2,0},{1,3},{3,1},{4,6},{6,4},{5,7},{7,5},{8,10},{10,8},{9,1... | collective-permute-start | bytes 393224 | tf_op jit(solution)/shard_map/ppermute | solution.py:222
  6.4 0.1 collective-permute-start.3
  6.5 0.6 %shard_map.69.refs_2_.refs_1_ = bf16[256,256]{1,0:T(8,128)(2,1)S(1)} custom-call(bf16[1,2,64,3840]{3,2,1,0:T(8,128)(2,1)S(1)} %collective-permute-done.volt_ref, bf16[8,256,256]{2,1,0:T(8,128)(2,1)S(1)} %copy-done, bf16[1,1,32,256]{3,2,1,0:T(8,128)(2,1)S(1)} %copy-done.2, bf16[1,1,32,256]{3,2,1,0:T(8,128)(2,1)S(1)} %copy-done.3, ...), custom_call_target="tpu_custom_call" | custom-call | flops 268435456 | bytes 2727936 | tf_op jit(solution)/shard_map/pallas_call | solution.py:174
  7.1 3.2 %collective-permute-done.3.refs_1_ = f32[8,128]{1,0:T(8,128)S(1)} collective-permute-done((f32[8,128]{1,0:T(8,128)S(1)}, f32[8,128]{1,0:T(8,128)S(1)}, u32[]{:S(2)}, u32[]{:S(2)}) %collective-permute-start.3) | collective-permute-done | bytes 4128 | tf_op jit(solution)/shard_map/ppermute | solution.py:222
  10.3 0.2 shard_map.70
  10.5 0.0 collective-permute-done.2.refs_0_
  10.5 0.5 %shard_map.71 = f32[32,128]{1,0:T(8,128)S(1)} custom-call(bf16[256,256]{1,0:T(8,128)(2,1)S(1)} %collective-permute-done.2.refs_0_, bf16[256,256]{1,0:T(8,128)(2,1)S(1)} %shard_map.69.refs_2_.refs_1_, bf16[64,192]{1,0:T(8,128)(2,1)S(1)} %get-tuple-element.11._table_ref.refs_2_, bf16[256,192]{1,0:T(8,128)(2,1)S(1)} %get-tuple-element.12.refs_3_, ...), custom_call_target="tpu_custom_call" | custom-call | bytes 565248 | tf_op jit(solution)/shard_map/pallas_call | solution.py:174
  11.0 13.1 %all_to_all.9.in_ref = f32[32,1,128]{2,1,0:T(1,128)S(1)} all-to-all(f32[32,1,128]{2,1,0:T(1,128)S(1)} %bitcast.3), channel_id=1, replica_groups=mesh['role'=2,'band'=4,'chip'=2,'core'=2] {'role','band','chip','core'}, dimensions={0} | all-to-all | bytes 32768 | tf_op jit(solution)/shard_map/all_to_all | solution.py:250
  24.0 0.5 %shard_map.72 = f32[1,128]{1,0:T(1,128)} custom-call(f32[32,1,128]{2,1,0:T(1,128)S(1)} %all_to_all.9.in_ref), custom_call_target="tpu_custom_call" | custom-call | bytes 16896 | tf_op jit(solution)/shard_map/pallas_call | solution.py:174
  (1 shorter events, 0.0 us)
Async XLA Ops:
  0.0 1.9 %copy-start.1 = (bf16[1,2,64,3840]{3,2,1,0:T(8,128)(2,1)S(1)}, bf16[1,2,64,3840]{3,2,1,0:T(8,128)(2,1)}, u32[]{:S(2)}) copy-start(bf16[1,2,64,3840]{3,2,1,0:T(8,128)(2,1)} %volt_ref.1) | copy-start | bytes 2949124
  0.0 1.9 %copy-start = (bf16[8,256,256]{2,1,0:T(8,128)(2,1)S(1)}, bf16[8,256,256]{2,1,0:T(8,128)(2,1)}, u32[]{:S(2)}) copy-start(bf16[8,256,256]{2,1,0:T(8,128)(2,1)} %taps_ref.5) | copy-start | bytes 3145732
  0.0 2.9 %collective-permute-start = (bf16[1,2,64,3840]{3,2,1,0:T(8,128)(2,1)}, bf16[1,2,64,3840]{3,2,1,0:T(8,128)(2,1)S(1)}, u32[]{:S(2)}, u32[]{:S(2)}) collective-permute-start(bf16[1,2,64,3840]{3,2,1,0:T(8,128)(2,1)} %volt_ref.1), channel_id=1, source_target_pairs={{0,1},{1,0},{2,3},{3,2},{4,5},{5,4},{6,7},{7,6},{8,9},{9,8},{10,11... | collective-permute-start | bytes 2949128 | tf_op jit(solution)/shard_map/ppermute | solution.py:197
  0.5 0.9 %copy-start.2 = (bf16[1,1,32,256]{3,2,1,0:T(8,128)(2,1)S(1)}, bf16[1,1,32,256]{3,2,1,0:T(8,128)(2,1)}, u32[]{:S(2)}) copy-start(bf16[1,1,32,256]{3,2,1,0:T(8,128)(2,1)} %rows_ref.5) | copy-start | bytes 49156
  0.5 0.9 %copy-start.3 = (bf16[1,1,32,256]{3,2,1,0:T(8,128)(2,1)S(1)}, bf16[1,1,32,256]{3,2,1,0:T(8,128)(2,1)}, u32[]{:S(2)}) copy-start(bf16[1,1,32,256]{3,2,1,0:T(8,128)(2,1)} %cols_ref.5) | copy-start | bytes 49156
  0.9 0.7 %copy-start.4 = (s32[2,32,1]{1,2,0:T(1,128)S(1)}, s32[2,32,1]{1,2,0:T(1,128)}, u32[]{:S(2)}) copy-start(s32[2,32,1]{1,2,0:T(1,128)} %param.11) | copy-start | bytes 772
  0.9 0.7 %copy-start.5 = (s32[64]{0:T(128)S(1)}, s32[64]{0:T(128)}, u32[]{:S(2)}) copy-start(s32[64]{0:T(128)} %param.7) | copy-start | bytes 772
  1.6 1.2 %collective-permute-start.1 = (f32[8,128]{1,0:T(8,128)S(1)}, f32[8,128]{1,0:T(8,128)S(1)}, u32[]{:S(2)}, u32[]{:S(2)}) collective-permute-start(f32[8,128]{1,0:T(8,128)S(1)} %shard_map.65.packed_ref.left_ref), channel_id=1, source_target_pairs={{0,1},{1,0},{2,3},{3,2},{4,5},{5,4},{6,7},{7,6},{8,9},{9,8},{10,11... | collective-permute-start | bytes 12296 | tf_op jit(solution)/shard_map/ppermute | solution.py:212
  3.5 7.0 %collective-permute-start.2 = (bf16[256,256]{1,0:T(8,128)(2,1)S(1)}, bf16[256,256]{1,0:T(8,128)(2,1)S(1)}, u32[]{:S(2)}, u32[]{:S(2)}) collective-permute-start(bf16[256,256]{1,0:T(8,128)(2,1)S(1)} %shard_map.67._), channel_id=1, source_target_pairs={{0,2},{2,0},{1,3},{3,1},{4,6},{6,4},{5,7},{7,5},{8,10},{10,8},{9,1... | collective-permute-start | bytes 393224 | tf_op jit(solution)/shard_map/ppermute | solution.py:222
  6.4 3.9 %collective-permute-start.3 = (f32[8,128]{1,0:T(8,128)S(1)}, f32[8,128]{1,0:T(8,128)S(1)}, u32[]{:S(2)}, u32[]{:S(2)}) collective-permute-start(f32[8,128]{1,0:T(8,128)S(1)} %shard_map.68.refs_0_), channel_id=1, source_target_pairs={{0,2},{2,0},{1,3},{3,1},{4,6},{6,4},{5,7},{7,5},{8,10},{10,8},{9,1... | collective-permute-start | bytes 12296 | tf_op jit(solution)/shard_map/ppermute | solution.py:222

commit v7 on v4

--- a/solution.py
+++ b/solution.py
@@ -79,10 +79,9 @@
 def gridded_frames(volt_ref, taps_ref, weights, firsts):
     taps, two_fine, _ = taps_ref.shape
     stations = volt_ref.shape[2]
-    core = lax.axis_index("core")
     lhs = jnp.concatenate(
         [
-            volt_ref[0, core, :, pl.ds(pl.multiple_of(first * two_fine, two_fine), taps * two_fine)]
+            volt_ref[0, 0, :, pl.ds(pl.multiple_of(first * two_fine, two_fine), taps * two_fine)]
             for first in firsts
         ],
         axis=0,
@@ -96,21 +95,31 @@
     return [gridded[:, index * two_fine : (index + 1) * two_fine] for index in range(len(firsts))]
 
 
-def own_kernel(volt_ref, taps_ref, rows_ref, cols_ref, packed_ref, out_ref):
-    weights = gridding_weights(rows_ref, cols_ref, packed_ref, lax.axis_index(TURN), volt_ref.shape[2])
+def own_kernel(first_ref, second_ref, taps_ref, rows_ref, cols_ref, packed_ref, out_ref):
+    weights = gridding_weights(rows_ref, cols_ref, packed_ref, lax.axis_index(TURN), first_ref.shape[2])
     rows = weights.shape[0]
-    for frame, gridded in enumerate(gridded_frames(volt_ref, taps_ref, weights, range(out_ref.shape[0] // rows))):
-        out_ref[frame * rows : (frame + 1) * rows] = gridded
-
-
-def sum_kernel(step, each, volt_ref, taps_ref, rows_ref, cols_ref, own_ref, packed_ref, part_ref, *refs):
+
+    def fill(volt_ref):
+        for frame, gridded in enumerate(gridded_frames(volt_ref, taps_ref, weights, range(out_ref.shape[0] // rows))):
+            out_ref[frame * rows : (frame + 1) * rows] = gridded
+
+    for core, volt_ref in enumerate((first_ref, second_ref)):
+        pl.when(lax.axis_index("core") == core)(functools.partial(fill, volt_ref))
+
+
+def sum_kernel(step, each, first_ref, second_ref, taps_ref, rows_ref, cols_ref, own_ref, packed_ref, part_ref, *refs):
     out_ref = refs[-1]
-    weights = gridding_weights(rows_ref, cols_ref, packed_ref, lax.axis_index(TURN) ^ 1, volt_ref.shape[2])
+    weights = gridding_weights(rows_ref, cols_ref, packed_ref, lax.axis_index(TURN) ^ 1, first_ref.shape[2])
     rows = weights.shape[0]
     firsts = [(lax.axis_index("chip") ^ step) * each + frame for frame in range(each)]
-    for index, gridded in enumerate(gridded_frames(volt_ref, taps_ref, weights, firsts)):
-        held = part_ref[pl.ds(pl.multiple_of(firsts[index] * rows, rows), rows)]
-        out_ref[index * rows : (index + 1) * rows] = (held + gridded).astype(jnp.bfloat16)
+
+    def add(volt_ref):
+        for index, gridded in enumerate(gridded_frames(volt_ref, taps_ref, weights, firsts)):
+            held = part_ref[pl.ds(pl.multiple_of(firsts[index] * rows, rows), rows)]
+            out_ref[index * rows : (index + 1) * rows] = (held + gridded).astype(jnp.bfloat16)
+
+    for core, volt_ref in enumerate((first_ref, second_ref)):
+        pl.when(lax.axis_index("core") == core)(functools.partial(add, volt_ref))
     digits = own_ref[...] + packed_ref[...]
     digits = jnp.concatenate([digits, jnp.zeros((PAD_ROWS - digits.shape[0], digits.shape[1]), jnp.float32)], axis=0)
     out_ref[each * rows :] = digits.astype(jnp.bfloat16)
@@ -190,7 +199,8 @@
     sub_rows = sub_u + sub_v
 
     swap = [(core, 1 - core) for core in range(CORES)]
-    other = lax.ppermute(voltages, "core", swap)
+    own = [voltages[:, core : core + 1] for core in range(CORES)]
+    other = [lax.ppermute(own[core], "core", [(1 - core, core)]) for core in range(CORES)]
     tables = call(
         tables_kernel,
         (
@@ -210,7 +220,7 @@
     part = call(
         own_kernel,
         jax.ShapeDtypeStruct((frames * sub_rows, two_fine), jnp.float32),
-        (voltages, filter_taps, kernel_rows, kernel_cols, packed),
+        (*own, filter_taps, kernel_rows, kernel_cols, packed),
         flops=frames * flops,
     )
 
@@ -220,7 +230,7 @@
         made = call(
             functools.partial(sum_kernel, step, each),
             jax.ShapeDtypeStruct((each * sub_rows + PAD_ROWS, two_fine), jnp.bfloat16),
-            (other, filter_taps, kernel_rows, kernel_cols, packed, other_packed, part, *after),
+            (*other, filter_taps, kernel_rows, kernel_cols, packed, other_packed, part, *after),
             flops=each * flops,
         )
         after = (made,)

time: 24.7 us -> 30.8 us (1.25)
  starting transfers between devices: 3.67 us -> 7.59 us
  local copies, waits for them, and re-layouts: 0.69 us -> 1.94 us
  Pallas kernels: 3.64 us -> 4.34 us
    ppermute x1 -> x2, starting transfers between devices: 0.45 us -> 4.51 us  [local(): lax.ppermute(own[core], 'core', [(1 - core, core)])]
    slice x0 -> x1, local copies, waits for them, and re-layouts: none -> 1.24 us  [local(): own = [voltages[:, core:core + 1] for core in range(CORES)]]
    pallas_call x7, Pallas kernels: 3.64 us -> 4.34 us  [call(): pl.pallas_call(kernel, out_shape=shape, in_specs=[pl.BlockSpec(memory_spa...]
    unnamed x12 -> x10, local copies, waits for them, and re-layouts: 0.69 us -> 0.7 us
  transfers between devices with their start and end apart: 3 -> 4, of which waited for: 1 -> 1; matrix products, arithmetic and copies ran while one was open for 0% -> 0% of each run, Pallas kernels for 8% -> 8%
where the time goes in v7:
time: 30.8 us; the launch traced here: 30.5 us
  blocking collectives  13.1 us (43%)
  starting transfers between devices  7.59 us (25%)
  Pallas kernels  4.34 us (14%)
  waiting for transfers between devices  3.48 us (11%)
  local copies, waits for them, and re-layouts  1.94 us (6%)
    all_to_all x1, blocking collectives, local(): lax.all_to_all(image, EVERYONE, split_axis=0, concat_axis=0, tiled=True)  13.1 us
    ppermute x2, starting transfers between devices, local(): lax.ppermute(own[core], 'core', [(1 - core, core)])  4.51 us
    pallas_call x7, Pallas kernels, call(): pl.pallas_call(kernel, out_shape=shape, in_specs=[pl.BlockSpec(memory_spa...  4.34 us
    ppermute x1, waiting for transfers between devices, local(): lax.ppermute(made, 'chip', [(source, source ^ step) for source in range(c...  3.47 us
    ppermute x1, starting transfers between devices, local(): lax.ppermute(made, 'chip', [(source, source ^ step) for source in range(c...  3 us
    slice x1, local copies, waits for them, and re-layouts, local(): own = [voltages[:, core:core + 1] for core in range(CORES)]  1.24 us
    unnamed x10, local copies, waits for them, and re-layouts  0.7 us
  transfers between devices with their start and end apart: 4, of which 1 were waited for; matrix products, arithmetic and copies ran while one was open for 0% of the time, Pallas kernels for 8%

profile of v7, /device:TPU:0, one launch (start us, length us, event | category | flops | bytes accessed | tf_op | source)
XLA Modules:
  0.0 30.5 jit_solution(2357826130869331441)
XLA Ops:
  0.0 1.2 %fusion = (bf16[1,1,64,3840]{3,2,1,0:T(8,128)(2,1)S(1)}, bf16[1,1,64,3840]{3,2,1,0:T(8,128)(2,1)S(1)}) fusion(bf16[1,2,64,3840]{3,2,1,0:T(8,128)(2,1)} %param.6), kind=kLoop, calls=%fused_computation | loop fusion | bytes 1966080 | tf_op jit(solution)/shard_map/slice | solution.py:202
  1.2 1.3 %collective-permute-start = (bf16[1,1,64,3840]{3,2,1,0:T(8,128)(2,1)S(1)}, bf16[1,1,64,3840]{3,2,1,0:T(8,128)(2,1)S(1)}, u32[]{:S(2)}, u32[]{:S(2)}) collective-permute-start(bf16[1,1,64,3840]{3,2,1,0:T(8,128)(2,1)S(1)} %get-tuple-element.10.first_ref), channel_id=1, source_target_pairs={{1,0},{3,2},{5,4},{7,6},{9,8},{11,10},{13,12},{15,14},{17,16},{19,... | collective-permute-start | bytes 1474568 | tf_op jit(solution)/shard_map/ppermute | solution.py:203
  2.5 0.0 copy-start
  2.6 3.2 %collective-permute-start.1 = (bf16[1,1,64,3840]{3,2,1,0:T(8,128)(2,1)S(1)}, bf16[1,1,64,3840]{3,2,1,0:T(8,128)(2,1)S(1)}, u32[]{:S(2)}, u32[]{:S(2)}) collective-permute-start(bf16[1,1,64,3840]{3,2,1,0:T(8,128)(2,1)S(1)} %get-tuple-element.9.second_ref), channel_id=1, source_target_pairs={{0,1},{2,3},{4,5},{6,7},{8,9},{10,11},{12,13},{14,15},{16,17},{18,... | collective-permute-start | bytes 1474568 | tf_op jit(solution)/shard_map/ppermute | solution.py:203
  5.8 0.0 copy-start.1
  5.8 0.0 copy-start.2
  5.8 0.4 %shard_map.64 = (bf16[64,192]{1,0:T(8,128)(2,1)S(1)}, bf16[256,192]{1,0:T(8,128)(2,1)S(1)}) custom-call(), custom_call_target="tpu_custom_call" | custom-call | flops 2013265920 | bytes 122880 | tf_op jit(solution)/shard_map/pallas_call | solution.py:179
  6.2 0.0 copy-start.3
  6.2 0.0 copy-start.4
  6.2 0.3 copy-done.1
  6.5 0.0 copy-done.2
  6.5 0.4 %copy-done.3 = s32[2,32,1]{1,2,0:T(1,128)S(1)} copy-done((s32[2,32,1]{1,2,0:T(1,128)S(1)}, s32[2,32,1]{1,2,0:T(1,128)}, u32[]{:S(2)}) %copy-start.3) | copy-done | bytes 280
  6.9 0.0 copy-done.4
  6.9 0.1 shard_map.65.packed_ref.own_ref
  7.0 0.1 collective-permute-start.2
  7.1 0.0 copy-done
  7.1 1.1 %shard_map.66.part_ref = f32[512,256]{1,0:T(8,128)S(1)} custom-call(bf16[1,1,64,3840]{3,2,1,0:T(8,128)(2,1)S(1)} %get-tuple-element.10.first_ref, bf16[1,1,64,3840]{3,2,1,0:T(8,128)(2,1)S(1)} %get-tuple-element.9.second_ref, bf16[8,256,256]{2,1,0:T(8,128)(2,1)S(1)} %copy-done, bf16[1,1,32,256]{3,2,1,0:T(8,128)(2,1)S(1)} %copy-done.1, ...), custom_call_target="tpu_custom_call" | custom-call | flops 536870912 | bytes 2596864 | tf_op jit(solution)/shard_map/pallas_call | solution.py:179
  8.2 0.0 collective-permute-done.2.packed_ref
  8.2 0.0 collective-permute-done.first_ref
  8.2 0.0 collective-permute-done.1.second_ref
  8.3 0.8 %shard_map.67.refs_0_ = bf16[272,256]{1,0:T(8,128)(2,1)S(1)} custom-call(bf16[1,1,64,3840]{3,2,1,0:T(8,128)(2,1)S(1)} %collective-permute-done.first_ref, bf16[1,1,64,3840]{3,2,1,0:T(8,128)(2,1)S(1)} %collective-permute-done.1.second_ref, bf16[8,256,256]{2,1,0:T(8,128)(2,1)S(1)} %copy-done, bf16[1,1,32,256]{3,2,1,0:T(8,128)(2,1)S(1)} %copy-done.1, ...), custom_call_target="tpu_custom_call" | custom-call | flops 268435456 | bytes 2744320 | tf_op jit(solution)/shard_map/pallas_call | solution.py:179
  9.1 3.0 %collective-permute-start.3 = (bf16[272,256]{1,0:T(8,128)(2,1)S(1)}, bf16[272,256]{1,0:T(8,128)(2,1)S(1)}, u32[]{:S(2)}, u32[]{:S(2)}) collective-permute-start(bf16[272,256]{1,0:T(8,128)(2,1)S(1)} %shard_map.67.refs_0_), channel_id=1, source_target_pairs={{0,2},{2,0},{1,3},{3,1},{4,6},{6,4},{5,7},{7,5},{8,10},{10,8},{9,1... | collective-permute-start | bytes 417800 | tf_op jit(solution)/shard_map/ppermute | solution.py:238
  12.1 0.8 %shard_map.68.refs_1_ = bf16[272,256]{1,0:T(8,128)(2,1)S(1)} custom-call(bf16[1,1,64,3840]{3,2,1,0:T(8,128)(2,1)S(1)} %collective-permute-done.first_ref, bf16[1,1,64,3840]{3,2,1,0:T(8,128)(2,1)S(1)} %collective-permute-done.1.second_ref, bf16[8,256,256]{2,1,0:T(8,128)(2,1)S(1)} %copy-done, bf16[1,1,32,256]{3,2,1,0:T(8,128)(2,1)S(1)} %copy-done.1, ...), custom_call_target="tpu_custom_call" | custom-call | flops 268435456 | bytes 2883584 | tf_op jit(solution)/shard_map/pallas_call | solution.py:179
  13.0 3.5 %collective-permute-done.3.refs_0_ = bf16[272,256]{1,0:T(8,128)(2,1)S(1)} collective-permute-done((bf16[272,256]{1,0:T(8,128)(2,1)S(1)}, bf16[272,256]{1,0:T(8,128)(2,1)S(1)}, u32[]{:S(2)}, u32[]{:S(2)}) %collective-permute-start.3) | collective-permute-done | bytes 139296 | tf_op jit(solution)/shard_map/ppermute | solution.py:238
  16.4 0.5 %shard_map.69 = f32[32,128]{1,0:T(8,128)S(1)} custom-call(bf16[272,256]{1,0:T(8,128)(2,1)S(1)} %collective-permute-done.3.refs_0_, bf16[272,256]{1,0:T(8,128)(2,1)S(1)} %shard_map.68.refs_1_, bf16[64,192]{1,0:T(8,128)(2,1)S(1)} %get-tuple-element.7._table_ref.refs_2_, bf16[256,192]{1,0:T(8,128)(2,1)S(1)} %get-tuple-element.8.refs_3_), custom_call_target="tpu_custom_call" | custom-call | bytes 417792 | tf_op jit(solution)/shard_map/pallas_call | solution.py:179
  16.9 13.1 %all_to_all.9.in_ref = f32[32,1,128]{2,1,0:T(1,128)S(1)} all-to-all(f32[32,1,128]{2,1,0:T(1,128)S(1)} %bitcast.3), channel_id=1, replica_groups=mesh['role'=2,'band'=4,'chip'=2,'core'=2] {'role','band','chip','core'}, dimensions={0} | all-to-all | bytes 32768 | tf_op jit(solution)/shard_map/all_to_all | solution.py:245
  30.0 0.5 %shard_map.70 = f32[1,128]{1,0:T(1,128)} custom-call(f32[32,1,128]{2,1,0:T(1,128)S(1)} %all_to_all.9.in_ref), custom_call_target="tpu_custom_call" | custom-call | bytes 16896 | tf_op jit(solution)/shard_map/pallas_call | solution.py:179
Async XLA Ops:
  1.2 7.0 %collective-permute-start = (bf16[1,1,64,3840]{3,2,1,0:T(8,128)(2,1)S(1)}, bf16[1,1,64,3840]{3,2,1,0:T(8,128)(2,1)S(1)}, u32[]{:S(2)}, u32[]{:S(2)}) collective-permute-start(bf16[1,1,64,3840]{3,2,1,0:T(8,128)(2,1)S(1)} %get-tuple-element.10.first_ref), channel_id=1, source_target_pairs={{1,0},{3,2},{5,4},{7,6},{9,8},{11,10},{13,12},{15,14},{17,16},{19,... | collective-permute-start | bytes 1474568 | tf_op jit(solution)/shard_map/ppermute | solution.py:203
  2.5 4.5 %copy-start = (bf16[8,256,256]{2,1,0:T(8,128)(2,1)S(1)}, bf16[8,256,256]{2,1,0:T(8,128)(2,1)}, u32[]{:S(2)}) copy-start(bf16[8,256,256]{2,1,0:T(8,128)(2,1)} %taps_ref.5) | copy-start | bytes 3145732
  2.6 5.7 %collective-permute-start.1 = (bf16[1,1,64,3840]{3,2,1,0:T(8,128)(2,1)S(1)}, bf16[1,1,64,3840]{3,2,1,0:T(8,128)(2,1)S(1)}, u32[]{:S(2)}, u32[]{:S(2)}) collective-permute-start(bf16[1,1,64,3840]{3,2,1,0:T(8,128)(2,1)S(1)} %get-tuple-element.9.second_ref), channel_id=1, source_target_pairs={{0,1},{2,3},{4,5},{6,7},{8,9},{10,11},{12,13},{14,15},{16,17},{18,... | collective-permute-start | bytes 1474568 | tf_op jit(solution)/shard_map/ppermute | solution.py:203
  5.8 0.7 %copy-start.1 = (bf16[1,1,32,256]{3,2,1,0:T(8,128)(2,1)S(1)}, bf16[1,1,32,256]{3,2,1,0:T(8,128)(2,1)}, u32[]{:S(2)}) copy-start(bf16[1,1,32,256]{3,2,1,0:T(8,128)(2,1)} %rows_ref.5) | copy-start | bytes 49156
  5.8 0.7 %copy-start.2 = (bf16[1,1,32,256]{3,2,1,0:T(8,128)(2,1)S(1)}, bf16[1,1,32,256]{3,2,1,0:T(8,128)(2,1)}, u32[]{:S(2)}) copy-start(bf16[1,1,32,256]{3,2,1,0:T(8,128)(2,1)} %cols_ref.5) | copy-start | bytes 49156
  6.2 0.7 %copy-start.3 = (s32[2,32,1]{1,2,0:T(1,128)S(1)}, s32[2,32,1]{1,2,0:T(1,128)}, u32[]{:S(2)}) copy-start(s32[2,32,1]{1,2,0:T(1,128)} %param.11) | copy-start | bytes 772
  6.2 0.7 %copy-start.4 = (s32[64]{0:T(128)S(1)}, s32[64]{0:T(128)}, u32[]{:S(2)}) copy-start(s32[64]{0:T(128)} %param.7) | copy-start | bytes 772
  7.0 1.2 %collective-permute-start.2 = (f32[8,256]{1,0:T(8,128)S(1)}, f32[8,256]{1,0:T(8,128)S(1)}, u32[]{:S(2)}, u32[]{:S(2)}) collective-permute-start(f32[8,256]{1,0:T(8,128)S(1)} %shard_map.65.packed_ref.own_ref), channel_id=1, source_target_pairs={{0,1},{1,0},{2,3},{3,2},{4,5},{5,4},{6,7},{7,6},{8,9},{9,8},{10,11... | collective-permute-start | bytes 24584 | tf_op jit(solution)/shard_map/ppermute | solution.py:218
  9.1 7.3 %collective-permute-start.3 = (bf16[272,256]{1,0:T(8,128)(2,1)S(1)}, bf16[272,256]{1,0:T(8,128)(2,1)S(1)}, u32[]{:S(2)}, u32[]{:S(2)}) collective-permute-start(bf16[272,256]{1,0:T(8,128)(2,1)S(1)} %shard_map.67.refs_0_), channel_id=1, source_target_pairs={{0,2},{2,0},{1,3},{3,1},{4,6},{6,4},{5,7},{7,5},{8,10},{10,8},{9,1... | collective-permute-start | bytes 417800 | tf_op jit(solution)/shard_map/ppermute | solution.py:238

commit v8 on v4

--- a/solution.py
+++ b/solution.py
@@ -103,59 +103,76 @@
         out_ref[frame * rows : (frame + 1) * rows] = gridded
 
 
-def sum_kernel(step, each, volt_ref, taps_ref, rows_ref, cols_ref, own_ref, packed_ref, part_ref, *refs):
-    out_ref = refs[-1]
+def other_added(step, each, volt_ref, taps_ref, rows_ref, cols_ref, packed_ref, part_ref):
     weights = gridding_weights(rows_ref, cols_ref, packed_ref, lax.axis_index(TURN) ^ 1, volt_ref.shape[2])
     rows = weights.shape[0]
     firsts = [(lax.axis_index("chip") ^ step) * each + frame for frame in range(each)]
-    for index, gridded in enumerate(gridded_frames(volt_ref, taps_ref, weights, firsts)):
-        held = part_ref[pl.ds(pl.multiple_of(firsts[index] * rows, rows), rows)]
-        out_ref[index * rows : (index + 1) * rows] = (held + gridded).astype(jnp.bfloat16)
-    digits = own_ref[...] + packed_ref[...]
+    return [
+        part_ref[pl.ds(pl.multiple_of(first * rows, rows), rows)] + gridded
+        for first, gridded in zip(firsts, gridded_frames(volt_ref, taps_ref, weights, firsts))
+    ]
+
+
+def far_kernel(step, each, own_ref, *refs):
+    out_ref = refs[-1]
+    made = other_added(step, each, *refs[:6])
+    rows = made[0].shape[0]
+    for index, frame in enumerate(made):
+        out_ref[index * rows : (index + 1) * rows] = frame.astype(jnp.bfloat16)
+    digits = own_ref[...] + refs[4][...]
     digits = jnp.concatenate([digits, jnp.zeros((PAD_ROWS - digits.shape[0], digits.shape[1]), jnp.float32)], axis=0)
     out_ref[each * rows :] = digits.astype(jnp.bfloat16)
 
 
-def image_kernel(pairs_each, *refs):
-    *got, row_dft_ref, col_dft_ref, out_ref = refs
+def cells_side(frames, first, sub):
+    fine = frames[0].shape[1] // 2
+    return jnp.concatenate(
+        [
+            jnp.concatenate([frame[first : first + sub, :fine], frame[first : first + sub, fine:]], axis=0)
+            for frame in frames
+        ],
+        axis=1,
+    )
+
+
+def near_kernel(each, *refs):
+    row_dft_ref, col_dft_ref, _, row_ref, col_ref = refs[6:]
+    made = other_added(0, each, *refs[:6])
+    sub = row_dft_ref.shape[1] // 6
+    for dft_ref, out_ref, first in ((row_dft_ref, row_ref, 0), (col_dft_ref, col_ref, sub)):
+        high, low = split_terms(cells_side(made, first, sub))
+        out_ref[...] = jnp.dot(
+            dft_ref[...], jnp.concatenate([high, high, low], axis=0), preferred_element_type=jnp.float32
+        )
+
+
+def image_kernel(each, own_ref, packed_ref, row_ref, col_ref, row_dft_ref, col_dft_ref, *refs):
+    *got, out_ref = refs
     fine = got[0].shape[1] // 2
     sub = row_dft_ref.shape[1] // 6
-    row_total = out_ref.shape[0]
-    total = got[0][...].astype(jnp.float32)
-    for source in got[1:]:
-        total = total + source[...].astype(jnp.float32)
-    digits = total[pairs_each * 2 * sub :]
+    digits = own_ref[...] + packed_ref[...]
+    for source in got:
+        digits = digits + source[each * 2 * sub :].astype(jnp.float32)[: digits.shape[0]]
     cell_u = (digits[0:1, :fine] * DIGIT + digits[2:3, :fine]).astype(jnp.int32)
     cell_v = (digits[1:2, :fine] * DIGIT + digits[3:4, :fine]).astype(jnp.int32)
 
-    def transform(dft_ref, first, cos, sin):
-        held = jnp.concatenate(
-            [
-                jnp.concatenate(
-                    [
-                        total[index * 2 * sub + first : index * 2 * sub + first + sub, :fine],
-                        total[index * 2 * sub + first : index * 2 * sub + first + sub, fine:],
-                    ],
-                    axis=0,
-                )
-                for index in range(pairs_each)
-            ],
-            axis=1,
-        )
-        high, low = split_terms(held)
-        plain = jnp.dot(
-            dft_ref[...], jnp.concatenate([high, high, low], axis=0), preferred_element_type=jnp.float32
-        )
+    def side(plain_ref, dft_ref, first, cell):
+        plain = plain_ref[...]
         half = plain.shape[0] // 2
+        for source in got:
+            frames = [source[index * 2 * sub : (index + 1) * 2 * sub] for index in range(each)]
+            held = cells_side(frames, first, sub)
+            plain = plain + jnp.dot(
+                dft_ref[:, : 4 * sub], jnp.concatenate([held, held], axis=0), preferred_element_type=jnp.float32
+            )
+        cos, sin = phase(cell, lax.broadcasted_iota(jnp.int32, (half, fine), 0) - half // 2)
+        cos = jnp.concatenate([cos] * each, axis=1)
+        sin = jnp.concatenate([sin] * each, axis=1)
         real, imag = plain[:half], plain[half:]
-        cos = jnp.concatenate([cos] * pairs_each, axis=1)
-        sin = jnp.concatenate([sin] * pairs_each, axis=1)
         return real * cos - imag * sin, real * sin + imag * cos
 
-    row = lax.broadcasted_iota(jnp.int32, (row_total, fine), 0)
-    row_real, row_imag = transform(row_dft_ref, 0, *phase(cell_u, row - row_total // 2))
-    col = lax.broadcasted_iota(jnp.int32, (MW, fine), 0)
-    col_real, col_imag = transform(col_dft_ref, sub, *phase(cell_v, col - MW // 2))
+    row_real, row_imag = side(row_ref, row_dft_ref, 0, cell_u)
+    col_real, col_imag = side(col_ref, col_dft_ref, sub, cell_v)
     left = jnp.concatenate([row_real, -row_imag], axis=1).astype(jnp.bfloat16)
     right = jnp.concatenate([col_real, col_imag], axis=1).astype(jnp.bfloat16)
     out_ref[...] = lax.dot_general(left, right, (((1,), (1,)), ((), ())), preferred_element_type=jnp.float32)
@@ -214,23 +231,32 @@
         flops=frames * flops,
     )
 
+    summed = (other, filter_taps, kernel_rows, kernel_cols, other_packed, part)
     after = ()
     got = []
-    for step in [*range(1, chips), 0]:
+    for step in range(1, chips):
         made = call(
-            functools.partial(sum_kernel, step, each),
+            functools.partial(far_kernel, step, each),
             jax.ShapeDtypeStruct((each * sub_rows + PAD_ROWS, two_fine), jnp.bfloat16),
-            (other, filter_taps, kernel_rows, kernel_cols, packed, other_packed, part, *after),
+            (packed, *summed, *after),
             flops=each * flops,
         )
         after = (made,)
-        if step:
-            made = lax.ppermute(made, "chip", [(source, source ^ step) for source in range(chips)])
-        got.append(made)
+        got.append(lax.ppermute(made, "chip", [(source, source ^ step) for source in range(chips)]))
+    lanes = each * two_fine // 2
+    sides = call(
+        functools.partial(near_kernel, each),
+        (
+            jax.ShapeDtypeStruct((2 * row_total, lanes), jnp.float32),
+            jax.ShapeDtypeStruct((2 * MW, lanes), jnp.float32),
+        ),
+        (*summed, *tables, *after),
+        flops=each * flops,
+    )
     image = call(
         functools.partial(image_kernel, each),
         jax.ShapeDtypeStruct((row_total, MW), jnp.float32),
-        (*got, *tables),
+        (packed, other_packed, *sides, *tables, *got),
     )
     rows = lax.all_to_all(image, EVERYONE, split_axis=0, concat_axis=0, tiled=True)
     return call(

time: 24.7 us -> 24.7 us (level)
  waiting for transfers between devices: 3.38 us -> 3.01 us
  Pallas kernels: 3.64 us -> 4.01 us
    pallas_call x7, Pallas kernels: 3.64 us -> 4.01 us  [call(): pl.pallas_call(kernel, out_shape=shape, in_specs=[pl.BlockSpec(memory_spa...]
    ppermute x1, waiting for transfers between devices: 3.36 us -> 2.99 us  [local(): lax.ppermute(made, 'chip', [(source, source ^ step) for source in range(c...]
  transfers between devices with their start and end apart: 3 -> 3, of which waited for: 1 -> 1; matrix products, arithmetic and copies ran while one was open for 0% -> 0% of each run, Pallas kernels for 8% -> 10%
where the time goes in v8:
time: 24.7 us; the launch traced here: 24.5 us
  blocking collectives  13.1 us (53%)
  Pallas kernels  4.01 us (16%)
  starting transfers between devices  3.67 us (15%)
  waiting for transfers between devices  3.01 us (12%)
  local copies, waits for them, and re-layouts  0.69 us (3%)
    all_to_all x1, blocking collectives, local(): lax.all_to_all(image, EVERYONE, split_axis=0, concat_axis=0, tiled=True)  13.1 us
    pallas_call x7, Pallas kernels, call(): pl.pallas_call(kernel, out_shape=shape, in_specs=[pl.BlockSpec(memory_spa...  4.01 us
    ppermute x1, waiting for transfers between devices, local(): lax.ppermute(made, 'chip', [(source, source ^ step) for source in range(c...  2.99 us
    ppermute x1, starting transfers between devices, local(): lax.ppermute(made, 'chip', [(source, source ^ step) for source in range(c...  2.91 us
    unnamed x12, local copies, waits for them, and re-layouts  0.69 us
  transfers between devices with their start and end apart: 3, of which 1 were waited for; matrix products, arithmetic and copies ran while one was open for 0% of the time, Pallas kernels for 10%

profile of v8, /device:TPU:0, one launch (start us, length us, event | category | flops | bytes accessed | tf_op | source)
XLA Modules:
  0.0 24.5 jit_solution(12046339525360781251)
XLA Ops:
  0.0 0.0 copy-start.1
  0.0 0.0 copy-start
  0.0 0.5 %collective-permute-start.1 = (bf16[1,2,64,3840]{3,2,1,0:T(8,128)(2,1)}, bf16[1,2,64,3840]{3,2,1,0:T(8,128)(2,1)S(1)}, u32[]{:S(2)}, u32[]{:S(2)}) collective-permute-start(bf16[1,2,64,3840]{3,2,1,0:T(8,128)(2,1)} %volt_ref.1), channel_id=1, source_target_pairs={{0,1},{1,0},{2,3},{3,2},{4,5},{5,4},{6,7},{7,6},{8,9},{9,8},{10,11... | collective-permute-start | bytes 2949128 | tf_op jit(solution)/shard_map/ppermute | solution.py:210
  0.5 0.0 copy-start.2
  0.5 0.0 copy-start.3
  0.5 0.4 %shard_map.64 = (bf16[64,192]{1,0:T(8,128)(2,1)S(1)}, bf16[256,192]{1,0:T(8,128)(2,1)S(1)}) custom-call(), custom_call_target="tpu_custom_call" | custom-call | flops 2013265920 | bytes 122880 | tf_op jit(solution)/shard_map/pallas_call | solution.py:187
  0.9 0.0 copy-start.4
  0.9 0.0 copy-start.5
  0.9 0.5 %copy-done.2 = bf16[1,1,32,256]{3,2,1,0:T(8,128)(2,1)S(1)} copy-done((bf16[1,1,32,256]{3,2,1,0:T(8,128)(2,1)S(1)}, bf16[1,1,32,256]{3,2,1,0:T(8,128)(2,1)}, u32[]{:S(2)}) %copy-start.2) | copy-done | bytes 16408
  1.3 0.0 copy-done.3
  1.3 0.2 copy-done.4
  1.5 0.0 copy-done.5
  1.5 0.1 shard_map.65.packed_ref.own_ref
  1.6 0.3 %collective-permute-start = (f32[8,256]{1,0:T(8,128)S(1)}, f32[8,256]{1,0:T(8,128)S(1)}, u32[]{:S(2)}, u32[]{:S(2)}) collective-permute-start(f32[8,256]{1,0:T(8,128)S(1)} %shard_map.65.packed_ref.own_ref), channel_id=1, source_target_pairs={{0,1},{1,0},{2,3},{3,2},{4,5},{5,4},{6,7},{7,6},{8,9},{9,8},{10,11... | collective-permute-start | bytes 24584 | tf_op jit(solution)/shard_map/ppermute | solution.py:225
  1.9 0.0 copy-done.1
  1.9 0.0 copy-done
  1.9 0.9 %shard_map.66.refs_5_ = f32[512,256]{1,0:T(8,128)S(1)} custom-call(bf16[1,2,64,3840]{3,2,1,0:T(8,128)(2,1)S(1)} %copy-done.1, bf16[8,256,256]{2,1,0:T(8,128)(2,1)S(1)} %copy-done, bf16[1,1,32,256]{3,2,1,0:T(8,128)(2,1)S(1)} %copy-done.2, bf16[1,1,32,256]{3,2,1,0:T(8,128)(2,1)S(1)} %copy-done.3, f32[8,256]{1,0:T(8,128)S(1)} %shard_map.65.packed_ref.own_ref), custom_call_target="tpu_custom_call" | custom-call | flops 536870912 | bytes 2596864 | tf_op jit(solution)/shard_map/pallas_call | solution.py:187
  2.8 0.0 collective-permute-done.refs_4_.packed_ref
  2.9 0.0 collective-permute-done.1.refs_0_
  2.9 0.6 %shard_map.67.refs_8_ = bf16[272,256]{1,0:T(8,128)(2,1)S(1)} custom-call(f32[8,256]{1,0:T(8,128)S(1)} %shard_map.65.packed_ref.own_ref, bf16[1,2,64,3840]{3,2,1,0:T(8,128)(2,1)S(1)} %collective-permute-done.1.refs_0_, bf16[8,256,256]{2,1,0:T(8,128)(2,1)S(1)} %copy-done, bf16[1,1,32,256]{3,2,1,0:T(8,128)(2,1)S(1)} %copy-done.2, ...), custom_call_target="tpu_custom_call" | custom-call | flops 268435456 | bytes 2744320 | tf_op jit(solution)/shard_map/pallas_call | solution.py:187
  3.5 2.9 %collective-permute-start.2 = (bf16[272,256]{1,0:T(8,128)(2,1)S(1)}, bf16[272,256]{1,0:T(8,128)(2,1)S(1)}, u32[]{:S(2)}, u32[]{:S(2)}) collective-permute-start(bf16[272,256]{1,0:T(8,128)(2,1)S(1)} %shard_map.67.refs_8_), channel_id=1, source_target_pairs={{0,2},{2,0},{1,3},{3,1},{4,6},{6,4},{5,7},{7,5},{8,10},{10,8},{9,1... | collective-permute-start | bytes 417800 | tf_op jit(solution)/shard_map/ppermute | solution.py:245
  6.4 1.0 %shard_map.68 = (f32[64,512]{1,0:T(8,128)S(1)}, f32[256,512]{1,0:T(8,128)S(1)}) custom-call(bf16[1,2,64,3840]{3,2,1,0:T(8,128)(2,1)S(1)} %collective-permute-done.1.refs_0_, bf16[8,256,256]{2,1,0:T(8,128)(2,1)S(1)} %copy-done, bf16[1,1,32,256]{3,2,1,0:T(8,128)(2,1)S(1)} %copy-done.2, bf16[1,1,32,256]{3,2,1,0:T(8,128)(2,1)S(1)} %copy-done.3, ...), custom_call_target="tpu_custom_call" | custom-call | flops 268435456 | bytes 3514368 | tf_op jit(solution)/shard_map/pallas_call | solution.py:187
  7.4 3.0 %collective-permute-done.2.refs_0_ = bf16[272,256]{1,0:T(8,128)(2,1)S(1)} collective-permute-done((bf16[272,256]{1,0:T(8,128)(2,1)S(1)}, bf16[272,256]{1,0:T(8,128)(2,1)S(1)}, u32[]{:S(2)}, u32[]{:S(2)}) %collective-permute-start.2) | collective-permute-done | bytes 139296 | tf_op jit(solution)/shard_map/ppermute | solution.py:245
  10.4 0.5 %shard_map.69 = f32[32,128]{1,0:T(8,128)S(1)} custom-call(f32[8,256]{1,0:T(8,128)S(1)} %shard_map.65.packed_ref.own_ref, f32[8,256]{1,0:T(8,128)S(1)} %collective-permute-done.refs_4_.packed_ref, f32[64,512]{1,0:T(8,128)S(1)} %get-tuple-element.11.row_ref, f32[256,512]{1,0:T(8,128)S(1)} %get-tuple-element.12.col_ref, ...), custom_call_target="tpu_custom_call" | custom-call | bytes 950272 | tf_op jit(solution)/shard_map/pallas_call | solution.py:187
  10.9 13.1 %all_to_all.9.in_ref = f32[32,1,128]{2,1,0:T(1,128)S(1)} all-to-all(f32[32,1,128]{2,1,0:T(1,128)S(1)} %bitcast.3), channel_id=1, replica_groups=mesh['role'=2,'band'=4,'chip'=2,'core'=2] {'role','band','chip','core'}, dimensions={0} | all-to-all | bytes 32768 | tf_op jit(solution)/shard_map/all_to_all | solution.py:261
  24.0 0.5 %shard_map.70 = f32[1,128]{1,0:T(1,128)} custom-call(f32[32,1,128]{2,1,0:T(1,128)S(1)} %all_to_all.9.in_ref), custom_call_target="tpu_custom_call" | custom-call | bytes 16896 | tf_op jit(solution)/shard_map/pallas_call | solution.py:187
Async XLA Ops:
  0.0 1.9 %copy-start.1 = (bf16[1,2,64,3840]{3,2,1,0:T(8,128)(2,1)S(1)}, bf16[1,2,64,3840]{3,2,1,0:T(8,128)(2,1)}, u32[]{:S(2)}) copy-start(bf16[1,2,64,3840]{3,2,1,0:T(8,128)(2,1)} %volt_ref.1) | copy-start | bytes 2949124
  0.0 1.9 %copy-start = (bf16[8,256,256]{2,1,0:T(8,128)(2,1)S(1)}, bf16[8,256,256]{2,1,0:T(8,128)(2,1)}, u32[]{:S(2)}) copy-start(bf16[8,256,256]{2,1,0:T(8,128)(2,1)} %refs_1_.3) | copy-start | bytes 3145732
  0.0 2.9 %collective-permute-start.1 = (bf16[1,2,64,3840]{3,2,1,0:T(8,128)(2,1)}, bf16[1,2,64,3840]{3,2,1,0:T(8,128)(2,1)S(1)}, u32[]{:S(2)}, u32[]{:S(2)}) collective-permute-start(bf16[1,2,64,3840]{3,2,1,0:T(8,128)(2,1)} %volt_ref.1), channel_id=1, source_target_pairs={{0,1},{1,0},{2,3},{3,2},{4,5},{5,4},{6,7},{7,6},{8,9},{9,8},{10,11... | collective-permute-start | bytes 2949128 | tf_op jit(solution)/shard_map/ppermute | solution.py:210
  0.5 0.9 %copy-start.2 = (bf16[1,1,32,256]{3,2,1,0:T(8,128)(2,1)S(1)}, bf16[1,1,32,256]{3,2,1,0:T(8,128)(2,1)}, u32[]{:S(2)}) copy-start(bf16[1,1,32,256]{3,2,1,0:T(8,128)(2,1)} %refs_2_.3) | copy-start | bytes 49156
  0.5 0.9 %copy-start.3 = (bf16[1,1,32,256]{3,2,1,0:T(8,128)(2,1)S(1)}, bf16[1,1,32,256]{3,2,1,0:T(8,128)(2,1)}, u32[]{:S(2)}) copy-start(bf16[1,1,32,256]{3,2,1,0:T(8,128)(2,1)} %refs_3_.3) | copy-start | bytes 49156
  0.9 0.7 %copy-start.4 = (s32[2,32,1]{1,2,0:T(1,128)S(1)}, s32[2,32,1]{1,2,0:T(1,128)}, u32[]{:S(2)}) copy-start(s32[2,32,1]{1,2,0:T(1,128)} %param.11) | copy-start | bytes 772
  0.9 0.7 %copy-start.5 = (s32[64]{0:T(128)S(1)}, s32[64]{0:T(128)}, u32[]{:S(2)}) copy-start(s32[64]{0:T(128)} %param.7) | copy-start | bytes 772
  1.6 1.2 %collective-permute-start = (f32[8,256]{1,0:T(8,128)S(1)}, f32[8,256]{1,0:T(8,128)S(1)}, u32[]{:S(2)}, u32[]{:S(2)}) collective-permute-start(f32[8,256]{1,0:T(8,128)S(1)} %shard_map.65.packed_ref.own_ref), channel_id=1, source_target_pairs={{0,1},{1,0},{2,3},{3,2},{4,5},{5,4},{6,7},{7,6},{8,9},{9,8},{10,11... | collective-permute-start | bytes 24584 | tf_op jit(solution)/shard_map/ppermute | solution.py:225
  3.5 6.9 %collective-permute-start.2 = (bf16[272,256]{1,0:T(8,128)(2,1)S(1)}, bf16[272,256]{1,0:T(8,128)(2,1)S(1)}, u32[]{:S(2)}, u32[]{:S(2)}) collective-permute-start(bf16[272,256]{1,0:T(8,128)(2,1)S(1)} %shard_map.67.refs_8_), channel_id=1, source_target_pairs={{0,2},{2,0},{1,3},{3,1},{4,6},{6,4},{5,7},{7,5},{8,10},{10,8},{9,1... | collective-permute-start | bytes 417800 | tf_op jit(solution)/shard_map/ppermute | solution.py:245

commit v9 on v8

--- a/solution.py
+++ b/solution.py
@@ -166,16 +166,18 @@
                 dft_ref[:, : 4 * sub], jnp.concatenate([held, held], axis=0), preferred_element_type=jnp.float32
             )
         cos, sin = phase(cell, lax.broadcasted_iota(jnp.int32, (half, fine), 0) - half // 2)
-        cos = jnp.concatenate([cos] * each, axis=1)
-        sin = jnp.concatenate([sin] * each, axis=1)
-        real, imag = plain[:half], plain[half:]
-        return real * cos - imag * sin, real * sin + imag * cos
-
-    row_real, row_imag = side(row_ref, row_dft_ref, 0, cell_u)
-    col_real, col_imag = side(col_ref, col_dft_ref, sub, cell_v)
-    left = jnp.concatenate([row_real, -row_imag], axis=1).astype(jnp.bfloat16)
-    right = jnp.concatenate([col_real, col_imag], axis=1).astype(jnp.bfloat16)
-    out_ref[...] = lax.dot_general(left, right, (((1,), (1,)), ((), ())), preferred_element_type=jnp.float32)
+        turned = []
+        for index in range(each):
+            real, imag = (plain[part : part + half, index * fine : (index + 1) * fine] for part in (0, half))
+            turned.append((real * cos - imag * sin, real * sin + imag * cos))
+        return turned
+
+    image = jnp.zeros(out_ref.shape, jnp.float32)
+    for row, col in zip(side(row_ref, row_dft_ref, 0, cell_u), side(col_ref, col_dft_ref, sub, cell_v)):
+        left = jnp.concatenate([row[0], -row[1]], axis=1).astype(jnp.bfloat16)
+        right = jnp.concatenate(col, axis=1).astype(jnp.bfloat16)
+        image = image + lax.dot_general(left, right, (((1,), (1,)), ((), ())), preferred_element_type=jnp.float32)
+    out_ref[...] = image
 
 
 def final_kernel(scale_factor, in_ref, out_ref):

time: 24.7 us -> 24.7 us (level)
  no operation moved by 1% of the time
where the time goes in v9:
time: 24.7 us; the launch traced here: 24.5 us
  blocking collectives  13.1 us (53%)
  Pallas kernels  4.01 us (16%)
  starting transfers between devices  3.67 us (15%)
  waiting for transfers between devices  3.01 us (12%)
  local copies, waits for them, and re-layouts  0.69 us (3%)
    all_to_all x1, blocking collectives, local(): lax.all_to_all(image, EVERYONE, split_axis=0, concat_axis=0, tiled=True)  13.1 us
    pallas_call x7, Pallas kernels, call(): pl.pallas_call(kernel, out_shape=shape, in_specs=[pl.BlockSpec(memory_spa...  4.01 us
    ppermute x1, waiting for transfers between devices, local(): lax.ppermute(made, 'chip', [(source, source ^ step) for source in range(c...  2.99 us
    ppermute x1, starting transfers between devices, local(): lax.ppermute(made, 'chip', [(source, source ^ step) for source in range(c...  2.91 us
    unnamed x12, local copies, waits for them, and re-layouts  0.69 us
  transfers between devices with their start and end apart: 3, of which 1 were waited for; matrix products, arithmetic and copies ran while one was open for 0% of the time, Pallas kernels for 10%

profile of v9, /device:TPU:0, one launch (start us, length us, event | category | flops | bytes accessed | tf_op | source)
XLA Modules:
  0.0 24.5 jit_solution(18128018964120782310)
XLA Ops:
  0.0 0.0 copy-start.1
  0.0 0.0 copy-start
  0.0 0.5 %collective-permute-start.1 = (bf16[1,2,64,3840]{3,2,1,0:T(8,128)(2,1)}, bf16[1,2,64,3840]{3,2,1,0:T(8,128)(2,1)S(1)}, u32[]{:S(2)}, u32[]{:S(2)}) collective-permute-start(bf16[1,2,64,3840]{3,2,1,0:T(8,128)(2,1)} %volt_ref.1), channel_id=1, source_target_pairs={{0,1},{1,0},{2,3},{3,2},{4,5},{5,4},{6,7},{7,6},{8,9},{9,8},{10,11... | collective-permute-start | bytes 2949128 | tf_op jit(solution)/shard_map/ppermute | solution.py:212
  0.5 0.0 copy-start.2
  0.5 0.0 copy-start.3
  0.5 0.4 %shard_map.64 = (bf16[64,192]{1,0:T(8,128)(2,1)S(1)}, bf16[256,192]{1,0:T(8,128)(2,1)S(1)}) custom-call(), custom_call_target="tpu_custom_call" | custom-call | flops 2013265920 | bytes 122880 | tf_op jit(solution)/shard_map/pallas_call | solution.py:189
  0.9 0.0 copy-start.4
  0.9 0.0 copy-start.5
  0.9 0.5 %copy-done.2 = bf16[1,1,32,256]{3,2,1,0:T(8,128)(2,1)S(1)} copy-done((bf16[1,1,32,256]{3,2,1,0:T(8,128)(2,1)S(1)}, bf16[1,1,32,256]{3,2,1,0:T(8,128)(2,1)}, u32[]{:S(2)}) %copy-start.2) | copy-done | bytes 16408
  1.3 0.0 copy-done.3
  1.3 0.2 copy-done.4
  1.5 0.0 copy-done.5
  1.5 0.1 shard_map.65.packed_ref.own_ref
  1.6 0.3 %collective-permute-start = (f32[8,256]{1,0:T(8,128)S(1)}, f32[8,256]{1,0:T(8,128)S(1)}, u32[]{:S(2)}, u32[]{:S(2)}) collective-permute-start(f32[8,256]{1,0:T(8,128)S(1)} %shard_map.65.packed_ref.own_ref), channel_id=1, source_target_pairs={{0,1},{1,0},{2,3},{3,2},{4,5},{5,4},{6,7},{7,6},{8,9},{9,8},{10,11... | collective-permute-start | bytes 24584 | tf_op jit(solution)/shard_map/ppermute | solution.py:227
  1.9 0.0 copy-done.1
  1.9 0.0 copy-done
  1.9 0.9 %shard_map.66.refs_5_ = f32[512,256]{1,0:T(8,128)S(1)} custom-call(bf16[1,2,64,3840]{3,2,1,0:T(8,128)(2,1)S(1)} %copy-done.1, bf16[8,256,256]{2,1,0:T(8,128)(2,1)S(1)} %copy-done, bf16[1,1,32,256]{3,2,1,0:T(8,128)(2,1)S(1)} %copy-done.2, bf16[1,1,32,256]{3,2,1,0:T(8,128)(2,1)S(1)} %copy-done.3, f32[8,256]{1,0:T(8,128)S(1)} %shard_map.65.packed_ref.own_ref), custom_call_target="tpu_custom_call" | custom-call | flops 536870912 | bytes 2596864 | tf_op jit(solution)/shard_map/pallas_call | solution.py:189
  2.8 0.0 collective-permute-done.refs_4_.packed_ref
  2.9 0.0 collective-permute-done.1.refs_0_
  2.9 0.6 %shard_map.67.refs_8_ = bf16[272,256]{1,0:T(8,128)(2,1)S(1)} custom-call(f32[8,256]{1,0:T(8,128)S(1)} %shard_map.65.packed_ref.own_ref, bf16[1,2,64,3840]{3,2,1,0:T(8,128)(2,1)S(1)} %collective-permute-done.1.refs_0_, bf16[8,256,256]{2,1,0:T(8,128)(2,1)S(1)} %copy-done, bf16[1,1,32,256]{3,2,1,0:T(8,128)(2,1)S(1)} %copy-done.2, ...), custom_call_target="tpu_custom_call" | custom-call | flops 268435456 | bytes 2744320 | tf_op jit(solution)/shard_map/pallas_call | solution.py:189
  3.5 2.9 %collective-permute-start.2 = (bf16[272,256]{1,0:T(8,128)(2,1)S(1)}, bf16[272,256]{1,0:T(8,128)(2,1)S(1)}, u32[]{:S(2)}, u32[]{:S(2)}) collective-permute-start(bf16[272,256]{1,0:T(8,128)(2,1)S(1)} %shard_map.67.refs_8_), channel_id=1, source_target_pairs={{0,2},{2,0},{1,3},{3,1},{4,6},{6,4},{5,7},{7,5},{8,10},{10,8},{9,1... | collective-permute-start | bytes 417800 | tf_op jit(solution)/shard_map/ppermute | solution.py:247
  6.4 1.0 %shard_map.68 = (f32[64,512]{1,0:T(8,128)S(1)}, f32[256,512]{1,0:T(8,128)S(1)}) custom-call(bf16[1,2,64,3840]{3,2,1,0:T(8,128)(2,1)S(1)} %collective-permute-done.1.refs_0_, bf16[8,256,256]{2,1,0:T(8,128)(2,1)S(1)} %copy-done, bf16[1,1,32,256]{3,2,1,0:T(8,128)(2,1)S(1)} %copy-done.2, bf16[1,1,32,256]{3,2,1,0:T(8,128)(2,1)S(1)} %copy-done.3, ...), custom_call_target="tpu_custom_call" | custom-call | flops 268435456 | bytes 3514368 | tf_op jit(solution)/shard_map/pallas_call | solution.py:189
  7.4 3.0 %collective-permute-done.2.refs_0_ = bf16[272,256]{1,0:T(8,128)(2,1)S(1)} collective-permute-done((bf16[272,256]{1,0:T(8,128)(2,1)S(1)}, bf16[272,256]{1,0:T(8,128)(2,1)S(1)}, u32[]{:S(2)}, u32[]{:S(2)}) %collective-permute-start.2) | collective-permute-done | bytes 139296 | tf_op jit(solution)/shard_map/ppermute | solution.py:247
  10.4 0.5 %shard_map.69 = f32[32,128]{1,0:T(8,128)S(1)} custom-call(f32[8,256]{1,0:T(8,128)S(1)} %shard_map.65.packed_ref.own_ref, f32[8,256]{1,0:T(8,128)S(1)} %collective-permute-done.refs_4_.packed_ref, f32[64,512]{1,0:T(8,128)S(1)} %get-tuple-element.11.row_ref, f32[256,512]{1,0:T(8,128)S(1)} %get-tuple-element.12.col_ref, ...), custom_call_target="tpu_custom_call" | custom-call | bytes 950272 | tf_op jit(solution)/shard_map/pallas_call | solution.py:189
  10.9 13.1 %all_to_all.9.in_ref = f32[32,1,128]{2,1,0:T(1,128)S(1)} all-to-all(f32[32,1,128]{2,1,0:T(1,128)S(1)} %bitcast.3), channel_id=1, replica_groups=mesh['role'=2,'band'=4,'chip'=2,'core'=2] {'role','band','chip','core'}, dimensions={0} | all-to-all | bytes 32768 | tf_op jit(solution)/shard_map/all_to_all | solution.py:263
  23.9 0.5 %shard_map.70 = f32[1,128]{1,0:T(1,128)} custom-call(f32[32,1,128]{2,1,0:T(1,128)S(1)} %all_to_all.9.in_ref), custom_call_target="tpu_custom_call" | custom-call | bytes 16896 | tf_op jit(solution)/shard_map/pallas_call | solution.py:189
Async XLA Ops:
  0.0 1.9 %copy-start.1 = (bf16[1,2,64,3840]{3,2,1,0:T(8,128)(2,1)S(1)}, bf16[1,2,64,3840]{3,2,1,0:T(8,128)(2,1)}, u32[]{:S(2)}) copy-start(bf16[1,2,64,3840]{3,2,1,0:T(8,128)(2,1)} %volt_ref.1) | copy-start | bytes 2949124
  0.0 1.9 %copy-start = (bf16[8,256,256]{2,1,0:T(8,128)(2,1)S(1)}, bf16[8,256,256]{2,1,0:T(8,128)(2,1)}, u32[]{:S(2)}) copy-start(bf16[8,256,256]{2,1,0:T(8,128)(2,1)} %refs_1_.3) | copy-start | bytes 3145732
  0.0 2.9 %collective-permute-start.1 = (bf16[1,2,64,3840]{3,2,1,0:T(8,128)(2,1)}, bf16[1,2,64,3840]{3,2,1,0:T(8,128)(2,1)S(1)}, u32[]{:S(2)}, u32[]{:S(2)}) collective-permute-start(bf16[1,2,64,3840]{3,2,1,0:T(8,128)(2,1)} %volt_ref.1), channel_id=1, source_target_pairs={{0,1},{1,0},{2,3},{3,2},{4,5},{5,4},{6,7},{7,6},{8,9},{9,8},{10,11... | collective-permute-start | bytes 2949128 | tf_op jit(solution)/shard_map/ppermute | solution.py:212
  0.5 0.9 %copy-start.2 = (bf16[1,1,32,256]{3,2,1,0:T(8,128)(2,1)S(1)}, bf16[1,1,32,256]{3,2,1,0:T(8,128)(2,1)}, u32[]{:S(2)}) copy-start(bf16[1,1,32,256]{3,2,1,0:T(8,128)(2,1)} %refs_2_.3) | copy-start | bytes 49156
  0.5 0.9 %copy-start.3 = (bf16[1,1,32,256]{3,2,1,0:T(8,128)(2,1)S(1)}, bf16[1,1,32,256]{3,2,1,0:T(8,128)(2,1)}, u32[]{:S(2)}) copy-start(bf16[1,1,32,256]{3,2,1,0:T(8,128)(2,1)} %refs_3_.3) | copy-start | bytes 49156
  0.9 0.7 %copy-start.4 = (s32[2,32,1]{1,2,0:T(1,128)S(1)}, s32[2,32,1]{1,2,0:T(1,128)}, u32[]{:S(2)}) copy-start(s32[2,32,1]{1,2,0:T(1,128)} %param.11) | copy-start | bytes 772
  0.9 0.7 %copy-start.5 = (s32[64]{0:T(128)S(1)}, s32[64]{0:T(128)}, u32[]{:S(2)}) copy-start(s32[64]{0:T(128)} %param.7) | copy-start | bytes 772
  1.6 1.2 %collective-permute-start = (f32[8,256]{1,0:T(8,128)S(1)}, f32[8,256]{1,0:T(8,128)S(1)}, u32[]{:S(2)}, u32[]{:S(2)}) collective-permute-start(f32[8,256]{1,0:T(8,128)S(1)} %shard_map.65.packed_ref.own_ref), channel_id=1, source_target_pairs={{0,1},{1,0},{2,3},{3,2},{4,5},{5,4},{6,7},{7,6},{8,9},{9,8},{10,11... | collective-permute-start | bytes 24584 | tf_op jit(solution)/shard_map/ppermute | solution.py:227
  3.5 6.9 %collective-permute-start.2 = (bf16[272,256]{1,0:T(8,128)(2,1)S(1)}, bf16[272,256]{1,0:T(8,128)(2,1)S(1)}, u32[]{:S(2)}, u32[]{:S(2)}) collective-permute-start(bf16[272,256]{1,0:T(8,128)(2,1)S(1)} %shard_map.67.refs_8_), channel_id=1, source_target_pairs={{0,2},{2,0},{1,3},{3,1},{4,6},{6,4},{5,7},{7,5},{8,10},{10,8},{9,1... | collective-permute-start | bytes 417800 | tf_op jit(solution)/shard_map/ppermute | solution.py:247

commit v10 on v8

--- a/solution.py
+++ b/solution.py
@@ -42,7 +42,11 @@
     )
 
 
-def tables_kernel(row_ref, col_ref):
+def token_kernel(out_ref):
+    out_ref[...] = jnp.zeros_like(out_ref)
+
+
+def tables_kernel(_, row_ref, col_ref):
     for out_ref, sign in ((row_ref, 1), (col_ref, -1)):
         pixels, cells = out_ref.shape[0] // 2, out_ref.shape[1] // 6
         place = lax.broadcasted_iota(jnp.int32, (2 * pixels, 2 * cells), 0)
@@ -208,19 +212,13 @@
 
     swap = [(core, 1 - core) for core in range(CORES)]
     other = lax.ppermute(voltages, "core", swap)
-    tables = call(
-        tables_kernel,
-        (
-            jax.ShapeDtypeStruct((2 * row_total, 6 * sub_u), jnp.bfloat16),
-            jax.ShapeDtypeStruct((2 * MW, 6 * sub_v), jnp.bfloat16),
-        ),
-        (),
-        flops=2 * voltages.size * two_fine * taps,
+    token = call(
+        token_kernel, jax.ShapeDtypeStruct((8, MW), jnp.float32), (), flops=2 * voltages.size * two_fine * taps
     )
     packed = call(
         pack_kernel,
         jax.ShapeDtypeStruct((8, two_fine), jnp.float32),
-        (station_flags.reshape(1, -1), cell_index.reshape(2, -1), kernel_rows, kernel_cols, tables[0]),
+        (station_flags.reshape(1, -1), cell_index.reshape(2, -1), kernel_rows, kernel_cols, token),
     )
     other_packed = lax.ppermute(packed, "core", swap)
     flops = 2 * station_rows * taps * two_fine * two_fine
@@ -243,6 +241,14 @@
         )
         after = (made,)
         got.append(lax.ppermute(made, "chip", [(source, source ^ step) for source in range(chips)]))
+    tables = call(
+        tables_kernel,
+        (
+            jax.ShapeDtypeStruct((2 * row_total, 6 * sub_u), jnp.bfloat16),
+            jax.ShapeDtypeStruct((2 * MW, 6 * sub_v), jnp.bfloat16),
+        ),
+        after,
+    )
     lanes = each * two_fine // 2
     sides = call(
         functools.partial(near_kernel, each),

time: 24.7 us -> 24.7 us (level)
    ppermute x1, waiting for transfers between devices: 2.99 us -> 2.59 us  [local(): lax.ppermute(made, 'chip', [(source, source ^ step) for source in range(c...]
    ppermute x1, waiting for transfers between devices: 0.02 us -> 0.27 us  [local(): other_packed = lax.ppermute(packed, 'core', swap)]
    pallas_call x7 -> x8, Pallas kernels: 4.01 us -> 4.02 us  [call(): pl.pallas_call(kernel, out_shape=shape, in_specs=[pl.BlockSpec(memory_spa...]
  transfers between devices with their start and end apart: 3 -> 3, of which waited for: 1 -> 3; matrix products, arithmetic and copies ran while one was open for 0% -> 0% of each run, Pallas kernels for 10% -> 10%
where the time goes in v10:
time: 24.7 us; the launch traced here: 24.6 us
  blocking collectives  13.1 us (53%)
  Pallas kernels  4.02 us (16%)
  starting transfers between devices  3.58 us (14%)
  waiting for transfers between devices  3.06 us (12%)
  local copies, waits for them, and re-layouts  0.8 us (3%)
    all_to_all x1, blocking collectives, local(): lax.all_to_all(image, EVERYONE, split_axis=0, concat_axis=0, tiled=True)  13.1 us
    pallas_call x8, Pallas kernels, call(): pl.pallas_call(kernel, out_shape=shape, in_specs=[pl.BlockSpec(memory_spa...  4.02 us
    ppermute x1, starting transfers between devices, local(): lax.ppermute(made, 'chip', [(source, source ^ step) for source in range(c...  2.92 us
    ppermute x1, waiting for transfers between devices, local(): lax.ppermute(made, 'chip', [(source, source ^ step) for source in range(c...  2.59 us
    unnamed x12, local copies, waits for them, and re-layouts  0.8 us
    ppermute x1, starting transfers between devices, local(): other = lax.ppermute(voltages, 'core', swap)  0.53 us
  transfers between devices with their start and end apart: 3, of which 3 were waited for; matrix products, arithmetic and copies ran while one was open for 0% of the time, Pallas kernels for 10%

profile of v10, /device:TPU:0, one launch (start us, length us, event | category | flops | bytes accessed | tf_op | source)
XLA Modules:
  0.0 24.6 jit_solution(12293514286598551350)
XLA Ops:
  0.0 0.0 copy-start.1
  0.0 0.0 copy-start.3
  0.0 0.0 copy-start.2
  0.0 0.0 copy-start
  0.0 0.5 %collective-permute-start.1 = (bf16[1,2,64,3840]{3,2,1,0:T(8,128)(2,1)}, bf16[1,2,64,3840]{3,2,1,0:T(8,128)(2,1)S(1)}, u32[]{:S(2)}, u32[]{:S(2)}) collective-permute-start(bf16[1,2,64,3840]{3,2,1,0:T(8,128)(2,1)} %volt_ref.1), channel_id=1, source_target_pairs={{0,1},{1,0},{2,3},{3,2},{4,5},{5,4},{6,7},{7,6},{8,9},{9,8},{10,11... | collective-permute-start | bytes 2949128 | tf_op jit(solution)/shard_map/ppermute | solution.py:214
  0.5 0.0 copy-start.4
  0.5 0.0 copy-start.5
  0.5 0.3 %copy-done.3 = bf16[1,1,32,256]{3,2,1,0:T(8,128)(2,1)S(1)} copy-done((bf16[1,1,32,256]{3,2,1,0:T(8,128)(2,1)S(1)}, bf16[1,1,32,256]{3,2,1,0:T(8,128)(2,1)}, u32[]{:S(2)}) %copy-start.3) | copy-done | bytes 16408
  0.8 0.0 copy-done.2
  0.8 0.5 %copy-done.4 = s32[2,32,1]{1,2,0:T(1,128)S(1)} copy-done((s32[2,32,1]{1,2,0:T(1,128)S(1)}, s32[2,32,1]{1,2,0:T(1,128)}, u32[]{:S(2)}) %copy-start.4) | copy-done | bytes 280
  1.3 0.0 copy-done.5
  1.3 0.1 shard_map.65.packed_ref.own_ref
  1.4 0.1 collective-permute-start
  1.5 0.0 copy-done.1
  1.5 0.0 copy-done
  1.6 0.9 %shard_map.66.refs_5_ = f32[512,256]{1,0:T(8,128)S(1)} custom-call(bf16[1,2,64,3840]{3,2,1,0:T(8,128)(2,1)S(1)} %copy-done.1, bf16[8,256,256]{2,1,0:T(8,128)(2,1)S(1)} %copy-done, bf16[1,1,32,256]{3,2,1,0:T(8,128)(2,1)S(1)} %copy-done.2, bf16[1,1,32,256]{3,2,1,0:T(8,128)(2,1)S(1)} %copy-done.3, f32[8,256]{1,0:T(8,128)S(1)} %shard_map.65.packed_ref.own_ref), custom_call_target="tpu_custom_call" | custom-call | flops 536870912 | bytes 2596864 | tf_op jit(solution)/shard_map/pallas_call | solution.py:191
  2.5 0.3 %collective-permute-done.refs_4_.packed_ref = f32[8,256]{1,0:T(8,128)S(1)} collective-permute-done((f32[8,256]{1,0:T(8,128)S(1)}, f32[8,256]{1,0:T(8,128)S(1)}, u32[]{:S(2)}, u32[]{:S(2)}) %collective-permute-start) | collective-permute-done | bytes 8224 | tf_op jit(solution)/shard_map/ppermute | solution.py:223
  2.7 0.2 collective-permute-done.1.refs_0_
  2.9 0.6 %shard_map.67._.refs_8_ = bf16[272,256]{1,0:T(8,128)(2,1)S(1)} custom-call(f32[8,256]{1,0:T(8,128)S(1)} %shard_map.65.packed_ref.own_ref, bf16[1,2,64,3840]{3,2,1,0:T(8,128)(2,1)S(1)} %collective-permute-done.1.refs_0_, bf16[8,256,256]{2,1,0:T(8,128)(2,1)S(1)} %copy-done, bf16[1,1,32,256]{3,2,1,0:T(8,128)(2,1)S(1)} %copy-done.2, ...), custom_call_target="tpu_custom_call" | custom-call | flops 268435456 | bytes 2744320 | tf_op jit(solution)/shard_map/pallas_call | solution.py:191
  3.6 2.9 %collective-permute-start.2 = (bf16[272,256]{1,0:T(8,128)(2,1)S(1)}, bf16[272,256]{1,0:T(8,128)(2,1)S(1)}, u32[]{:S(2)}, u32[]{:S(2)}) collective-permute-start(bf16[272,256]{1,0:T(8,128)(2,1)S(1)} %shard_map.67._.refs_8_), channel_id=1, source_target_pairs={{0,2},{2,0},{1,3},{3,1},{4,6},{6,4},{5,7},{7,5},{8,10},{10,8},{9,1... | collective-permute-start | bytes 417800 | tf_op jit(solution)/shard_map/ppermute | solution.py:243
  6.5 0.4 %shard_map.68 = (bf16[64,192]{1,0:T(8,128)(2,1)S(1)}, bf16[256,192]{1,0:T(8,128)(2,1)S(1)}) custom-call(bf16[272,256]{1,0:T(8,128)(2,1)S(1)} %shard_map.67._.refs_8_), custom_call_target="tpu_custom_call" | custom-call | bytes 262144 | tf_op jit(solution)/shard_map/pallas_call | solution.py:191
  6.9 1.0 %shard_map.69 = (f32[64,512]{1,0:T(8,128)S(1)}, f32[256,512]{1,0:T(8,128)S(1)}) custom-call(bf16[1,2,64,3840]{3,2,1,0:T(8,128)(2,1)S(1)} %collective-permute-done.1.refs_0_, bf16[8,256,256]{2,1,0:T(8,128)(2,1)S(1)} %copy-done, bf16[1,1,32,256]{3,2,1,0:T(8,128)(2,1)S(1)} %copy-done.2, bf16[1,1,32,256]{3,2,1,0:T(8,128)(2,1)S(1)} %copy-done.3, ...), custom_call_target="tpu_custom_call" | custom-call | flops 268435456 | bytes 3514368 | tf_op jit(solution)/shard_map/pallas_call | solution.py:191
  7.9 2.6 %collective-permute-done.2.refs_0_ = bf16[272,256]{1,0:T(8,128)(2,1)S(1)} collective-permute-done((bf16[272,256]{1,0:T(8,128)(2,1)S(1)}, bf16[272,256]{1,0:T(8,128)(2,1)S(1)}, u32[]{:S(2)}, u32[]{:S(2)}) %collective-permute-start.2) | collective-permute-done | bytes 139296 | tf_op jit(solution)/shard_map/ppermute | solution.py:243
  10.5 0.5 %shard_map.70 = f32[32,128]{1,0:T(8,128)S(1)} custom-call(f32[8,256]{1,0:T(8,128)S(1)} %shard_map.65.packed_ref.own_ref, f32[8,256]{1,0:T(8,128)S(1)} %collective-permute-done.refs_4_.packed_ref, f32[64,512]{1,0:T(8,128)S(1)} %get-tuple-element.11.row_ref, f32[256,512]{1,0:T(8,128)S(1)} %get-tuple-element.12.col_ref, ...), custom_call_target="tpu_custom_call" | custom-call | bytes 950272 | tf_op jit(solution)/shard_map/pallas_call | solution.py:191
  10.9 13.1 %all_to_all.9.in_ref = f32[32,1,128]{2,1,0:T(1,128)S(1)} all-to-all(f32[32,1,128]{2,1,0:T(1,128)S(1)} %bitcast.3), channel_id=1, replica_groups=mesh['role'=2,'band'=4,'chip'=2,'core'=2] {'role','band','chip','core'}, dimensions={0} | all-to-all | bytes 32768 | tf_op jit(solution)/shard_map/all_to_all | solution.py:267
  24.0 0.5 %shard_map.71 = f32[1,128]{1,0:T(1,128)} custom-call(f32[32,1,128]{2,1,0:T(1,128)S(1)} %all_to_all.9.in_ref), custom_call_target="tpu_custom_call" | custom-call | bytes 16896 | tf_op jit(solution)/shard_map/pallas_call | solution.py:191
  (1 shorter events, 0.0 us)
Async XLA Ops:
  0.0 1.5 %copy-start.1 = (bf16[1,2,64,3840]{3,2,1,0:T(8,128)(2,1)S(1)}, bf16[1,2,64,3840]{3,2,1,0:T(8,128)(2,1)}, u32[]{:S(2)}) copy-start(bf16[1,2,64,3840]{3,2,1,0:T(8,128)(2,1)} %volt_ref.1) | copy-start | bytes 2949124
  0.0 0.8 %copy-start.3 = (bf16[1,1,32,256]{3,2,1,0:T(8,128)(2,1)S(1)}, bf16[1,1,32,256]{3,2,1,0:T(8,128)(2,1)}, u32[]{:S(2)}) copy-start(bf16[1,1,32,256]{3,2,1,0:T(8,128)(2,1)} %refs_3_.3) | copy-start | bytes 49156
  0.0 0.8 %copy-start.2 = (bf16[1,1,32,256]{3,2,1,0:T(8,128)(2,1)S(1)}, bf16[1,1,32,256]{3,2,1,0:T(8,128)(2,1)}, u32[]{:S(2)}) copy-start(bf16[1,1,32,256]{3,2,1,0:T(8,128)(2,1)} %refs_2_.3) | copy-start | bytes 49156
  0.0 1.5 %copy-start = (bf16[8,256,256]{2,1,0:T(8,128)(2,1)S(1)}, bf16[8,256,256]{2,1,0:T(8,128)(2,1)}, u32[]{:S(2)}) copy-start(bf16[8,256,256]{2,1,0:T(8,128)(2,1)} %refs_1_.3) | copy-start | bytes 3145732
  0.0 2.9 %collective-permute-start.1 = (bf16[1,2,64,3840]{3,2,1,0:T(8,128)(2,1)}, bf16[1,2,64,3840]{3,2,1,0:T(8,128)(2,1)S(1)}, u32[]{:S(2)}, u32[]{:S(2)}) collective-permute-start(bf16[1,2,64,3840]{3,2,1,0:T(8,128)(2,1)} %volt_ref.1), channel_id=1, source_target_pairs={{0,1},{1,0},{2,3},{3,2},{4,5},{5,4},{6,7},{7,6},{8,9},{9,8},{10,11... | collective-permute-start | bytes 2949128 | tf_op jit(solution)/shard_map/ppermute | solution.py:214
  0.5 0.8 %copy-start.4 = (s32[2,32,1]{1,2,0:T(1,128)S(1)}, s32[2,32,1]{1,2,0:T(1,128)}, u32[]{:S(2)}) copy-start(s32[2,32,1]{1,2,0:T(1,128)} %param.11) | copy-start | bytes 772
  0.5 0.8 %copy-start.5 = (s32[64]{0:T(128)S(1)}, s32[64]{0:T(128)}, u32[]{:S(2)}) copy-start(s32[64]{0:T(128)} %param.7) | copy-start | bytes 772
  1.4 1.3 %collective-permute-start = (f32[8,256]{1,0:T(8,128)S(1)}, f32[8,256]{1,0:T(8,128)S(1)}, u32[]{:S(2)}, u32[]{:S(2)}) collective-permute-start(f32[8,256]{1,0:T(8,128)S(1)} %shard_map.65.packed_ref.own_ref), channel_id=1, source_target_pairs={{0,1},{1,0},{2,3},{3,2},{4,5},{5,4},{6,7},{7,6},{8,9},{9,8},{10,11... | collective-permute-start | bytes 24584 | tf_op jit(solution)/shard_map/ppermute | solution.py:223
  3.6 6.9 %collective-permute-start.2 = (bf16[272,256]{1,0:T(8,128)(2,1)S(1)}, bf16[272,256]{1,0:T(8,128)(2,1)S(1)}, u32[]{:S(2)}, u32[]{:S(2)}) collective-permute-start(bf16[272,256]{1,0:T(8,128)(2,1)S(1)} %shard_map.67._.refs_8_), channel_id=1, source_target_pairs={{0,2},{2,0},{1,3},{3,1},{4,6},{6,4},{5,7},{7,5},{8,10},{10,8},{9,1... | collective-permute-start | bytes 417800 | tf_op jit(solution)/shard_map/ppermute | solution.py:243

commit v11 on v8

--- a/solution.py
+++ b/solution.py
@@ -88,7 +88,10 @@
         axis=0,
     )
     filt = taps_ref[...].reshape(taps * two_fine, two_fine)
-    spectra = jnp.dot(lhs, filt, preferred_element_type=jnp.float32).astype(jnp.bfloat16)
+    half = taps // 2 * two_fine
+    spectra = jnp.dot(lhs[:, :half], filt[:half], preferred_element_type=jnp.float32)
+    spectra = spectra + jnp.dot(lhs[:, half:], filt[half:], preferred_element_type=jnp.float32)
+    spectra = spectra.astype(jnp.bfloat16)
     beside = jnp.concatenate(
         [spectra[index * stations : (index + 1) * stations] for index in range(len(firsts))], axis=1
     )

time: 24.7 us -> 24.7 us (level)
  no operation moved by 1% of the time
where the time goes in v11:
time: 24.7 us; the launch traced here: 24.5 us
  blocking collectives  13.1 us (53%)
  Pallas kernels  4.01 us (16%)
  starting transfers between devices  3.67 us (15%)
  waiting for transfers between devices  3.01 us (12%)
  local copies, waits for them, and re-layouts  0.69 us (3%)
    all_to_all x1, blocking collectives, local(): lax.all_to_all(image, EVERYONE, split_axis=0, concat_axis=0, tiled=True)  13.1 us
    pallas_call x7, Pallas kernels, call(): pl.pallas_call(kernel, out_shape=shape, in_specs=[pl.BlockSpec(memory_spa...  4.01 us
    ppermute x1, waiting for transfers between devices, local(): lax.ppermute(made, 'chip', [(source, source ^ step) for source in range(c...  2.99 us
    ppermute x1, starting transfers between devices, local(): lax.ppermute(made, 'chip', [(source, source ^ step) for source in range(c...  2.91 us
    unnamed x12, local copies, waits for them, and re-layouts  0.69 us
  transfers between devices with their start and end apart: 3, of which 1 were waited for; matrix products, arithmetic and copies ran while one was open for 0% of the time, Pallas kernels for 10%

profile of v11, /device:TPU:0, one launch (start us, length us, event | category | flops | bytes accessed | tf_op | source)
XLA Modules:
  0.0 24.5 jit_solution(16375508222489156116)
XLA Ops:
  0.0 0.0 copy-start.1
  0.0 0.0 copy-start
  0.0 0.5 %collective-permute-start.1 = (bf16[1,2,64,3840]{3,2,1,0:T(8,128)(2,1)}, bf16[1,2,64,3840]{3,2,1,0:T(8,128)(2,1)S(1)}, u32[]{:S(2)}, u32[]{:S(2)}) collective-permute-start(bf16[1,2,64,3840]{3,2,1,0:T(8,128)(2,1)} %volt_ref.1), channel_id=1, source_target_pairs={{0,1},{1,0},{2,3},{3,2},{4,5},{5,4},{6,7},{7,6},{8,9},{9,8},{10,11... | collective-permute-start | bytes 2949128 | tf_op jit(solution)/shard_map/ppermute | solution.py:213
  0.5 0.0 copy-start.2
  0.5 0.0 copy-start.3
  0.5 0.4 %shard_map.64 = (bf16[64,192]{1,0:T(8,128)(2,1)S(1)}, bf16[256,192]{1,0:T(8,128)(2,1)S(1)}) custom-call(), custom_call_target="tpu_custom_call" | custom-call | flops 2013265920 | bytes 122880 | tf_op jit(solution)/shard_map/pallas_call | solution.py:190
  0.9 0.0 copy-start.4
  0.9 0.0 copy-start.5
  0.9 0.5 %copy-done.2 = bf16[1,1,32,256]{3,2,1,0:T(8,128)(2,1)S(1)} copy-done((bf16[1,1,32,256]{3,2,1,0:T(8,128)(2,1)S(1)}, bf16[1,1,32,256]{3,2,1,0:T(8,128)(2,1)}, u32[]{:S(2)}) %copy-start.2) | copy-done | bytes 16408
  1.3 0.0 copy-done.3
  1.3 0.2 copy-done.4
  1.5 0.0 copy-done.5
  1.5 0.1 shard_map.65.packed_ref.own_ref
  1.6 0.3 %collective-permute-start = (f32[8,256]{1,0:T(8,128)S(1)}, f32[8,256]{1,0:T(8,128)S(1)}, u32[]{:S(2)}, u32[]{:S(2)}) collective-permute-start(f32[8,256]{1,0:T(8,128)S(1)} %shard_map.65.packed_ref.own_ref), channel_id=1, source_target_pairs={{0,1},{1,0},{2,3},{3,2},{4,5},{5,4},{6,7},{7,6},{8,9},{9,8},{10,11... | collective-permute-start | bytes 24584 | tf_op jit(solution)/shard_map/ppermute | solution.py:228
  1.9 0.0 copy-done.1
  1.9 0.0 copy-done
  1.9 0.9 %shard_map.66.refs_5_ = f32[512,256]{1,0:T(8,128)S(1)} custom-call(bf16[1,2,64,3840]{3,2,1,0:T(8,128)(2,1)S(1)} %copy-done.1, bf16[8,256,256]{2,1,0:T(8,128)(2,1)S(1)} %copy-done, bf16[1,1,32,256]{3,2,1,0:T(8,128)(2,1)S(1)} %copy-done.2, bf16[1,1,32,256]{3,2,1,0:T(8,128)(2,1)S(1)} %copy-done.3, f32[8,256]{1,0:T(8,128)S(1)} %shard_map.65.packed_ref.own_ref), custom_call_target="tpu_custom_call" | custom-call | flops 536870912 | bytes 2596864 | tf_op jit(solution)/shard_map/pallas_call | solution.py:190
  2.8 0.0 collective-permute-done.refs_4_.packed_ref
  2.9 0.0 collective-permute-done.1.refs_0_
  2.9 0.6 %shard_map.67.refs_8_ = bf16[272,256]{1,0:T(8,128)(2,1)S(1)} custom-call(f32[8,256]{1,0:T(8,128)S(1)} %shard_map.65.packed_ref.own_ref, bf16[1,2,64,3840]{3,2,1,0:T(8,128)(2,1)S(1)} %collective-permute-done.1.refs_0_, bf16[8,256,256]{2,1,0:T(8,128)(2,1)S(1)} %copy-done, bf16[1,1,32,256]{3,2,1,0:T(8,128)(2,1)S(1)} %copy-done.2, ...), custom_call_target="tpu_custom_call" | custom-call | flops 268435456 | bytes 2744320 | tf_op jit(solution)/shard_map/pallas_call | solution.py:190
  3.5 2.9 %collective-permute-start.2 = (bf16[272,256]{1,0:T(8,128)(2,1)S(1)}, bf16[272,256]{1,0:T(8,128)(2,1)S(1)}, u32[]{:S(2)}, u32[]{:S(2)}) collective-permute-start(bf16[272,256]{1,0:T(8,128)(2,1)S(1)} %shard_map.67.refs_8_), channel_id=1, source_target_pairs={{0,2},{2,0},{1,3},{3,1},{4,6},{6,4},{5,7},{7,5},{8,10},{10,8},{9,1... | collective-permute-start | bytes 417800 | tf_op jit(solution)/shard_map/ppermute | solution.py:248
  6.4 1.0 %shard_map.68 = (f32[64,512]{1,0:T(8,128)S(1)}, f32[256,512]{1,0:T(8,128)S(1)}) custom-call(bf16[1,2,64,3840]{3,2,1,0:T(8,128)(2,1)S(1)} %collective-permute-done.1.refs_0_, bf16[8,256,256]{2,1,0:T(8,128)(2,1)S(1)} %copy-done, bf16[1,1,32,256]{3,2,1,0:T(8,128)(2,1)S(1)} %copy-done.2, bf16[1,1,32,256]{3,2,1,0:T(8,128)(2,1)S(1)} %copy-done.3, ...), custom_call_target="tpu_custom_call" | custom-call | flops 268435456 | bytes 3514368 | tf_op jit(solution)/shard_map/pallas_call | solution.py:190
  7.4 3.0 %collective-permute-done.2.refs_0_ = bf16[272,256]{1,0:T(8,128)(2,1)S(1)} collective-permute-done((bf16[272,256]{1,0:T(8,128)(2,1)S(1)}, bf16[272,256]{1,0:T(8,128)(2,1)S(1)}, u32[]{:S(2)}, u32[]{:S(2)}) %collective-permute-start.2) | collective-permute-done | bytes 139296 | tf_op jit(solution)/shard_map/ppermute | solution.py:248
  10.4 0.5 %shard_map.69 = f32[32,128]{1,0:T(8,128)S(1)} custom-call(f32[8,256]{1,0:T(8,128)S(1)} %shard_map.65.packed_ref.own_ref, f32[8,256]{1,0:T(8,128)S(1)} %collective-permute-done.refs_4_.packed_ref, f32[64,512]{1,0:T(8,128)S(1)} %get-tuple-element.11.row_ref, f32[256,512]{1,0:T(8,128)S(1)} %get-tuple-element.12.col_ref, ...), custom_call_target="tpu_custom_call" | custom-call | bytes 950272 | tf_op jit(solution)/shard_map/pallas_call | solution.py:190
  10.9 13.1 %all_to_all.9.in_ref = f32[32,1,128]{2,1,0:T(1,128)S(1)} all-to-all(f32[32,1,128]{2,1,0:T(1,128)S(1)} %bitcast.3), channel_id=1, replica_groups=mesh['role'=2,'band'=4,'chip'=2,'core'=2] {'role','band','chip','core'}, dimensions={0} | all-to-all | bytes 32768 | tf_op jit(solution)/shard_map/all_to_all | solution.py:264
  24.0 0.5 %shard_map.70 = f32[1,128]{1,0:T(1,128)} custom-call(f32[32,1,128]{2,1,0:T(1,128)S(1)} %all_to_all.9.in_ref), custom_call_target="tpu_custom_call" | custom-call | bytes 16896 | tf_op jit(solution)/shard_map/pallas_call | solution.py:190
Async XLA Ops:
  0.0 1.9 %copy-start.1 = (bf16[1,2,64,3840]{3,2,1,0:T(8,128)(2,1)S(1)}, bf16[1,2,64,3840]{3,2,1,0:T(8,128)(2,1)}, u32[]{:S(2)}) copy-start(bf16[1,2,64,3840]{3,2,1,0:T(8,128)(2,1)} %volt_ref.1) | copy-start | bytes 2949124
  0.0 1.9 %copy-start = (bf16[8,256,256]{2,1,0:T(8,128)(2,1)S(1)}, bf16[8,256,256]{2,1,0:T(8,128)(2,1)}, u32[]{:S(2)}) copy-start(bf16[8,256,256]{2,1,0:T(8,128)(2,1)} %refs_1_.3) | copy-start | bytes 3145732
  0.0 2.9 %collective-permute-start.1 = (bf16[1,2,64,3840]{3,2,1,0:T(8,128)(2,1)}, bf16[1,2,64,3840]{3,2,1,0:T(8,128)(2,1)S(1)}, u32[]{:S(2)}, u32[]{:S(2)}) collective-permute-start(bf16[1,2,64,3840]{3,2,1,0:T(8,128)(2,1)} %volt_ref.1), channel_id=1, source_target_pairs={{0,1},{1,0},{2,3},{3,2},{4,5},{5,4},{6,7},{7,6},{8,9},{9,8},{10,11... | collective-permute-start | bytes 2949128 | tf_op jit(solution)/shard_map/ppermute | solution.py:213
  0.5 0.9 %copy-start.2 = (bf16[1,1,32,256]{3,2,1,0:T(8,128)(2,1)S(1)}, bf16[1,1,32,256]{3,2,1,0:T(8,128)(2,1)}, u32[]{:S(2)}) copy-start(bf16[1,1,32,256]{3,2,1,0:T(8,128)(2,1)} %refs_2_.3) | copy-start | bytes 49156
  0.5 0.9 %copy-start.3 = (bf16[1,1,32,256]{3,2,1,0:T(8,128)(2,1)S(1)}, bf16[1,1,32,256]{3,2,1,0:T(8,128)(2,1)}, u32[]{:S(2)}) copy-start(bf16[1,1,32,256]{3,2,1,0:T(8,128)(2,1)} %refs_3_.3) | copy-start | bytes 49156
  0.9 0.7 %copy-start.4 = (s32[2,32,1]{1,2,0:T(1,128)S(1)}, s32[2,32,1]{1,2,0:T(1,128)}, u32[]{:S(2)}) copy-start(s32[2,32,1]{1,2,0:T(1,128)} %param.11) | copy-start | bytes 772
  0.9 0.7 %copy-start.5 = (s32[64]{0:T(128)S(1)}, s32[64]{0:T(128)}, u32[]{:S(2)}) copy-start(s32[64]{0:T(128)} %param.7) | copy-start | bytes 772
  1.6 1.2 %collective-permute-start = (f32[8,256]{1,0:T(8,128)S(1)}, f32[8,256]{1,0:T(8,128)S(1)}, u32[]{:S(2)}, u32[]{:S(2)}) collective-permute-start(f32[8,256]{1,0:T(8,128)S(1)} %shard_map.65.packed_ref.own_ref), channel_id=1, source_target_pairs={{0,1},{1,0},{2,3},{3,2},{4,5},{5,4},{6,7},{7,6},{8,9},{9,8},{10,11... | collective-permute-start | bytes 24584 | tf_op jit(solution)/shard_map/ppermute | solution.py:228
  3.5 6.9 %collective-permute-start.2 = (bf16[272,256]{1,0:T(8,128)(2,1)S(1)}, bf16[272,256]{1,0:T(8,128)(2,1)S(1)}, u32[]{:S(2)}, u32[]{:S(2)}) collective-permute-start(bf16[272,256]{1,0:T(8,128)(2,1)S(1)} %shard_map.67.refs_8_), channel_id=1, source_target_pairs={{0,2},{2,0},{1,3},{3,1},{4,6},{6,4},{5,7},{7,5},{8,10},{10,8},{9,1... | collective-permute-start | bytes 417800 | tf_op jit(solution)/shard_map/ppermute | solution.py:248
